TPU v7x, 32 devices: a whole 2x2x4 slice. The times are simulated.
32 devices in a mesh: group: 2 (over y), layer: 4 (over x, core), feat: 4 (over z).
Axes of the slice: x: 2, y: 2, z: 4, core: 2. Of those that a mesh axis runs over, the one named last changes fastest.
Arguments:
- inputs: bfloat16 [8, 4096, 1024], P(('group', 'layer'), 'feat'), parts along dimension 0, may hold values from -6 to 6
- targets: bfloat16 [8, 4096, 1024], P(('group', 'layer'), 'feat'), parts along dimension 0, may hold values from -6 to 6
- enc_weight: float32 [8, 128, 4096], P(('group', 'layer'), 'feat'), parts along dimension 0, may hold values from -0.09375 to 0.09375
- enc_bias: float32 [8, 128], P(('group', 'layer'), 'feat'), parts along dimension 0, may hold values from -1 to 0.5
- dec_weight: float32 [8, 4, 128, 4096], P(('group', 'layer'), None, 'feat'), parts along dimension 0, may hold values from -0.5 to 0.5
- dec_bias: float32 [8, 4096], P(('group', 'layer'), 'feat'), parts along dimension 0, may hold values from -3 to 3
- enc_moments: float32 [2, 8, 128, 4096], P(None, ('group', 'layer'), 'feat'), parts along dimension 1, as said below
- enc_bias_moments: float32 [2, 8, 128], P(None, ('group', 'layer'), 'feat'), parts along dimension 1, as said below
- dec_moments: float32 [2, 8, 4, 128, 4096], P(None, ('group', 'layer'), None, 'feat'), parts along dimension 1, as said below
- dec_bias_moments: float32 [2, 8, 4096], P(None, ('group', 'layer'), 'feat'), parts along dimension 1, as said below
- block_lists: int32 [8, 64, 128], P(('group', 'layer')), parts along dimension 0, may hold values from 0 to 255, as said below
- block_counts: int32 [8, 64], P(('group', 'layer')), parts along dimension 0, may hold values from 1 to 128, as said below
- slot_block: int32 [8], P(('group', 'layer')), parts along dimension 0, may hold values from 0 to 255
Outputs:
- enc_weight_new: float32 [8, 128, 4096], P(('group', 'layer'), 'feat'), parts along dimension 0
- enc_bias_new: float32 [8, 128], P(('group', 'layer'), 'feat'), parts along dimension 0
- dec_weight_new: float32 [8, 4, 128, 4096], P(('group', 'layer'), None, 'feat'), parts along dimension 0
- dec_bias_new: float32 [8, 4096], P(('group', 'layer'), 'feat'), parts along dimension 0
- enc_moments_new: float32 [2, 8, 128, 4096], P(None, ('group', 'layer'), 'feat'), parts along dimension 1
- enc_bias_moments_new: float32 [2, 8, 128], P(None, ('group', 'layer'), 'feat'), parts along dimension 1
- dec_moments_new: float32 [2, 8, 4, 128, 4096], P(None, ('group', 'layer'), None, 'feat'), parts along dimension 1
- dec_bias_moments_new: float32 [2, 8, 4096], P(None, ('group', 'layer'), 'feat'), parts along dimension 1
There are 2 independent parts, one for each index of `group`. A program takes and returns all parts, laid end to end along the dimension named above; each array names one. Nothing has to cross between parts.
Inputs may be any that keep to these rules, and one draw needn't show every extreme that they name: `block_lists`: entries of one list are distinct block numbers; only the first block_counts entries of a list are live. `block_counts`: some layer and tile has all 128 entries live in every draw. `enc_moments`: the first moment is signed, the second positive. `enc_bias_moments`: the first moment is signed, the second positive. `dec_moments`: the first moment is signed, the second positive. `dec_bias_moments`: the first moment is signed, the second positive.
All inputs are finite; a program needn't handle non-finite values.
Results may differ from a plain program's by a relative error of at most 0.0003.
Values may be sent and summed in bfloat16 or wider, within the bound.
No kernel may reach another device: no remote copies, remote signals or barrier semaphores. Data moves between devices by JAX's collectives and lax.ppermute only.
A program may use at most 128 MiB of HBM per device.

v0:
```python
import jax
import jax.numpy as jnp
from jax import lax
from jax.sharding import PartitionSpec as P

beta_one = 0.9
beta_two = 0.999
learn_rate = 0.001
adam_eps = 1e-08
step_count = 100.0
highest = lax.Precision.HIGHEST


def shifted(value, axis, steps):
    count = lax.axis_size(axis)
    initial, last = (max(0, -steps), min(count, count - steps))
    return lax.ppermute(value, axis, [(source, source + steps) for source in range(initial, last)])


def adam_update(weight, moments, grad):
    first = beta_one * moments[0] + (1.0 - beta_one) * grad
    second = beta_two * moments[1] + (1.0 - beta_two) * grad * grad
    scaled_first = first / (1.0 - beta_one**step_count)
    scaled_second = second / (1.0 - beta_two**step_count)
    updated = weight - learn_rate * scaled_first / (jnp.sqrt(scaled_second) + adam_eps)
    return (updated, jnp.stack([first, second]))


def send_sources(codes, reach_count):
    stacked = [codes]
    for offset in range(1, reach_count):
        stacked.append(shifted(codes, "layer", offset))
    return jnp.stack(stacked)


def return_grads(code_parts, reach_count):
    total = code_parts[0]
    for offset in range(1, reach_count):
        total = total + shifted(code_parts[offset], "layer", -offset)
    return total


def local(
    inputs,
    targets,
    enc_weight,
    enc_bias,
    dec_weight,
    dec_bias,
    enc_moments,
    enc_bias_moments,
    dec_moments,
    dec_bias_moments,
    block_lists,
    block_counts,
    slot_block,
):
    inputs_local = inputs[0]
    targets_local = targets[0].astype(jnp.float32)
    enc_local = enc_weight[0]
    encb_local = enc_bias[0]
    dec_local = dec_weight[0]
    decb_local = dec_bias[0]
    reach_count = dec_local.shape[0]
    row_count = inputs_local.shape[1]
    tile_count = block_counts.shape[1]
    tile_rows = row_count // tile_count
    live = jnp.arange(block_lists.shape[2])[None, :] < block_counts[0][:, None]
    hits = (block_lists[0] == slot_block[0]) & live
    tile_active = jnp.any(hits, axis=1).astype(jnp.float32)
    row_mask = jnp.repeat(tile_active, tile_rows, axis=0)[None, :]
    dec_cols = lax.all_to_all(dec_local, "feat", split_axis=2, concat_axis=1, tiled=True)
    full_inputs = lax.all_gather(inputs_local, "feat", axis=0, tiled=True).astype(jnp.float32)
    pre = (
        jnp.dot(enc_local, full_inputs, precision=highest, preferred_element_type=jnp.float32)
        + encb_local[:, None]
    )
    codes = jnp.maximum(pre, 0.0) * row_mask
    sources = send_sources(codes, reach_count)
    all_sources = lax.all_gather(sources, "feat", axis=1, tiled=True)
    recon = (
        jnp.einsum("kfd,kfr->dr", dec_cols, all_sources, precision=highest) + decb_local[:, None]
    )
    resid = recon - targets_local
    grad_dec_cols = jnp.einsum("kfr,dr->kfd", all_sources, resid, precision=highest)
    code_partial = jnp.einsum("kfd,dr->kfr", dec_cols, resid, precision=highest)
    code_parts = lax.psum_scatter(code_partial, "feat", scatter_dimension=1, tiled=True)
    code_grad = return_grads(code_parts, reach_count)
    pre_grad = code_grad * row_mask * (pre > 0.0).astype(jnp.float32)
    grad_enc = jnp.dot(
        pre_grad, full_inputs.T, precision=highest, preferred_element_type=jnp.float32
    )
    grad_dec = lax.all_to_all(grad_dec_cols, "feat", split_axis=1, concat_axis=2, tiled=True)
    grad_dec_bias = jnp.sum(resid, axis=1)
    grad_enc_bias = jnp.sum(pre_grad, axis=1)
    enc_new, enc_mom = adam_update(enc_local, enc_moments[:, 0], grad_enc)
    encb_new, encb_mom = adam_update(encb_local, enc_bias_moments[:, 0], grad_enc_bias)
    dec_new, dec_mom = adam_update(dec_local, dec_moments[:, 0], grad_dec)
    decb_new, decb_mom = adam_update(decb_local, dec_bias_moments[:, 0], grad_dec_bias)
    return (
        enc_new[None],
        encb_new[None],
        dec_new[None],
        decb_new[None],
        enc_mom[:, None],
        encb_mom[:, None],
        dec_mom[:, None],
        decb_mom[:, None],
    )


def solution(mesh):
    return jax.shard_map(
        local,
        mesh=mesh,
        in_specs=(
            P(("group", "layer"), "feat", None),
            P(("group", "layer"), "feat", None),
            P(("group", "layer"), "feat", None),
            P(("group", "layer"), "feat"),
            P(("group", "layer"), None, "feat", None),
            P(("group", "layer"), "feat"),
            P(None, ("group", "layer"), "feat", None),
            P(None, ("group", "layer"), "feat"),
            P(None, ("group", "layer"), None, "feat", None),
            P(None, ("group", "layer"), "feat"),
            P(("group", "layer"), None, None),
            P(("group", "layer"), None),
            P(("group", "layer")),
        ),
        out_specs=(
            P(("group", "layer"), "feat", None),
            P(("group", "layer"), "feat"),
            P(("group", "layer"), None, "feat", None),
            P(("group", "layer"), "feat"),
            P(None, ("group", "layer"), "feat", None),
            P(None, ("group", "layer"), "feat"),
            P(None, ("group", "layer"), None, "feat", None),
            P(None, ("group", "layer"), "feat"),
        ),
        check_vma=False,
    )
```

profile of v0, /device:TPU:2, one launch (start us, length us, event | category | flops | bytes accessed | tf_op | source)
XLA Modules:
  0.0 448.3 jit_solution(7150951326400052093)
XLA Ops:
  7.2 0.7 all-gather.6.cloned.1.call-update
  9.0 5.9 %copy.35 = f32[1,4,32,4096]{2,1,3,0:T(4,128)} copy(f32[1,4,32,4096]{3,2,1,0:T(8,128)S(1)} %copy-done.2) | data formatting | bytes 4194304 | tf_op args[4]
  14.9 145.6 %all-gather.6.cloned.1.call-done = bf16[1,4096,1024]{2,1,0:T(8,128)(2,1)} async-done(((bf16[1,1024,1024]{2,1,0:T(8,128)(2,1)}), bf16[1,4096,1024]{2,1,0:T(8,128)(2,1)}) %all-gather.6.cloned.1.call-update) | async-done | bytes 8388624 | tf_op jit(solution)/shard_map/all_gather | solution.py:73
  160.5 6.6 %maximum_multiply_fusion = (f32[32,1024]{1,0:T(8,128)S(1)}, f32[32,1024]{1,0:T(8,128)S(1)}) fusion(f32[1024]{0:T(1024)S(1)} %mul.348, f32[32]{0:T(128)S(1)} %bitcast.147, bf16[1,4096,1024]{2,1,0:T(8,128)(2,1)} %all-gather.6.cloned.1.call-done, f32[1,32,4096]{2,1,0:T(8,128)S(1)} %copy-done.6), kind=kOutput, calls=%fused_computation.35 | convolution fusion | flops 1610711040 | bytes 9179264 | tf_op jit(solution)/shard_map/dot_general | solution.py:75
  167.8 1.3 collective-permute-start.1
  169.1 2.6 collective-permute-start
  171.7 3.6 bitcast_bitcast_fusion
  175.3 8.4 %reshape.289 = f32[4,1,131072]{2,1,0:T(1,128)} reshape(f32[4096,4,32]{2,1,0:T(4,128)} %bitcast_bitcast_fusion) | data formatting | bytes 4194304
  183.7 3.6 all-to-all-start
  187.9 0.8 pad_maximum_fusion
  188.8 3.9 copy.37
  192.7 76.3 %all-to-all-done = f32[4,1,131072]{2,1,0:T(1,128)S(1)} async-done(((f32[4,1,131072]{2,1,0:T(1,128)}), f32[4,1,131072]{2,1,0:T(1,128)S(1)}, u32[]{:S(2)}, u32[]{:S(2)}) %all-to-all-start) | async-done | bytes 2097184 | tf_op jit(solution)/shard_map/all_to_all | solution.py:72
  269.1 1.3 copy-done.4
  270.9 7.7 %reduce = f32[4,131072]{1,0:T(4,128)S(1)} reduce(f32[4,1,131072]{2,1,0:T(1,128)} %copy-done.4, f32[]{:T(128)} %broadcast.261), dimensions={1}, to_apply=%all_to_all.26.reduce_sub_computation | reduce | bytes 4194308 | tf_op jit(solution)/shard_map/all_to_all | solution.py:72
  278.6 7.8 %reshape.290 = f32[4096,4,32]{2,1,0:T(4,128)} reshape(f32[4,131072]{1,0:T(4,128)S(1)} %reduce) | data formatting | bytes 4194304
  286.4 6.7 %copy.36 = f32[4,32,4,1024]{3,1,2,0:T(8,128)S(1)} copy(f32[4,32,4,1024]{1,0,3,2:T(4,128)} %bitcast.138) | data formatting | bytes 4194304 | tf_op jit(solution)/shard_map/all_to_all | solution.py:72
  293.2 9.1 %fusion.36 = (f32[1024]{0:T(1024)S(1)}, f32[1024,1024]{0,1:T(8,128)S(1)}) fusion(bf16[1,1024,1024]{1,2,0:T(8,128)(2,1)} %copy.37, f32[1024]{0:T(1024)S(1)} %bitcast.145, f32[4,128,1024]{2,1,0:T(8,128)} %all-gather.4.cloned.1.call-done, f32[4,128,1024]{2,1,0:T(8,128)S(1)} %bitcast.139), kind=kOutput, calls=%fused_computation.52 | convolution fusion | flops 6446644224 | bytes 10493952 | tf_op jit(solution)/shard_map/kfd,kfr->dr/dot_general | solution.py:82
  302.3 6.9 %fusion.4 = f32[4,128,1024]{2,1,0:T(8,128)S(1)} fusion(f32[4,128,1024]{2,1,0:T(8,128)S(1)} %copy-done.5, f32[1024,1024]{0,1:T(8,128)S(1)} %get-tuple-element.52), kind=kOutput, calls=%fused_computation.6 | convolution fusion | flops 6442450944 | bytes 8388608 | tf_op jit(solution)/shard_map/kfr,dr->kfd/dot_general | solution.py:85
  309.2 2.7 copy.40
  311.9 4.5 all-to-all-start.1
  316.5 9.8 %fusion.9 = f32[4,128,1024]{2,1,0:T(8,128)} fusion(f32[4,128,1024]{2,1,0:T(8,128)S(1)} %bitcast.140, f32[1024,1024]{0,1:T(8,128)} %copy-done), kind=kOutput, calls=%fused_computation.15 | convolution fusion | flops 6442450944 | bytes 8388608 | tf_op jit(solution)/shard_map/kfd,dr->kfr/dot_general | solution.py:86
  328.2 68.4 %all-to-all-done.1 = f32[4,128,1024]{2,0,1:T(4,128)} async-done(((f32[4,128,1024]{2,0,1:T(4,128)}), f32[4,128,1024]{2,0,1:T(4,128)}, u32[]{:S(2)}, u32[]{:S(2)}) %all-to-all-start.1) | async-done | bytes 2097184 | tf_op jit(solution)/shard_map/all_to_all | solution.py:93
  396.6 4.3 copy.41
  400.9 3.8 all_to_all.33
  404.7 6.5 %divide_subtract_fusion = (f32[1,4,32,4096]{3,2,1,0:T(8,128)}, f32[1,4,32,4096]{3,2,1,0:T(8,128)}, f32[1,4,32,4096]{3,2,1,0:T(8,128)}) fusion(f32[1,4,32,4096]{3,2,1,0:T(8,128)S(1)} %copy-done.3, f32[1,4,32,4096]{3,2,1,0:T(8,128)} %all_to_all.33, f32[2,1,4,32,4096]{4,3,2,1,0:T(8,128)} %param.21), kind=kLoop, calls=%fused_computation.14 | loop fusion | flops 6291456 | bytes 14680064 | tf_op jit(solution)/shard_map/sub | solution.py:25
  411.2 1.1 slice_bitcast_fusion.2
  412.9 6.9 %collective-permute-start.4 = (f32[32,1024]{1,0:T(8,128)S(1)}, f32[32,1024]{1,0:T(8,128)S(1)}, u32[]{:S(2)}, u32[]{:S(2)}) collective-permute-start(f32[32,1024]{1,0:T(8,128)S(1)} %get-tuple-element.48), channel_id=1, source_target_pairs={{8,0},{12,4},{9,1},{13,5},{10,2},{14,6},{11,3},{15,7},{24,16},{28,... | collective-permute-start | bytes 393224 | tf_op jit(solution)/shard_map/ppermute | solution.py:17
  419.8 2.2 collective-permute-start.3
  422.0 4.8 %maximum_bitcast_fusion = f32[2,1,4,32,4096]{4,3,2,1,0:T(8,128)} fusion(f32[1,4,32,4096]{3,2,1,0:T(8,128)} %get-tuple-element.37, f32[1,4,32,4096]{3,2,1,0:T(8,128)} %get-tuple-element.36), kind=kLoop, calls=%fused_computation.4 | loop fusion | flops 1048576 | bytes 8388608 | tf_op jit(solution)/shard_map/broadcast_in_dim | solution.py:107
  426.8 1.0 fusion.34
  428.4 11.6 %fusion.18 = (f32[1,32,4096]{2,1,0:T(8,128)S(1)}, f32[1,32,4096]{2,1,0:T(8,128)S(1)}, f32[1,32,4096]{2,1,0:T(8,128)}) fusion(f32[2,1,32,4096]{3,2,1,0:T(8,128)S(1)} %copy-done.7, f32[1,32,4096]{2,1,0:T(8,128)S(1)} %copy-done.6, f32[32,1024]{1,0:T(8,128)S(1)} %get-tuple-element.42, bf16[1,4096,1024]{2,1,0:T(8,128)(2,1)} %all-gather.6.cloned.1.call-done), kind=kOutput, calls=%fused_computation.25 | convolution fusion | flops 1612185600 | bytes 11665408 | tf_op jit(solution)/shard_map/dot_general | solution.py:90
  439.9 1.0 maximum_bitcast_fusion.1
  (52 shorter events, 6.0 us)
Async XLA Ops:
  7.2 1.4 copy-start.8
  7.2 1.4 copy-start.13
  7.2 1.8 copy-start.2
  7.2 153.3 %all-gather.6.cloned.1.call-start = ((), (), s32[]{:S(2)}) async-start(), calls=%async_computation.5 | async-start | bytes 10485760 | tf_op jit(solution)/shard_map/all_gather | solution.py:73
  8.9 151.6 %copy-start.6 = (f32[1,32,4096]{2,1,0:T(8,128)S(1)}, f32[1,32,4096]{2,1,0:T(8,128)}, u32[]{:S(2)}) copy-start(f32[1,32,4096]{2,1,0:T(8,128)} %param.15) | copy-start | bytes 1572868
  9.0 151.5 %copy-start.11 = (f32[1,32]{1,0:T(1,128)S(1)}, f32[1,32]{1,0:T(1,128)}, u32[]{:S(2)}) copy-start(f32[1,32]{1,0:T(1,128)} %param.16) | copy-start | bytes 388
  160.5 11.2 %copy-start.1 = (f32[1,4,32,4096]{2,1,3,0:T(4,128)S(1)}, f32[1,4,32,4096]{2,1,3,0:T(4,128)}, u32[]{:S(2)}) copy-start(f32[1,4,32,4096]{2,1,3,0:T(4,128)} %copy.35) | copy-start | bytes 6291460
  167.1 20.8 %collective-permute-start.2 = (f32[32,1024]{1,0:T(8,128)S(1)}, f32[32,1024]{1,0:T(8,128)S(1)}, u32[]{:S(2)}, u32[]{:S(2)}) collective-permute-start(f32[32,1024]{1,0:T(8,128)S(1)} %get-tuple-element.49), channel_id=1, source_target_pairs={{0,12},{1,13},{2,14},{3,15},{16,28},{17,29},{18,30},{19,31}} | collective-permute-start | bytes 393224 | tf_op jit(solution)/shard_map/ppermute | solution.py:17
  167.8 20.2 %collective-permute-start.1 = (f32[32,1024]{1,0:T(8,128)S(1)}, f32[32,1024]{1,0:T(8,128)S(1)}, u32[]{:S(2)}, u32[]{:S(2)}) collective-permute-start(f32[32,1024]{1,0:T(8,128)S(1)} %get-tuple-element.49), channel_id=1, source_target_pairs={{0,8},{4,12},{1,9},{5,13},{2,10},{6,14},{3,11},{7,15},{16,24},{20,... | collective-permute-start | bytes 393224 | tf_op jit(solution)/shard_map/ppermute | solution.py:17
  169.1 18.9 %collective-permute-start = (f32[32,1024]{1,0:T(8,128)S(1)}, f32[32,1024]{1,0:T(8,128)S(1)}, u32[]{:S(2)}, u32[]{:S(2)}) collective-permute-start(f32[32,1024]{1,0:T(8,128)S(1)} %get-tuple-element.49), channel_id=1, source_target_pairs={{0,4},{4,8},{8,12},{1,5},{5,9},{9,13},{2,6},{6,10},{10,14},{3,7},{... | collective-permute-start | bytes 393224 | tf_op jit(solution)/shard_map/ppermute | solution.py:17
  183.7 85.4 %all-to-all-start = ((f32[4,1,131072]{2,1,0:T(1,128)}), f32[4,1,131072]{2,1,0:T(1,128)S(1)}, u32[]{:S(2)}, u32[]{:S(2)}) async-start(f32[4,1,131072]{2,1,0:T(1,128)} %reshape.289), calls=%async_computation | async-start | bytes 4194304 | tf_op jit(solution)/shard_map/all_to_all | solution.py:72
  187.3 105.8 %all-gather.4.cloned.1.call-start = ((), (), s32[]{:S(2)}) async-start(), calls=%async_computation.3 | async-start | bytes 2621440 | tf_op jit(solution)/shard_map/all_gather | solution.py:80
  269.1 1.3 copy-start.4
  286.4 6.7 %copy-start.9 = (f32[1,1024]{1,0:T(1,128)S(1)}, f32[1,1024]{1,0:T(1,128)}, u32[]{:S(2)}) copy-start(f32[1,1024]{1,0:T(1,128)} %param.18) | copy-start | bytes 12292
  293.2 9.1 %copy-start.5 = (f32[4,128,1024]{2,1,0:T(8,128)S(1)}, f32[4,128,1024]{2,1,0:T(8,128)}, u32[]{:S(2)}) copy-start(f32[4,128,1024]{2,1,0:T(8,128)} %all-gather.4.cloned.1.call-done) | copy-start | bytes 6291460
  302.3 6.9 %copy-start = (f32[1024,1024]{0,1:T(8,128)}, f32[1024,1024]{0,1:T(8,128)S(1)}, u32[]{:S(2)}) copy-start(f32[1024,1024]{0,1:T(8,128)S(1)} %get-tuple-element.52) | copy-start | bytes 12582916
  311.9 84.7 %all-to-all-start.1 = ((f32[4,128,1024]{2,0,1:T(4,128)}), f32[4,128,1024]{2,0,1:T(4,128)}, u32[]{:S(2)}, u32[]{:S(2)}) async-start(f32[4,128,1024]{2,0,1:T(4,128)} %copy.40), calls=%async_computation.2 | async-start | bytes 4194304 | tf_op jit(solution)/shard_map/all_to_all | solution.py:93
  316.4 94.8 %reduce-scatter.2.cloned.1.call-start = ((), (), s32[]{:S(2)}) async-start(), calls=%async_computation.4 | async-start | bytes 2621440 | tf_op jit(solution)/shard_map/reduce_scatter | solution.py:87
  326.3 0.7 copy-start.10
  400.9 3.8 copy-start.3
  412.2 14.5 %collective-permute-start.5 = (f32[32,1024]{1,0:T(8,128)S(1)}, f32[32,1024]{1,0:T(8,128)S(1)}, u32[]{:S(2)}, u32[]{:S(2)}) collective-permute-start(f32[32,1024]{1,0:T(8,128)S(1)} %get-tuple-element.47), channel_id=1, source_target_pairs={{12,0},{13,1},{14,2},{15,3},{28,16},{29,17},{30,18},{31,19}} | collective-permute-start | bytes 393224 | tf_op jit(solution)/shard_map/ppermute | solution.py:17
  412.9 13.9 %collective-permute-start.4 = (f32[32,1024]{1,0:T(8,128)S(1)}, f32[32,1024]{1,0:T(8,128)S(1)}, u32[]{:S(2)}, u32[]{:S(2)}) collective-permute-start(f32[32,1024]{1,0:T(8,128)S(1)} %get-tuple-element.48), channel_id=1, source_target_pairs={{8,0},{12,4},{9,1},{13,5},{10,2},{14,6},{11,3},{15,7},{24,16},{28,... | collective-permute-start | bytes 393224 | tf_op jit(solution)/shard_map/ppermute | solution.py:17
  419.8 7.0 %collective-permute-start.3 = (f32[32,1024]{1,0:T(8,128)S(1)}, f32[32,1024]{1,0:T(8,128)S(1)}, u32[]{:S(2)}, u32[]{:S(2)}) collective-permute-start(f32[32,1024]{1,0:T(8,128)S(1)} %get-tuple-element.46), channel_id=1, source_target_pairs={{4,0},{8,4},{12,8},{5,1},{9,5},{13,9},{6,2},{10,6},{14,10},{7,3},{... | collective-permute-start | bytes 393224 | tf_op jit(solution)/shard_map/ppermute | solution.py:17
  422.0 5.9 %copy-start.12 = (f32[2,1,32]{2,1,0:T(1,128)S(1)}, f32[2,1,32]{2,1,0:T(1,128)}, u32[]{:S(2)}) copy-start(f32[2,1,32]{2,1,0:T(1,128)} %param.20) | copy-start | bytes 772
  422.0 6.4 %copy-start.7 = (f32[2,1,32,4096]{3,2,1,0:T(8,128)S(1)}, f32[2,1,32,4096]{3,2,1,0:T(8,128)}, u32[]{:S(2)}) copy-start(f32[2,1,32,4096]{3,2,1,0:T(8,128)} %param.19) | copy-start | bytes 3145732
Sparse Core Ops, SparseCore 0:
  9.6 150.8 all-gather.5
  190.3 75.0 all-gather.3
  326.4 69.0 reduce-scatter.1
where the time goes:
time: 453 us; the launch traced here: 448 us
  waiting for transfers between devices  291 us (64%)
  local copies, waits for them, and re-layouts  51.5 us (11%)
  matrix products  43.9 us (10%)
  other arithmetic  23.9 us (5%)
  starting transfers between devices  23 us (5%)
  between operations  14.9 us (3%)
    all_gather x1, waiting for transfers between devices, local(): lax.all_gather(inputs_local, 'feat', axis=0, tiled=True).astype(jnp.float32)  146 us
    all_to_all x1, waiting for transfers between devices, local(): lax.all_to_all(dec_local, 'feat', split_axis=2, concat_axis=1, tiled=True)  76.3 us
    all_to_all x1, waiting for transfers between devices, local(): lax.all_to_all(grad_dec_cols, 'feat', split_axis=1, concat_axis=2, tiled=...  68.4 us
    unnamed x33, local copies, waits for them, and re-layouts  31.8 us
    ppermute x6, starting transfers between devices, shifted(): lax.ppermute(value, axis, [(source, source + steps) for source in range(i...  14.3 us
    dot_general x1, matrix products, local(): jnp.dot(pre_grad, full_inputs.T, precision=highest, preferred_element_typ...  11.6 us
    dot_general x1, matrix products, local(): code_partial = jnp.einsum('kfd,dr->kfr', dec_cols, resid, precision=highest)  9.8 us
    dot_general x1, matrix products, local(): jnp.einsum('kfd,kfr->dr', dec_cols, all_sources, precision=highest)  9.1 us
  transfers between devices with their start and end apart: 11, of which 3 were waited for; matrix products, arithmetic and copies ran while one was open for 16% of the time, Pallas kernels for 0%

commit v1 on v0

v1 whole, which is shorter than its diff:
```python
import jax
import jax.numpy as jnp
from jax import lax
from jax.sharding import PartitionSpec as P

beta_one = 0.9
beta_two = 0.999
learn_rate = 0.001
adam_eps = 1e-08
step_count = 100.0
highest = lax.Precision.HIGHEST
high = lax.Precision.HIGH


def shifted(value, axis, steps):
    count = lax.axis_size(axis)
    initial, last = (max(0, -steps), min(count, count - steps))
    return lax.ppermute(value, axis, [(source, source + steps) for source in range(initial, last)])


def rotated(value, steps):
    count = lax.axis_size("feat")
    steps = steps % count
    if steps == 0:
        return value
    return lax.ppermute(value, "feat", [(s, (s + steps) % count) for s in range(count)])


def adam_update(weight, moments, grad):
    first = beta_one * moments[0] + (1.0 - beta_one) * grad
    second = beta_two * moments[1] + (1.0 - beta_two) * grad * grad
    scaled_first = first / (1.0 - beta_one**step_count)
    scaled_second = second / (1.0 - beta_two**step_count)
    updated = weight - learn_rate * scaled_first / (jnp.sqrt(scaled_second) + adam_eps)
    return (updated, jnp.stack([first, second]))


def slab_of(value, steps, width):
    count = lax.axis_size("feat")
    place = lax.rem(lax.axis_index("feat") + steps, count) * width
    return lax.dynamic_slice_in_dim(value, place, width, axis=value.ndim - 1)


def in_order(slabs):
    count = len(slabs)
    width = slabs[0].shape[-1]
    full = jnp.zeros(slabs[0].shape[:-1] + (count * width,), slabs[0].dtype)
    for steps, slab in enumerate(slabs):
        place = lax.rem(lax.axis_index("feat") + steps, count) * width
        full = lax.dynamic_update_slice_in_dim(full, slab, place, axis=full.ndim - 1)
    return full


def local(
    inputs,
    targets,
    enc_weight,
    enc_bias,
    dec_weight,
    dec_bias,
    enc_moments,
    enc_bias_moments,
    dec_moments,
    dec_bias_moments,
    block_lists,
    block_counts,
    slot_block,
):
    inputs_local = inputs[0].astype(jnp.float32)
    targets_local = targets[0].astype(jnp.float32)
    enc_local = enc_weight[0]
    encb_local = enc_bias[0]
    dec_local = dec_weight[0]
    decb_local = dec_bias[0]
    reach_count = dec_local.shape[0]
    width, row_count = inputs_local.shape
    feats = enc_local.shape[0]
    count = lax.axis_size("feat")
    tile_count = block_counts.shape[1]
    tile_rows = row_count // tile_count
    live = jnp.arange(block_lists.shape[2])[None, :] < block_counts[0][:, None]
    hits = (block_lists[0] == slot_block[0]) & live
    tile_active = jnp.any(hits, axis=1).astype(jnp.float32)
    row_mask = jnp.repeat(tile_active, tile_rows, axis=0)[None, :]

    enc_cols = jnp.concatenate(
        [rotated(slab_of(enc_local, j, width), j) for j in range(count)], axis=0
    )
    dec_cols = jnp.concatenate(
        [rotated(slab_of(dec_local, j, width), j) for j in range(count)], axis=1
    )
    partial = jnp.dot(
        enc_cols, inputs_local, precision=highest, preferred_element_type=jnp.float32
    ).reshape(count, feats, row_count)
    pre = encb_local[:, None] + sum(rotated(partial[j], -j) for j in range(count))
    codes = jnp.maximum(pre, 0.0) * row_mask
    own = jnp.concatenate([rotated(codes, j) for j in range(count)], axis=0)
    sources = jnp.stack([own] + [shifted(own, "layer", k) for k in range(1, reach_count)])
    recon = jnp.einsum("kfd,kfr->dr", dec_cols, sources, precision=high) + decb_local[:, None]
    resid = recon - targets_local
    code_parts = jnp.einsum("kfd,dr->kfr", dec_cols, resid, precision=high)
    grad_dec_cols = jnp.einsum("kfr,dr->kfd", sources, resid, precision=high)
    code_sum = code_parts[0]
    for k in range(1, reach_count):
        code_sum = code_sum + shifted(code_parts[k], "layer", -k)
    code_sum = code_sum.reshape(count, feats, row_count)
    code_grad = sum(rotated(code_sum[j], -j) for j in range(count))
    pre_grad = code_grad * row_mask * (pre > 0.0).astype(jnp.float32)
    pre_grads = jnp.concatenate([rotated(pre_grad, j) for j in range(count)], axis=0)
    grad_enc_cols = jnp.einsum("fr,dr->fd", pre_grads, inputs_local, precision=high)
    grad_enc_cols = grad_enc_cols.reshape(count, feats, width)
    grad_dec_cols = grad_dec_cols.reshape(reach_count, count, feats, width)
    grad_dec = in_order([rotated(grad_dec_cols[:, j], -j) for j in range(count)])
    grad_enc = in_order([rotated(grad_enc_cols[j], -j) for j in range(count)])
    grad_dec_bias = jnp.sum(resid, axis=1)
    grad_enc_bias = jnp.sum(pre_grad, axis=1)
    enc_new, enc_mom = adam_update(enc_local, enc_moments[:, 0], grad_enc)
    encb_new, encb_mom = adam_update(encb_local, enc_bias_moments[:, 0], grad_enc_bias)
    dec_new, dec_mom = adam_update(dec_local, dec_moments[:, 0], grad_dec)
    decb_new, decb_mom = adam_update(decb_local, dec_bias_moments[:, 0], grad_dec_bias)
    return (
        enc_new[None],
        encb_new[None],
        dec_new[None],
        decb_new[None],
        enc_mom[:, None],
        encb_mom[:, None],
        dec_mom[:, None],
        decb_mom[:, None],
    )


def solution(mesh):
    cols = P(("group", "layer"), "feat", None)
    vec = P(("group", "layer"), "feat")
    dec = P(("group", "layer"), None, "feat", None)
    cols_mom = P(None, ("group", "layer"), "feat", None)
    vec_mom = P(None, ("group", "layer"), "feat")
    dec_mom = P(None, ("group", "layer"), None, "feat", None)
    return jax.shard_map(
        local,
        mesh=mesh,
        in_specs=(
            cols,
            cols,
            cols,
            vec,
            dec,
            vec,
            cols_mom,
            vec_mom,
            dec_mom,
            vec_mom,
            P(("group", "layer"), None, None),
            P(("group", "layer"), None),
            P(("group", "layer")),
        ),
        out_specs=(cols, vec, dec, vec, cols_mom, vec_mom, dec_mom, vec_mom),
        check_vma=False,
    )
```

time: 453 us -> 221 us (0.49)
  waiting for transfers between devices: 291 us -> 123 us
  local copies, waits for them, and re-layouts: 51.5 us -> 8.72 us
  starting transfers between devices: 23 us -> 56.4 us
  matrix products: 43.9 us -> 18.6 us
  between operations: 14.9 us -> 1.71 us
  other arithmetic: 23.9 us -> 11.6 us
    all_gather x2 -> x0, waiting for transfers between devices: 146 us -> none  [the longest x1 146 us: local(): lax.all_gather(inputs_local, 'feat', axis=0, tiled=True).astype(jnp.float32)]
    all_to_all x2 -> x0, waiting for transfers between devices: 145 us -> none  [the longest x1 76.3 us: local(): lax.all_to_all(dec_local, 'feat', split_axis=2, concat_axis=1, tiled=True)]
    ppermute x0 -> x24, waiting for transfers between devices: none -> 90.5 us  [rotated(): lax.ppermute(value, 'feat', [(s, (s + steps) % count) for s in range(coun...]
    ppermute x0 -> x24, starting transfers between devices: none -> 47.4 us  [rotated(): lax.ppermute(value, 'feat', [(s, (s + steps) % count) for s in range(coun...]
    ppermute x6, waiting for transfers between devices: 0.02 us -> 32.6 us  [shifted(): lax.ppermute(value, axis, [(source, source + steps) for source in range(i...]
    unnamed x33 -> x25, local copies, waits for them, and re-layouts: 31.8 us -> 4 us
    dot_general x5, matrix products: 43.9 us -> 18.6 us  [the longest x1 6.28 us: local(): jnp.einsum('kfd,kfr->dr', dec_cols, sources, precision=high)]
    all_to_all x4 -> x0, local copies, waits for them, and re-layouts: 15.3 us -> none  [the longest x2 8.05 us: local(): lax.all_to_all(grad_dec_cols, 'feat', split_axis=1, concat_axis=2, tiled=...]
  transfers between devices with their start and end apart: 11 -> 30, of which waited for: 3 -> 16; matrix products, arithmetic and copies ran while one was open for 16% -> 7% of each run, Pallas kernels for 0% -> 0%
where the time goes in v1:
time: 221 us; the launch traced here: 220 us
  waiting for transfers between devices  123 us (56%)
  starting transfers between devices  56.4 us (26%)
  matrix products  18.6 us (8%)
  other arithmetic  11.6 us (5%)
  local copies, waits for them, and re-layouts  8.72 us (4%)
    ppermute x24, waiting for transfers between devices, rotated(): lax.ppermute(value, 'feat', [(s, (s + steps) % count) for s in range(coun...  90.5 us
    ppermute x24, starting transfers between devices, rotated(): lax.ppermute(value, 'feat', [(s, (s + steps) % count) for s in range(coun...  47.4 us
    ppermute x6, waiting for transfers between devices, shifted(): lax.ppermute(value, axis, [(source, source + steps) for source in range(i...  32.6 us
    ppermute x6, starting transfers between devices, shifted(): lax.ppermute(value, axis, [(source, source + steps) for source in range(i...  9 us
    dot_general x1, matrix products, local(): jnp.einsum('kfd,kfr->dr', dec_cols, sources, precision=high)  6.28 us
    dot_general x1, matrix products, local(): grad_dec_cols = jnp.einsum('kfr,dr->kfd', sources, resid, precision=high)  4.91 us
    dot_general x1, matrix products, local(): code_parts = jnp.einsum('kfd,dr->kfr', dec_cols, resid, precision=high)  4.88 us
    another operation x4, other arithmetic, adam_update(): return (updated, jnp.stack([first, second]))  4.56 us
  transfers between devices with their start and end apart: 30, of which 16 were waited for; matrix products, arithmetic and copies ran while one was open for 7% of the time, Pallas kernels for 0%

profile of v1, /device:TPU:2, one launch (start us, length us, event | category | flops | bytes accessed | tf_op | source)
XLA Modules:
  0.0 220.1 jit_solution(10771524472751675074)
XLA Ops:
  0.7 1.3 dynamic-slice_bitcast_fusion.7
  2.0 3.7 %collective-permute-start.2 = (f32[32,1024]{1,0:T(8,128)S(1)}, f32[32,1024]{1,0:T(8,128)S(1)}, u32[]{:S(2)}, u32[]{:S(2)}) collective-permute-start(f32[32,1024]{1,0:T(8,128)S(1)} %get-tuple-element.64), channel_id=1, source_target_pairs={{0,3},{1,0},{2,1},{3,2},{4,7},{5,4},{6,5},{7,6},{8,11},{9,8},{10,9... | collective-permute-start | bytes 393224 | tf_op jit(solution)/shard_map/ppermute | solution.py:26
  6.6 2.9 %collective-permute-done.2 = f32[32,1024]{1,0:T(8,128)S(1)} collective-permute-done((f32[32,1024]{1,0:T(8,128)S(1)}, f32[32,1024]{1,0:T(8,128)S(1)}, u32[]{:S(2)}, u32[]{:S(2)}) %collective-permute-start.2) | collective-permute-done | bytes 131104 | tf_op jit(solution)/shard_map/ppermute | solution.py:26
  9.5 7.3 %collective-permute-done.1 = f32[32,1024]{1,0:T(8,128)S(1)} collective-permute-done((f32[32,1024]{1,0:T(8,128)S(1)}, f32[32,1024]{1,0:T(8,128)S(1)}, u32[]{:S(2)}, u32[]{:S(2)}) %collective-permute-start.1) | collective-permute-done | bytes 131104 | tf_op jit(solution)/shard_map/ppermute | solution.py:26
  19.3 1.9 collective-permute-start.4
  21.3 2.9 %collective-permute-start.3 = (f32[32,1024]{1,0:T(8,128)}, f32[32,1024]{1,0:T(8,128)}, u32[]{:S(2)}, u32[]{:S(2)}) collective-permute-start(f32[32,1024]{1,0:T(8,128)} %get-tuple-element.59), channel_id=1, source_target_pairs={{0,3},{1,0},{2,1},{3,2},{4,7},{5,4},{6,5},{7,6},{8,11},{9,8},{10,9... | collective-permute-start | bytes 393224 | tf_op jit(solution)/shard_map/ppermute | solution.py:26
  27.1 4.1 %collective-permute-done.4 = f32[32,1024]{1,0:T(8,128)S(1)} collective-permute-done((f32[32,1024]{1,0:T(8,128)}, f32[32,1024]{1,0:T(8,128)S(1)}, u32[]{:S(2)}, u32[]{:S(2)}) %collective-permute-start.4) | collective-permute-done | bytes 131104 | tf_op jit(solution)/shard_map/ppermute | solution.py:26
  32.2 15.5 %collective-permute-start.11 = (f32[32,1024]{1,0:T(8,128)S(1)}, f32[32,1024]{1,0:T(8,128)S(1)}, u32[]{:S(2)}, u32[]{:S(2)}) collective-permute-start(f32[32,1024]{1,0:T(8,128)S(1)} %get-tuple-element.32), channel_id=1, source_target_pairs={{0,3},{1,0},{2,1},{3,2},{4,7},{5,4},{6,5},{7,6},{8,11},{9,8},{10,9... | collective-permute-start | bytes 393224 | tf_op jit(solution)/shard_map/ppermute | solution.py:26
  48.4 2.3 %collective-permute-start.7 = (f32[4,32,1024]{2,1,0:T(8,128)}, f32[4,32,1024]{2,1,0:T(8,128)}, u32[]{:S(2)}, u32[]{:S(2)}) collective-permute-start(f32[4,32,1024]{2,1,0:T(8,128)} %get-tuple-element.44), channel_id=1, source_target_pairs={{0,2},{1,3},{2,0},{3,1},{4,6},{5,7},{6,4},{7,5},{8,10},{9,11},{10,... | collective-permute-start | bytes 1572872 | tf_op jit(solution)/shard_map/ppermute | solution.py:26
  52.2 28.8 %collective-permute-done.10 = f32[32,1024]{1,0:T(8,128)S(1)} collective-permute-done((f32[32,1024]{1,0:T(8,128)S(1)}, f32[32,1024]{1,0:T(8,128)S(1)}, u32[]{:S(2)}, u32[]{:S(2)}) %collective-permute-start.10) | collective-permute-done | bytes 131104 | tf_op jit(solution)/shard_map/ppermute | solution.py:26
  82.0 1.6 collective-permute-start.14
  84.9 2.1 collective-permute-start.12
  87.0 3.9 %copy.31 = bf16[1,1024,1024]{1,2,0:T(8,128)(2,1)} copy(bf16[1,1024,1024]{2,1,0:T(8,128)(2,1)} %param.14) | data formatting | bytes 4194304 | tf_op args[1]
  91.7 16.2 %collective-permute-done.13 = f32[128,1024]{1,0:T(8,128)} collective-permute-done((f32[128,1024]{1,0:T(8,128)}, f32[128,1024]{1,0:T(8,128)}, u32[]{:S(2)}, u32[]{:S(2)}) %collective-permute-start.13) | collective-permute-done | bytes 524320 | tf_op jit(solution)/shard_map/ppermute | solution.py:18
  108.5 6.3 %fusion.61 = (f32[1024]{0:T(1024)S(1)}, f32[1024,1024]{0,1:T(8,128)S(1)}) fusion(bf16[1,1024,1024]{1,2,0:T(8,128)(2,1)} %copy.31, f32[1024]{0:T(1024)S(1)} %bitcast.152, f32[1,128,1024]{2,1,0:T(8,128)} %bitcast.18, f32[1,128,1024]{2,1,0:T(8,128)} %bitcast.17, f32[1,128,1024]{2,1,0:T(8,128)} %bitcast.16, f32[1,128,1024]{2,1,0:T(8,128)S(1)} %get-tuple-element.57, ...), kind=kOutput, calls=%fused_computation.104 | convolution fusion | flops 3228564480 | bytes 10493952 | tf_op jit(solution)/shard_map/kfd,kfr->dr/dot_general | solution.py:99
  114.8 4.9 %fusion = f32[4,128,1024]{2,1,0:T(8,128)S(1)} fusion(f32[1024,1024]{0,1:T(8,128)S(1)} %get-tuple-element.67, f32[1,128,1024]{2,1,0:T(8,128)} %bitcast.18, f32[1,128,1024]{2,1,0:T(8,128)} %bitcast.17, f32[1,128,1024]{2,1,0:T(8,128)} %bitcast.16, f32[1,128,1024]{2,1,0:T(8,128)S(1)} %get-tuple-element.57), kind=kOutput, calls=%fused_computation.2 | convolution fusion | flops 3222798336 | bytes 8388608 | tf_op jit(solution)/shard_map/kfr,dr->kfd/dot_general | solution.py:102
  119.8 4.9 %fusion.2 = f32[4,128,1024]{2,1,0:T(8,128)S(1)} fusion(f32[1024,1024]{0,1:T(8,128)S(1)} %get-tuple-element.67, f32[4,32,1024]{2,1,0:T(8,128)} %collective-permute-done.8, f32[4,32,1024]{2,1,0:T(8,128)} %collective-permute-done.7, f32[4,32,1024]{2,1,0:T(8,128)} %collective-permute-done.6, f32[4,32,1024]{2,1,0:T(8,128)S(1)} %get-tuple-element.43), kind=kOutput, calls=%fused_computation.4 | convolution fusion | flops 3222798336 | bytes 8388608 | tf_op jit(solution)/shard_map/kfd,dr->kfr/dot_general | solution.py:101
  125.5 1.4 collective-permute-start.16
  126.9 1.9 collective-permute-start.15
  130.8 2.0 collective-permute-start.29
  132.8 6.4 %collective-permute-done.16 = f32[128,1024]{1,0:T(8,128)S(1)} collective-permute-done((f32[128,1024]{1,0:T(8,128)S(1)}, f32[128,1024]{1,0:T(8,128)S(1)}, u32[]{:S(2)}, u32[]{:S(2)}) %collective-permute-start.16) | collective-permute-done | bytes 524320 | tf_op jit(solution)/shard_map/ppermute | solution.py:18
  139.2 9.3 %collective-permute-done.15 = f32[128,1024]{1,0:T(8,128)S(1)} collective-permute-done((f32[128,1024]{1,0:T(8,128)S(1)}, f32[128,1024]{1,0:T(8,128)S(1)}, u32[]{:S(2)}, u32[]{:S(2)}) %collective-permute-start.15) | collective-permute-done | bytes 524320 | tf_op jit(solution)/shard_map/ppermute | solution.py:18
  148.9 3.7 %collective-permute-start.18 = (f32[32,1024]{1,0:T(8,128)S(1)}, f32[32,1024]{1,0:T(8,128)S(1)}, u32[]{:S(2)}, u32[]{:S(2)}) collective-permute-start(f32[32,1024]{1,0:T(8,128)S(1)} %get-tuple-element.54), channel_id=1, source_target_pairs={{0,3},{1,0},{2,1},{3,2},{4,7},{5,4},{6,5},{7,6},{8,11},{9,8},{10,9... | collective-permute-start | bytes 393224 | tf_op jit(solution)/shard_map/ppermute | solution.py:26
  152.6 28.2 %collective-permute-done.28 = f32[4,32,1024]{2,1,0:T(8,128)S(1)} collective-permute-done((f32[4,32,1024]{2,1,0:T(8,128)S(1)}, f32[4,32,1024]{2,1,0:T(8,128)S(1)}, u32[]{:S(2)}, u32[]{:S(2)}) %collective-permute-start.28) | collective-permute-done | bytes 524320 | tf_op jit(solution)/shard_map/ppermute | solution.py:26
  181.0 2.8 %fusion.10 = (f32[1,4,32,4096]{3,2,1,0:T(8,128)S(1)}, f32[1,4,32,4096]{3,2,1,0:T(8,128)S(1)}, f32[1,4,32,4096]{3,2,1,0:T(8,128)}) fusion(f32[4,32,4096]{2,1,0:T(8,128)S(1)} %constant_dynamic-update-slice_fusion, f32[2,1,4,32,4096]{4,3,2,1,0:T(8,128)S(1)} %copy-done.3, f32[1,4,32,4096]{3,2,1,0:T(8,128)S(1)} %copy-done.2), kind=kLoop, calls=%fused_computation.20 | loop fusion | flops 6291456 | bytes 14680064 | tf_op jit(solution)/shard_map/stack | solution.py:35
  184.0 6.8 %collective-permute-start.23 = (f32[32,1024]{1,0:T(8,128)S(1)}, f32[32,1024]{1,0:T(8,128)S(1)}, u32[]{:S(2)}, u32[]{:S(2)}) collective-permute-start(f32[32,1024]{1,0:T(8,128)S(1)} %get-tuple-element.31), channel_id=1, source_target_pairs={{0,3},{1,0},{2,1},{3,2},{4,7},{5,4},{6,5},{7,6},{8,11},{9,8},{10,9... | collective-permute-start | bytes 393224 | tf_op jit(solution)/shard_map/ppermute | solution.py:26
  191.5 2.5 %maximum_bitcast_fusion = f32[2,1,4,32,4096]{4,3,2,1,0:T(8,128)} fusion(f32[1,4,32,4096]{3,2,1,0:T(8,128)S(1)} %get-tuple-element.35, f32[1,4,32,4096]{3,2,1,0:T(8,128)S(1)} %get-tuple-element.34), kind=kLoop, calls=%fused_computation | loop fusion | flops 1048576 | bytes 8388608 | tf_op jit(solution)/shard_map/broadcast_in_dim | solution.py:128
  194.8 7.7 %collective-permute-done.22 = f32[32,1024]{1,0:T(8,128)S(1)} collective-permute-done((f32[32,1024]{1,0:T(8,128)S(1)}, f32[32,1024]{1,0:T(8,128)S(1)}, u32[]{:S(2)}, u32[]{:S(2)}) %collective-permute-start.22) | collective-permute-done | bytes 131104 | tf_op jit(solution)/shard_map/ppermute | solution.py:26
  202.5 1.5 fusion.6
  204.1 1.4 collective-permute-start.24
  207.6 2.0 collective-permute-start.26
  209.8 8.0 %collective-permute-done.25 = f32[32,1024]{1,0:T(8,128)S(1)} collective-permute-done((f32[32,1024]{1,0:T(8,128)S(1)}, f32[32,1024]{1,0:T(8,128)S(1)}, u32[]{:S(2)}, u32[]{:S(2)}) %collective-permute-start.25) | collective-permute-done | bytes 131104 | tf_op jit(solution)/shard_map/ppermute | solution.py:26
  (91 shorter events, 22.1 us)
Async XLA Ops:
  2.0 7.6 %collective-permute-start.2 = (f32[32,1024]{1,0:T(8,128)S(1)}, f32[32,1024]{1,0:T(8,128)S(1)}, u32[]{:S(2)}, u32[]{:S(2)}) collective-permute-start(f32[32,1024]{1,0:T(8,128)S(1)} %get-tuple-element.64), channel_id=1, source_target_pairs={{0,3},{1,0},{2,1},{3,2},{4,7},{5,4},{6,5},{7,6},{8,11},{9,8},{10,9... | collective-permute-start | bytes 393224 | tf_op jit(solution)/shard_map/ppermute | solution.py:26
  5.6 11.2 %collective-permute-start.1 = (f32[32,1024]{1,0:T(8,128)S(1)}, f32[32,1024]{1,0:T(8,128)S(1)}, u32[]{:S(2)}, u32[]{:S(2)}) collective-permute-start(f32[32,1024]{1,0:T(8,128)S(1)} %get-tuple-element.65), channel_id=1, source_target_pairs={{0,2},{1,3},{2,0},{3,1},{4,6},{5,7},{6,4},{7,5},{8,10},{9,11},{10,... | collective-permute-start | bytes 393224 | tf_op jit(solution)/shard_map/ppermute | solution.py:26
  5.6 11.2 %collective-permute-start = (f32[32,1024]{1,0:T(8,128)S(1)}, f32[32,1024]{1,0:T(8,128)S(1)}, u32[]{:S(2)}, u32[]{:S(2)}) collective-permute-start(f32[32,1024]{1,0:T(8,128)S(1)} %get-tuple-element.63), channel_id=1, source_target_pairs={{0,1},{1,2},{2,3},{3,0},{4,5},{5,6},{6,7},{7,4},{8,9},{9,10},{10,1... | collective-permute-start | bytes 393224 | tf_op jit(solution)/shard_map/ppermute | solution.py:26
  18.6 8.5 %collective-permute-start.5 = (f32[32,1024]{1,0:T(8,128)}, f32[32,1024]{1,0:T(8,128)S(1)}, u32[]{:S(2)}, u32[]{:S(2)}) collective-permute-start(f32[32,1024]{1,0:T(8,128)} %get-tuple-element.60), channel_id=1, source_target_pairs={{0,1},{1,2},{2,3},{3,0},{4,5},{5,6},{6,7},{7,4},{8,9},{9,10},{10,1... | collective-permute-start | bytes 393224 | tf_op jit(solution)/shard_map/ppermute | solution.py:26
  19.3 11.8 %collective-permute-start.4 = (f32[32,1024]{1,0:T(8,128)}, f32[32,1024]{1,0:T(8,128)S(1)}, u32[]{:S(2)}, u32[]{:S(2)}) collective-permute-start(f32[32,1024]{1,0:T(8,128)} %get-tuple-element.61), channel_id=1, source_target_pairs={{0,2},{1,3},{2,0},{3,1},{4,6},{5,7},{6,4},{7,5},{8,10},{9,11},{10,... | collective-permute-start | bytes 393224 | tf_op jit(solution)/shard_map/ppermute | solution.py:26
  21.3 9.9 %collective-permute-start.3 = (f32[32,1024]{1,0:T(8,128)}, f32[32,1024]{1,0:T(8,128)}, u32[]{:S(2)}, u32[]{:S(2)}) collective-permute-start(f32[32,1024]{1,0:T(8,128)} %get-tuple-element.59), channel_id=1, source_target_pairs={{0,3},{1,0},{2,1},{3,2},{4,7},{5,4},{6,5},{7,6},{8,11},{9,8},{10,9... | collective-permute-start | bytes 393224 | tf_op jit(solution)/shard_map/ppermute | solution.py:26
  25.4 59.5 %collective-permute-start.8 = (f32[4,32,1024]{2,1,0:T(8,128)}, f32[4,32,1024]{2,1,0:T(8,128)}, u32[]{:S(2)}, u32[]{:S(2)}) collective-permute-start(f32[4,32,1024]{2,1,0:T(8,128)} %get-tuple-element.46), channel_id=1, source_target_pairs={{0,3},{1,0},{2,1},{3,2},{4,7},{5,4},{6,5},{7,6},{8,11},{9,8},{10,9... | collective-permute-start | bytes 1572872 | tf_op jit(solution)/shard_map/ppermute | solution.py:26
  32.2 19.5 %collective-permute-start.11 = (f32[32,1024]{1,0:T(8,128)S(1)}, f32[32,1024]{1,0:T(8,128)S(1)}, u32[]{:S(2)}, u32[]{:S(2)}) collective-permute-start(f32[32,1024]{1,0:T(8,128)S(1)} %get-tuple-element.32), channel_id=1, source_target_pairs={{0,3},{1,0},{2,1},{3,2},{4,7},{5,4},{6,5},{7,6},{8,11},{9,8},{10,9... | collective-permute-start | bytes 393224 | tf_op jit(solution)/shard_map/ppermute | solution.py:26
  47.7 33.4 %collective-permute-start.10 = (f32[32,1024]{1,0:T(8,128)S(1)}, f32[32,1024]{1,0:T(8,128)S(1)}, u32[]{:S(2)}, u32[]{:S(2)}) collective-permute-start(f32[32,1024]{1,0:T(8,128)S(1)} %get-tuple-element.32), channel_id=1, source_target_pairs={{0,2},{1,3},{2,0},{3,1},{4,6},{5,7},{6,4},{7,5},{8,10},{9,11},{10,... | collective-permute-start | bytes 393224 | tf_op jit(solution)/shard_map/ppermute | solution.py:26
  47.7 33.4 %collective-permute-start.9 = (f32[32,1024]{1,0:T(8,128)S(1)}, f32[32,1024]{1,0:T(8,128)S(1)}, u32[]{:S(2)}, u32[]{:S(2)}) collective-permute-start(f32[32,1024]{1,0:T(8,128)S(1)} %get-tuple-element.32), channel_id=1, source_target_pairs={{0,1},{1,2},{2,3},{3,0},{4,5},{5,6},{6,7},{7,4},{8,9},{9,10},{10,1... | collective-permute-start | bytes 393224 | tf_op jit(solution)/shard_map/ppermute | solution.py:26
  48.4 43.3 %collective-permute-start.7 = (f32[4,32,1024]{2,1,0:T(8,128)}, f32[4,32,1024]{2,1,0:T(8,128)}, u32[]{:S(2)}, u32[]{:S(2)}) collective-permute-start(f32[4,32,1024]{2,1,0:T(8,128)} %get-tuple-element.44), channel_id=1, source_target_pairs={{0,2},{1,3},{2,0},{3,1},{4,6},{5,7},{6,4},{7,5},{8,10},{9,11},{10,... | collective-permute-start | bytes 1572872 | tf_op jit(solution)/shard_map/ppermute | solution.py:26
  51.7 40.0 %collective-permute-start.6 = (f32[4,32,1024]{2,1,0:T(8,128)}, f32[4,32,1024]{2,1,0:T(8,128)}, u32[]{:S(2)}, u32[]{:S(2)}) collective-permute-start(f32[4,32,1024]{2,1,0:T(8,128)} %get-tuple-element.45), channel_id=1, source_target_pairs={{0,1},{1,2},{2,3},{3,0},{4,5},{5,6},{6,7},{7,4},{8,9},{9,10},{10,1... | collective-permute-start | bytes 1572872 | tf_op jit(solution)/shard_map/ppermute | solution.py:26
  82.0 9.7 %collective-permute-start.14 = (f32[128,1024]{1,0:T(8,128)}, f32[128,1024]{1,0:T(8,128)}, u32[]{:S(2)}, u32[]{:S(2)}) collective-permute-start(f32[128,1024]{1,0:T(8,128)} %get-tuple-element.58), channel_id=1, source_target_pairs={{0,12},{1,13},{2,14},{3,15},{16,28},{17,29},{18,30},{19,31}} | collective-permute-start | bytes 1572872 | tf_op jit(solution)/shard_map/ppermute | solution.py:18
  83.6 24.3 %collective-permute-start.13 = (f32[128,1024]{1,0:T(8,128)}, f32[128,1024]{1,0:T(8,128)}, u32[]{:S(2)}, u32[]{:S(2)}) collective-permute-start(f32[128,1024]{1,0:T(8,128)} %get-tuple-element.58), channel_id=1, source_target_pairs={{0,8},{4,12},{1,9},{5,13},{2,10},{6,14},{3,11},{7,15},{16,24},{20,... | collective-permute-start | bytes 1572872 | tf_op jit(solution)/shard_map/ppermute | solution.py:18
  84.9 23.6 %collective-permute-start.12 = (f32[128,1024]{1,0:T(8,128)}, f32[128,1024]{1,0:T(8,128)}, u32[]{:S(2)}, u32[]{:S(2)}) collective-permute-start(f32[128,1024]{1,0:T(8,128)} %get-tuple-element.58), channel_id=1, source_target_pairs={{0,4},{4,8},{8,12},{1,5},{5,9},{9,13},{2,6},{6,10},{10,14},{3,7},{... | collective-permute-start | bytes 1572872 | tf_op jit(solution)/shard_map/ppermute | solution.py:18
  124.8 6.0 %collective-permute-start.17 = (f32[128,1024]{1,0:T(8,128)S(1)}, f32[128,1024]{1,0:T(8,128)S(1)}, u32[]{:S(2)}, u32[]{:S(2)}) collective-permute-start(f32[128,1024]{1,0:T(8,128)S(1)} %get-tuple-element.41), channel_id=1, source_target_pairs={{12,0},{13,1},{14,2},{15,3},{28,16},{29,17},{30,18},{31,19}} | collective-permute-start | bytes 1572872 | tf_op jit(solution)/shard_map/ppermute | solution.py:18
  125.5 13.7 %collective-permute-start.16 = (f32[128,1024]{1,0:T(8,128)S(1)}, f32[128,1024]{1,0:T(8,128)S(1)}, u32[]{:S(2)}, u32[]{:S(2)}) collective-permute-start(f32[128,1024]{1,0:T(8,128)S(1)} %get-tuple-element.42), channel_id=1, source_target_pairs={{8,0},{12,4},{9,1},{13,5},{10,2},{14,6},{11,3},{15,7},{24,16},{28,... | collective-permute-start | bytes 1572872 | tf_op jit(solution)/shard_map/ppermute | solution.py:18
  126.9 21.6 %collective-permute-start.15 = (f32[128,1024]{1,0:T(8,128)S(1)}, f32[128,1024]{1,0:T(8,128)S(1)}, u32[]{:S(2)}, u32[]{:S(2)}) collective-permute-start(f32[128,1024]{1,0:T(8,128)S(1)} %get-tuple-element.40), channel_id=1, source_target_pairs={{4,0},{8,4},{12,8},{5,1},{9,5},{13,9},{6,2},{10,6},{14,10},{7,3},{... | collective-permute-start | bytes 1572872 | tf_op jit(solution)/shard_map/ppermute | solution.py:18
  128.9 19.9 %collective-permute-start.27 = (f32[4,32,1024]{2,1,0:T(8,128)S(1)}, f32[4,32,1024]{2,1,0:T(8,128)S(1)}, u32[]{:S(2)}, u32[]{:S(2)}) collective-permute-start(f32[4,32,1024]{2,1,0:T(8,128)S(1)} %get-tuple-element.39), channel_id=1, source_target_pairs={{0,3},{1,0},{2,1},{3,2},{4,7},{5,4},{6,5},{7,6},{8,11},{9,8},{10,9... | collective-permute-start | bytes 1572872 | tf_op jit(solution)/shard_map/ppermute | solution.py:26
  129.2 51.7 %collective-permute-start.28 = (f32[4,32,1024]{2,1,0:T(8,128)S(1)}, f32[4,32,1024]{2,1,0:T(8,128)S(1)}, u32[]{:S(2)}, u32[]{:S(2)}) collective-permute-start(f32[4,32,1024]{2,1,0:T(8,128)S(1)} %get-tuple-element.38), channel_id=1, source_target_pairs={{0,2},{1,3},{2,0},{3,1},{4,6},{5,7},{6,4},{7,5},{8,10},{9,11},{10,... | collective-permute-start | bytes 1572872 | tf_op jit(solution)/shard_map/ppermute | solution.py:26
  130.8 50.1 %collective-permute-start.29 = (f32[4,32,1024]{2,1,0:T(8,128)S(1)}, f32[4,32,1024]{2,1,0:T(8,128)S(1)}, u32[]{:S(2)}, u32[]{:S(2)}) collective-permute-start(f32[4,32,1024]{2,1,0:T(8,128)S(1)} %get-tuple-element.37), channel_id=1, source_target_pairs={{0,1},{1,2},{2,3},{3,0},{4,5},{5,6},{6,7},{7,4},{8,9},{9,10},{10,1... | collective-permute-start | bytes 1572872 | tf_op jit(solution)/shard_map/ppermute | solution.py:26
  148.5 32.5 %copy-start.3 = (f32[2,1,4,32,4096]{4,3,2,1,0:T(8,128)S(1)}, f32[2,1,4,32,4096]{4,3,2,1,0:T(8,128)}, u32[]{:S(2)}) copy-start(f32[2,1,4,32,4096]{4,3,2,1,0:T(8,128)} %param.21) | copy-start | bytes 12582916
  148.6 32.4 %copy-start.2 = (f32[1,4,32,4096]{3,2,1,0:T(8,128)S(1)}, f32[1,4,32,4096]{3,2,1,0:T(8,128)}, u32[]{:S(2)}) copy-start(f32[1,4,32,4096]{3,2,1,0:T(8,128)} %param.17) | copy-start | bytes 6291460
  148.7 35.1 %collective-permute-start.20 = (f32[32,1024]{1,0:T(8,128)S(1)}, f32[32,1024]{1,0:T(8,128)S(1)}, u32[]{:S(2)}, u32[]{:S(2)}) collective-permute-start(f32[32,1024]{1,0:T(8,128)S(1)} %get-tuple-element.55), channel_id=1, source_target_pairs={{0,1},{1,2},{2,3},{3,0},{4,5},{5,6},{6,7},{7,4},{8,9},{9,10},{10,1... | collective-permute-start | bytes 393224 | tf_op jit(solution)/shard_map/ppermute | solution.py:26
  148.8 35.1 %collective-permute-start.19 = (f32[32,1024]{1,0:T(8,128)S(1)}, f32[32,1024]{1,0:T(8,128)S(1)}, u32[]{:S(2)}, u32[]{:S(2)}) collective-permute-start(f32[32,1024]{1,0:T(8,128)S(1)} %get-tuple-element.56), channel_id=1, source_target_pairs={{0,2},{1,3},{2,0},{3,1},{4,6},{5,7},{6,4},{7,5},{8,10},{9,11},{10,... | collective-permute-start | bytes 393224 | tf_op jit(solution)/shard_map/ppermute | solution.py:26
  148.9 35.0 %collective-permute-start.18 = (f32[32,1024]{1,0:T(8,128)S(1)}, f32[32,1024]{1,0:T(8,128)S(1)}, u32[]{:S(2)}, u32[]{:S(2)}) collective-permute-start(f32[32,1024]{1,0:T(8,128)S(1)} %get-tuple-element.54), channel_id=1, source_target_pairs={{0,3},{1,0},{2,1},{3,2},{4,7},{5,4},{6,5},{7,6},{8,11},{9,8},{10,9... | collective-permute-start | bytes 393224 | tf_op jit(solution)/shard_map/ppermute | solution.py:26
  184.0 10.8 %collective-permute-start.23 = (f32[32,1024]{1,0:T(8,128)S(1)}, f32[32,1024]{1,0:T(8,128)S(1)}, u32[]{:S(2)}, u32[]{:S(2)}) collective-permute-start(f32[32,1024]{1,0:T(8,128)S(1)} %get-tuple-element.31), channel_id=1, source_target_pairs={{0,3},{1,0},{2,1},{3,2},{4,7},{5,4},{6,5},{7,6},{8,11},{9,8},{10,9... | collective-permute-start | bytes 393224 | tf_op jit(solution)/shard_map/ppermute | solution.py:26
  190.8 11.7 %collective-permute-start.22 = (f32[32,1024]{1,0:T(8,128)S(1)}, f32[32,1024]{1,0:T(8,128)S(1)}, u32[]{:S(2)}, u32[]{:S(2)}) collective-permute-start(f32[32,1024]{1,0:T(8,128)S(1)} %get-tuple-element.31), channel_id=1, source_target_pairs={{0,2},{1,3},{2,0},{3,1},{4,6},{5,7},{6,4},{7,5},{8,10},{9,11},{10,... | collective-permute-start | bytes 393224 | tf_op jit(solution)/shard_map/ppermute | solution.py:26
  190.8 11.7 %collective-permute-start.21 = (f32[32,1024]{1,0:T(8,128)S(1)}, f32[32,1024]{1,0:T(8,128)S(1)}, u32[]{:S(2)}, u32[]{:S(2)}) collective-permute-start(f32[32,1024]{1,0:T(8,128)S(1)} %get-tuple-element.31), channel_id=1, source_target_pairs={{0,1},{1,2},{2,3},{3,0},{4,5},{5,6},{6,7},{7,4},{8,9},{9,10},{10,1... | collective-permute-start | bytes 393224 | tf_op jit(solution)/shard_map/ppermute | solution.py:26
  204.1 5.7 %collective-permute-start.24 = (f32[32,1024]{1,0:T(8,128)S(1)}, f32[32,1024]{1,0:T(8,128)S(1)}, u32[]{:S(2)}, u32[]{:S(2)}) collective-permute-start(f32[32,1024]{1,0:T(8,128)S(1)} %get-tuple-element.52), channel_id=1, source_target_pairs={{0,3},{1,0},{2,1},{3,2},{4,7},{5,4},{6,5},{7,6},{8,11},{9,8},{10,9... | collective-permute-start | bytes 393224 | tf_op jit(solution)/shard_map/ppermute | solution.py:26
  206.0 11.8 %collective-permute-start.25 = (f32[32,1024]{1,0:T(8,128)S(1)}, f32[32,1024]{1,0:T(8,128)S(1)}, u32[]{:S(2)}, u32[]{:S(2)}) collective-permute-start(f32[32,1024]{1,0:T(8,128)S(1)} %get-tuple-element.51), channel_id=1, source_target_pairs={{0,2},{1,3},{2,0},{3,1},{4,6},{5,7},{6,4},{7,5},{8,10},{9,11},{10,... | collective-permute-start | bytes 393224 | tf_op jit(solution)/shard_map/ppermute | solution.py:26
  207.6 10.2 %collective-permute-start.26 = (f32[32,1024]{1,0:T(8,128)S(1)}, f32[32,1024]{1,0:T(8,128)S(1)}, u32[]{:S(2)}, u32[]{:S(2)}) collective-permute-start(f32[32,1024]{1,0:T(8,128)S(1)} %get-tuple-element.50), channel_id=1, source_target_pairs={{0,1},{1,2},{2,3},{3,0},{4,5},{5,6},{6,7},{7,4},{8,9},{9,10},{10,1... | collective-permute-start | bytes 393224 | tf_op jit(solution)/shard_map/ppermute | solution.py:26
  (10 other events, 148.4 us)

commit v2 on v1

v2 whole, which is shorter than its diff:
```python
import functools

import jax
import jax.numpy as jnp
from jax import lax
from jax.experimental import pallas as pl
from jax.experimental.pallas import tpu as pltpu
from jax.sharding import PartitionSpec as P

beta_one = 0.9
beta_two = 0.999
learn_rate = 0.001
adam_eps = 1e-08
step_count = 100.0
highest = lax.Precision.HIGHEST
lanes = 128
log_two = 0.6931471805599453
levels = 32767.0
vmem_bytes = 60 * 1024 * 1024
held_types = (jnp.float32, jnp.bfloat16, jnp.int16)


def shifted(value, axis, steps):
    count = lax.axis_size(axis)
    initial, last = (max(0, -steps), min(count, count - steps))
    return lax.ppermute(value, axis, [(source, source + steps) for source in range(initial, last)])


def rotated(value, steps, first_layer=0):
    count = lax.axis_size("feat")
    steps = steps % count
    if steps == 0:
        return value
    pairs = [
        (layer * count + s, layer * count + (s + steps) % count)
        for layer in range(first_layer, lax.axis_size("layer"))
        for s in range(count)
    ]
    return lax.ppermute(value, ("layer", "feat"), pairs)


def adam_update(weight, moments, grad):
    first = beta_one * moments[0] + (1.0 - beta_one) * grad
    second = beta_two * moments[1] + (1.0 - beta_two) * grad * grad
    scaled_first = first / (1.0 - beta_one**step_count)
    scaled_second = second / (1.0 - beta_two**step_count)
    updated = weight - learn_rate * scaled_first / (jnp.sqrt(scaled_second) + adam_eps)
    return (updated, jnp.stack([first, second]))


def slab_of(value, steps, width):
    count = lax.axis_size("feat")
    place = lax.rem(lax.axis_index("feat") + steps, count) * width
    return lax.dynamic_slice_in_dim(value, place, width, axis=value.ndim - 1)


def code_into(out_ref, rows, value):
    width = value.shape[1]
    top = jnp.max(jnp.abs(value), axis=1, keepdims=True)
    exponent = jnp.ceil(jnp.log(jnp.maximum(top, 1e-30)) * (8.0 / log_two))
    scale = levels * jnp.exp(exponent * (-log_two / 8.0))
    whole = jnp.clip(jnp.round(value * scale), -levels, levels)
    out_ref[rows, 0:width] = whole.astype(jnp.int32).astype(jnp.int16)
    tail = jnp.broadcast_to(exponent, (value.shape[0], lanes))
    out_ref[rows, width : width + lanes] = tail.astype(jnp.int32).astype(jnp.int16)


def step_of(exponent):
    return jnp.exp(exponent.astype(jnp.float32) * (log_two / 8.0)) * (1.0 / levels)


def decoded(ref, rows):
    width = ref.shape[1] - lanes
    whole = ref[rows, 0:width].astype(jnp.int32).astype(jnp.float32)
    exponent = ref[rows, width : width + lanes].astype(jnp.int32)[:, 0:1]
    return whole * step_of(exponent)


def split(value):
    upper = value.astype(jnp.bfloat16)
    return upper, (value - upper.astype(jnp.float32)).astype(jnp.bfloat16)


def product(left, right, dims):
    dot = functools.partial(
        lax.dot_general, dimension_numbers=(dims, ((), ())), preferred_element_type=jnp.float32
    )
    return dot(left[0], right[0]) + (dot(left[0], right[1]) + dot(left[1], right[0]))


def blocks_of(size, block):
    block = min(size, block)
    return [slice(start, start + block) for start in range(0, size, block)]


def held_bytes(array):
    size = array.dtype.itemsize
    if len(array.shape) == 1:
        return 4096
    rows, columns = array.shape[-2:]
    tile = 32 // size
    rows, columns = -(-rows // tile) * tile, -(-columns // lanes) * lanes
    for extent in array.shape[:-2]:
        rows = rows * extent
    return rows * columns * size


def call(kernel, out_shape, args, flops=0, scratch=(), after=(), far=(), far_out=()):
    size = sum(a.size * a.dtype.itemsize for a in [*far, *args])
    size += sum(o.size * o.dtype.itemsize for o in [*far_out, *out_shape])
    distant, taken, skipped = len(far), len(args), len(after)
    need = sum(held_bytes(a) for a in [*args, *out_shape]) + 4 * 1024 * 1024
    need += sum(held_bytes(a) for a in scratch if a.dtype in held_types)

    def body(*refs):
        kernel(*refs[: distant + taken], *refs[distant + taken + skipped :])

    spaces = [pltpu.HBM] * distant
    spaces += [pltpu.SMEM if a.shape == (1,) else pltpu.VMEM for a in args]
    spaces += [pl.ANY] * skipped
    out_spaces = [pltpu.HBM] * len(far_out) + [pltpu.VMEM] * len(out_shape)
    return pl.pallas_call(
        body,
        out_shape=(*far_out, *out_shape),
        in_specs=[pl.BlockSpec(memory_space=space) for space in spaces],
        out_specs=tuple(pl.BlockSpec(memory_space=space) for space in out_spaces),
        scratch_shapes=list(scratch),
        cost_estimate=pl.CostEstimate(flops=flops, bytes_accessed=size, transcendentals=0),
        compiler_params=pltpu.CompilerParams(vmem_limit_bytes=max(need, vmem_bytes if far else 0)),
    )(*far, *args, *after)


def buffer_like(array):
    return pltpu.VMEM(array.shape, array.dtype)


class Fetched:
    def __init__(self, sources, buffers, semaphores):
        self.copies = [
            pltpu.make_async_copy(source, held, semaphores.at[i])
            for i, (source, held) in enumerate(zip(sources, buffers, strict=True))
        ]
        self.buffers = buffers
        for copy in self.copies:
            copy.start()

    def __getitem__(self, i):
        self.copies[i].wait()
        return self.buffers[i]


def shape(rows, columns, dtype=jnp.float32):
    return jax.ShapeDtypeStruct((rows, columns), dtype)


def coded_shape(rows, columns):
    return jax.ShapeDtypeStruct((rows, columns + lanes), jnp.int16)


def pack_kernel(count, first, last, me_ref, in_ref, *outs):
    reach, feats, total = in_ref.shape
    width = total // count
    for j in range(count):
        place = pl.multiple_of(lax.rem(me_ref[0] + j, count) * width, lanes)
        for k in range(first, last):
            rows = slice((k - first) * feats, (k - first + 1) * feats)
            code_into(outs[j], rows, in_ref[k, :, pl.ds(place, width)])


def packed(me, weights, first, last, after=()):
    count = lax.axis_size("feat")
    reach, feats, total = weights.shape
    out = coded_shape((last - first) * feats, total // count)
    kernel = functools.partial(pack_kernel, count, first, last)
    return call(kernel, [out] * count, [me, weights], after=after)


def adam_kernel(count, starts, me_ref, *refs):
    grads, (weight_ref, moments_ref, new_ref, new_moments_ref) = refs[:-4], refs[-4:]
    k = pl.program_id(0)
    feats, total = weight_ref.shape[1:]
    width = total // count

    def update(j, grad):
        place = pl.multiple_of(lax.rem(me_ref[0] + j, count) * width, lanes)
        cols = pl.ds(place, width)
        first = beta_one * moments_ref[0, 0, :, cols] + (1.0 - beta_one) * grad
        second = beta_two * moments_ref[1, 0, :, cols] + (1.0 - beta_two) * grad * grad
        new_moments_ref[0, 0, :, cols] = first
        new_moments_ref[1, 0, :, cols] = second
        scaled_first = first * (learn_rate / (1.0 - beta_one**step_count))
        scaled_second = second * (1.0 / (1.0 - beta_two**step_count))
        new_ref[0, :, cols] = weight_ref[0, :, cols] - scaled_first / (
            jnp.sqrt(scaled_second) + adam_eps
        )

    for part, (start, stop) in enumerate(starts):

        @pl.when((k >= start) & (k < stop))
        def _(part=part):
            for j in range(count):
                update(j, decoded(grads[part * count + j], slice(None)))


def adam_call(me, starts, grads, weight, moments, after=()):
    count = lax.axis_size("feat")
    reach, feats, total = weight.shape
    skipped = len(after)

    def body(*refs):
        adam_kernel(count, starts, *refs[: len(grads) + 3], *refs[len(grads) + 3 + skipped :])

    def grad_spec(start, stop):
        coded_width = total // count + lanes
        return pl.BlockSpec(
            (feats, coded_width), lambda k: (jnp.clip(k - start, 0, stop - start - 1), 0)
        )

    weight_spec = pl.BlockSpec((1, feats, total), lambda k: (k, 0, 0))
    moments_spec = pl.BlockSpec((2, 1, feats, total), lambda k: (0, k, 0, 0))
    return pl.pallas_call(
        body,
        grid=(reach,),
        out_shape=(
            jax.ShapeDtypeStruct(weight.shape, weight.dtype),
            jax.ShapeDtypeStruct(moments.shape, moments.dtype),
        ),
        in_specs=[pl.BlockSpec(memory_space=pltpu.SMEM)]
        + [grad_spec(*limits) for limits in starts for _ in range(count)]
        + [weight_spec, moments_spec]
        + [pl.BlockSpec(memory_space=pl.ANY)] * skipped,
        out_specs=(weight_spec, moments_spec),
        cost_estimate=pl.CostEstimate(
            flops=20 * weight.size, bytes_accessed=26 * weight.size, transcendentals=weight.size
        ),
        compiler_params=pltpu.CompilerParams(vmem_limit_bytes=24 * 1024 * 1024),
    )(me, *grads, weight, moments, *after)


def gather_kernel(*refs):
    *parts, out_ref = refs
    feats = parts[0].shape[0]
    for j, part in enumerate(parts):
        out_ref[j * feats : (j + 1) * feats, :] = part[...]


def codes_kernel(count, *refs):
    parts, bias_ref, mask_ref, codes_ref, coded_ref = refs[:count], *refs[count:]
    pre = bias_ref[...] + sum(part[...] for part in parts)
    codes = jnp.maximum(pre, 0.0) * mask_ref[...]
    codes_ref[...] = codes
    code_into(coded_ref, slice(None), codes)


def resid_kernel(count, reach, feats, starts, *refs):
    parts = len(starts)
    sources = parts * count + count + reach - 1 + 2
    fars, refs = refs[:sources], refs[sources:]
    res_out, src_out, refs = refs[0:2], refs[2:4], refs[4:]
    part_ref, refs = refs[0], refs[1:]
    coded_parts, refs = refs[: reach - 1], refs[reach - 1 :]
    sum_ref, refs = refs[0], refs[1:]
    buffers, refs = refs[:sources], refs[sources:]
    w_full, s_full, w_up, w_low, res_up, res_low, src_up, src_low, arrive, leave = refs
    held = Fetched(fars, buffers, arrive)
    block = count * feats
    owns, moves = parts * count, parts * count + count
    near = [held[owns + j] for j in range(count)]
    for j in range(count):
        s_full[j * feats : (j + 1) * feats, :] = decoded(near[j], slice(None))
    for part, (start, stop) in enumerate(starts):
        for j in range(count):
            weights = held[part * count + j]
            for k in range(start, stop):
                rows = slice(k * block + j * feats, k * block + (j + 1) * feats)
                w_full[rows, :] = decoded(weights, slice((k - start) * feats, (k - start + 1) * feats))
    for k in range(1, reach):
        moved = held[moves + k - 1]
        for rows in blocks_of(block, 32):
            s_full[k * block + rows.start : k * block + rows.stop, :] = decoded(moved, rows)
    for rows in blocks_of(reach * block, 32):
        w_up[rows, :], w_low[rows, :] = split(w_full[rows, :])
        src_up[rows, :], src_low[rows, :] = split(s_full[rows, :])
    sends = [
        pltpu.make_async_copy(source, out, leave.at[i])
        for i, (source, out) in enumerate(zip((src_up, src_low), src_out))
    ]
    targets_ref, bias_ref = held[sources - 2], held[sources - 1]
    for send in sends:
        send.start()
    width, row_count = targets_ref.shape
    chunk = min(256, width)

    def recon_chunk(i, carry):
        cols = pl.ds(pl.multiple_of(i * chunk, chunk), chunk)
        recon = product(
            (w_up[:, cols], w_low[:, cols]), (src_up[...], src_low[...]), ((0,), (0,))
        )
        resid = recon + bias_ref[cols, :] - targets_ref[cols, :].astype(jnp.float32)
        sum_ref[cols, :] = jnp.sum(resid, axis=1, keepdims=True)
        res_up[cols, :], res_low[cols, :] = split(resid)
        return carry

    lax.fori_loop(0, width // chunk, recon_chunk, 0)
    more = [
        pltpu.make_async_copy(source, out, leave.at[2 + i])
        for i, (source, out) in enumerate(zip((res_up, res_low), res_out))
    ]
    for send in more:
        send.start()
    span = min(256, row_count)

    def part_chunk(i, carry):
        cols = pl.ds(pl.multiple_of(i * span, span), span)
        s_full[:, cols] = product(
            (w_up[...], w_low[...]), (res_up[:, cols], res_low[:, cols]), ((1,), (0,))
        )
        return carry

    lax.fori_loop(0, row_count // span, part_chunk, 0)
    part_ref[...] = s_full[0:block, :]
    for k in range(1, reach):
        for rows in blocks_of(block, 32):
            source = slice(k * block + rows.start, k * block + rows.stop)
            code_into(coded_parts[k - 1], rows, s_full[source, :])
    for send in [*sends, *more]:
        send.wait()


def grad_dec_kernel(count, feats, starts, *refs):
    src_far, res_far, refs = refs[0:2], refs[2:4], refs[4:]
    outs, refs = refs[: len(starts) * count], refs[len(starts) * count :]
    src_up, src_low, res_up, res_low, grad, arrive = refs
    width = res_up.shape[0]
    chunk = min(256, width)
    held = Fetched(
        [*src_far] + [far.at[pl.ds(i, chunk)] for i in range(0, width, chunk) for far in res_far],
        [src_up, src_low]
        + [ref.at[pl.ds(i, chunk)] for i in range(0, width, chunk) for ref in (res_up, res_low)],
        arrive,
    )
    source = (held[0][...], held[1][...])
    for i in range(width // chunk):
        right = (held[2 + 2 * i][...], held[3 + 2 * i][...])
        grad[:, i * chunk : (i + 1) * chunk] = product(source, right, ((1,), (1,)))
    for part, (start, stop) in enumerate(starts):
        for j in range(count):
            for k in range(start, stop):
                row = (k * count + j) * feats
                rows = slice((k - start) * feats, (k - start + 1) * feats)
                code_into(outs[part * count + j], rows, grad[row : row + feats, :])


def code_sum_kernel(count, feats, moved_count, *refs):
    own, moved, outs = refs[0], refs[1 : 1 + moved_count], refs[1 + moved_count :]
    for j in range(count):
        rows = slice(j * feats, (j + 1) * feats)
        total = own[rows, :]
        for ref in moved:
            total = total + decoded(ref, rows)
        if j == 0:
            outs[0][...] = total
        else:
            code_into(outs[j], slice(None), total)


def pre_grad_kernel(count, *refs):
    own, arrived, codes_ref, coded_ref, sum_ref = refs[0], refs[1:count], *refs[count:]
    total = own[...]
    for ref in arrived:
        total = total + decoded(ref, slice(None))
    pre_grad = jnp.where(codes_ref[...] > 0.0, total, 0.0)
    sum_ref[...] = jnp.sum(pre_grad, axis=1, keepdims=True)
    code_into(coded_ref, slice(None), pre_grad)


def grad_enc_kernel(count, feats, *refs):
    grads, inputs_ref, outs, full, grad = refs[:count], refs[count], *[refs[count + 1 : -2]], *refs[-2:]
    for j in range(count):
        full[j * feats : (j + 1) * feats, :] = decoded(grads[j], slice(None))
    upper, lower = split(full[...])
    width = inputs_ref.shape[0]
    chunk = min(256, width)
    dot = functools.partial(
        lax.dot_general,
        dimension_numbers=(((1,), (1,)), ((), ())),
        preferred_element_type=jnp.float32,
    )
    for rows in blocks_of(width, chunk):
        right = inputs_ref[rows, :]
        grad[:, rows] = dot(upper, right) + dot(lower, right)
    for j in range(count):
        code_into(outs[j], slice(None), grad[j * feats : (j + 1) * feats, :])


def local(
    inputs,
    targets,
    enc_weight,
    enc_bias,
    dec_weight,
    dec_bias,
    enc_moments,
    enc_bias_moments,
    dec_moments,
    dec_bias_moments,
    block_lists,
    block_counts,
    slot_block,
):
    inputs_local = inputs[0]
    targets_local = targets[0]
    enc_local = enc_weight[0]
    encb_local = enc_bias[0]
    dec_local = dec_weight[0]
    decb_local = dec_bias[0]
    reach = dec_local.shape[0]
    width, row_count = inputs_local.shape
    feats = enc_local.shape[0]
    count = lax.axis_size("feat")
    block = count * feats
    depth = reach * block
    tile_count = block_counts.shape[1]
    tile_rows = row_count // tile_count
    live = jnp.arange(block_lists.shape[2])[None, :] < block_counts[0][:, None]
    hits = (block_lists[0] == slot_block[0]) & live
    tile_active = jnp.any(hits, axis=1).astype(jnp.float32)
    row_mask = jnp.repeat(tile_active, tile_rows, axis=0)[None, :]

    enc_cols = jnp.concatenate(
        [rotated(slab_of(enc_local, j, width), j) for j in range(count)], axis=0
    )
    me = lax.axis_index("feat").astype(jnp.int32).reshape(1)
    starts = ((0, reach - 1), (reach - 1, reach)) if reach > 1 else ((0, reach),)
    dec_cols = []
    for first, last in starts[1:]:
        sent = packed(me, dec_local, first, last)
        dec_cols += [rotated(sent[j], j, first) for j in range(count)]
    partial = jnp.dot(
        enc_cols,
        inputs_local.astype(jnp.float32),
        precision=highest,
        preferred_element_type=jnp.float32,
    ).reshape(count, feats, row_count)
    partials = [rotated(partial[j], -j) for j in range(count)]
    codes, coded_codes = call(
        functools.partial(codes_kernel, count),
        [shape(feats, row_count), coded_shape(feats, row_count)],
        [*partials, encb_local[:, None], row_mask],
        after=dec_cols[1:count],
    )
    own = [rotated(coded_codes, j) for j in range(count)]
    gathered = call(gather_kernel, [coded_shape(block, row_count)], own)[0]
    moved = [shifted(gathered, "layer", k) for k in range(1, reach)]
    sent = packed(me, dec_local, *starts[0], after=[coded_codes])
    dec_cols = [rotated(sent[j], j) for j in range(count)] + dec_cols
    half = jnp.bfloat16
    far = [*dec_cols, *own, *moved, targets_local, decb_local[:, None]]
    outs = call(
        functools.partial(resid_kernel, count, reach, feats, starts),
        [shape(block, row_count)]
        + [coded_shape(block, row_count)] * (reach - 1)
        + [shape(width, 1)],
        [],
        flops=12 * depth * width * row_count,
        scratch=[buffer_like(a) for a in far]
        + [pltpu.VMEM((depth, width), jnp.float32), pltpu.VMEM((depth, row_count), jnp.float32)]
        + [pltpu.VMEM((depth, width), half)] * 2
        + [pltpu.VMEM((width, row_count), half)] * 2
        + [pltpu.VMEM((depth, row_count), half)] * 2
        + [pltpu.SemaphoreType.DMA((len(far),)), pltpu.SemaphoreType.DMA((4,))],
        far=far,
        far_out=[shape(width, row_count, half)] * 2 + [shape(depth, row_count, half)] * 2,
    )
    res, src, part, parts, grad_dec_bias = outs[0:2], outs[2:4], outs[4], outs[5:-1], outs[-1]
    returned = [shifted(parts[k - 1], "layer", -k) for k in range(1, reach)]

    grad_parts = call(
        functools.partial(grad_dec_kernel, count, feats, starts),
        [coded_shape((last - first) * feats, width) for first, last in starts for _ in range(count)],
        [],
        flops=6 * depth * width * row_count,
        scratch=[pltpu.VMEM((depth, row_count), half)] * 2
        + [pltpu.VMEM((width, row_count), half)] * 2
        + [pltpu.VMEM((depth, width), jnp.float32)]
        + [pltpu.SemaphoreType.DMA((2 + 2 * (width // min(256, width)),))],
        far=[*src, *res],
    )
    grad_dec_cols = [
        rotated(grad_parts[part * count + j], -j, first if part else 0)
        for part, (first, last) in enumerate(starts)
        for j in range(count)
    ]
    sums = call(
        functools.partial(code_sum_kernel, count, feats, reach - 1),
        [shape(feats, row_count)] + [coded_shape(feats, row_count)] * (count - 1),
        [part, *returned],
        after=[grad_parts[0]],
    )
    arrived = [rotated(sums[j], -j) for j in range(count)]
    coded_grad, grad_enc_bias = call(
        functools.partial(pre_grad_kernel, count),
        [coded_shape(feats, row_count), shape(feats, 1)],
        [*arrived, codes],
        after=grad_dec_cols[1:count],
    )
    pre_grads = [rotated(coded_grad, j) for j in range(count)]
    grad_enc_cols = call(
        functools.partial(grad_enc_kernel, count, feats),
        [coded_shape(feats, width)] * count,
        [*pre_grads, inputs_local],
        flops=4 * block * width * row_count,
        scratch=[
            pltpu.VMEM((block, row_count), jnp.float32),
            pltpu.VMEM((block, width), jnp.float32),
        ],
    )
    dec_new, dec_mom = adam_call(
        me, starts, grad_dec_cols, dec_local, dec_moments[:, 0], after=[grad_enc_cols[0]]
    )
    enc_arrived = [rotated(grad_enc_cols[j], -j) for j in range(count)]
    enc_new, enc_mom = adam_call(me, ((0, 1),), enc_arrived, enc_local[None], enc_moments)
    encb_new, encb_mom = adam_update(encb_local, enc_bias_moments[:, 0], grad_enc_bias[:, 0])
    decb_new, decb_mom = adam_update(decb_local, dec_bias_moments[:, 0], grad_dec_bias[:, 0])
    return (
        enc_new,
        encb_new[None],
        dec_new[None],
        decb_new[None],
        enc_mom,
        encb_mom[:, None],
        dec_mom[:, None],
        decb_mom[:, None],
    )


def solution(mesh):
    cols = P(("group", "layer"), "feat", None)
    vec = P(("group", "layer"), "feat")
    dec = P(("group", "layer"), None, "feat", None)
    cols_mom = P(None, ("group", "layer"), "feat", None)
    vec_mom = P(None, ("group", "layer"), "feat")
    dec_mom = P(None, ("group", "layer"), None, "feat", None)
    return jax.shard_map(
        local,
        mesh=mesh,
        in_specs=(
            cols,
            cols,
            cols,
            vec,
            dec,
            vec,
            cols_mom,
            vec_mom,
            dec_mom,
            vec_mom,
            P(("group", "layer"), None, None),
            P(("group", "layer"), None),
            P(("group", "layer")),
        ),
        out_specs=(cols, vec, dec, vec, cols_mom, vec_mom, dec_mom, vec_mom),
        check_vma=False,
    )
```

time: 221 us -> 162 us (0.73)
  waiting for transfers between devices: 123 us -> 49.1 us
  Pallas kernels: 0 us -> 34.5 us
  matrix products: 18.6 us -> 1.05 us
  other arithmetic: 11.6 us -> 3.28 us
  local copies, waits for them, and re-layouts: 8.72 us -> 13.2 us
    ppermute x24 -> x30, waiting for transfers between devices: 90.5 us -> 47.5 us  [rotated(): return lax.ppermute(value, ('layer', 'feat'), pairs)]
    pallas_call x0 -> x11, Pallas kernels: none -> 34.5 us  [the longest x9 28.2 us: call(): pl.pallas_call(body, out_shape=(*far_out, *out_shape), in_specs=[pl.Block...]
    ppermute x6, waiting for transfers between devices: 32.6 us -> 1.58 us  [shifted(): lax.ppermute(value, axis, [(source, source + steps) for source in range(i...]
    dot_general x5 -> x1, matrix products: 18.6 us -> 1.05 us  [local(): jnp.dot(enc_cols, inputs_local.astype(jnp.float32), precision=highest, pr...]
    unnamed x25 -> x59, local copies, waits for them, and re-layouts: 4 us -> 10.8 us
    another operation x4 -> x1, other arithmetic: 4.56 us -> 0.57 us  [adam_update(): return (updated, jnp.stack([first, second]))]
    broadcast_in_dim x2 -> x1, other arithmetic: 3.51 us -> 0.01 us  [local(): decb_mom[:, None]]
    ppermute x6, starting transfers between devices: 9 us -> 12 us  [shifted(): lax.ppermute(value, axis, [(source, source + steps) for source in range(i...]
  transfers between devices with their start and end apart: 30 -> 36, of which waited for: 16 -> 13; matrix products, arithmetic and copies ran while one was open for 7% -> 4% of each run, Pallas kernels for 0% -> 12%
where the time goes in v2:
time: 162 us; the launch traced here: 160 us
  starting transfers between devices  57.6 us (36%)
  waiting for transfers between devices  49.1 us (30%)
  Pallas kernels  34.5 us (21%)
  local copies, waits for them, and re-layouts  13.2 us (8%)
  other arithmetic  3.28 us (2%)
  between operations  1.78 us (1%)
    ppermute x30, waiting for transfers between devices, rotated(): return lax.ppermute(value, ('layer', 'feat'), pairs)  47.5 us
    ppermute x30, starting transfers between devices, rotated(): return lax.ppermute(value, ('layer', 'feat'), pairs)  45.6 us
    pallas_call x9, Pallas kernels, call(): pl.pallas_call(body, out_shape=(*far_out, *out_shape), in_specs=[pl.Block...  28.2 us
    ppermute x6, starting transfers between devices, shifted(): lax.ppermute(value, axis, [(source, source + steps) for source in range(i...  12 us
    unnamed x59, local copies, waits for them, and re-layouts  10.8 us
    pallas_call x2, Pallas kernels, adam_call(): pl.pallas_call(body, grid=(reach,), out_shape=(jax.ShapeDtypeStruct(weigh...  6.32 us
  transfers between devices with their start and end apart: 36, of which 13 were waited for; matrix products, arithmetic and copies ran while one was open for 4% of the time, Pallas kernels for 12%

profile of v2, /device:TPU:2, one launch (start us, length us, event | category | flops | bytes accessed | tf_op | source)
XLA Modules:
  0.0 160.5 jit_solution(2797918226064439214)
XLA Ops:
  1.8 2.7 %collective-permute-start.1 = (f32[32,1024]{1,0:T(8,128)S(1)}, f32[32,1024]{1,0:T(8,128)S(1)}, u32[]{:S(2)}, u32[]{:S(2)}) collective-permute-start(f32[32,1024]{1,0:T(8,128)S(1)} %get-tuple-element.117), channel_id=1, source_target_pairs={{0,2},{1,3},{2,0},{3,1},{4,6},{5,7},{6,4},{7,5},{8,10},{9,11},{10,... | collective-permute-start | bytes 393224 | tf_op jit(solution)/shard_map/ppermute | solution.py:39
  4.5 1.6 collective-permute-start
  6.0 2.2 %collective-permute-start.2 = (f32[32,1024]{1,0:T(8,128)S(1)}, f32[32,1024]{1,0:T(8,128)S(1)}, u32[]{:S(2)}, u32[]{:S(2)}) collective-permute-start(f32[32,1024]{1,0:T(8,128)S(1)} %get-tuple-element.119), channel_id=1, source_target_pairs={{0,3},{1,0},{2,1},{3,2},{4,7},{5,4},{6,5},{7,6},{8,11},{9,8},{10,9... | collective-permute-start | bytes 393224 | tf_op jit(solution)/shard_map/ppermute | solution.py:39
  8.3 1.6 copy-done
  11.4 3.4 %collective-permute-done.1 = f32[32,1024]{1,0:T(8,128)S(1)} collective-permute-done((f32[32,1024]{1,0:T(8,128)S(1)}, f32[32,1024]{1,0:T(8,128)S(1)}, u32[]{:S(2)}, u32[]{:S(2)}) %collective-permute-start.1) | collective-permute-done | bytes 131104 | tf_op jit(solution)/shard_map/ppermute | solution.py:39
  16.4 2.7 %collective-permute-start.5 = (f32[32,1024]{1,0:T(8,128)S(1)}, f32[32,1024]{1,0:T(8,128)S(1)}, u32[]{:S(2)}, u32[]{:S(2)}) collective-permute-start(f32[32,1024]{1,0:T(8,128)S(1)} %get-tuple-element.112), channel_id=1, source_target_pairs={{0,1},{1,2},{2,3},{3,0},{4,5},{5,6},{6,7},{7,4},{8,9},{9,10},{10,1... | collective-permute-start | bytes 393224 | tf_op jit(solution)/shard_map/ppermute | solution.py:39
  20.4 2.8 %collective-permute-start.3 = (f32[32,1024]{1,0:T(8,128)S(1)}, f32[32,1024]{1,0:T(8,128)S(1)}, u32[]{:S(2)}, u32[]{:S(2)}) collective-permute-start(f32[32,1024]{1,0:T(8,128)S(1)} %get-tuple-element.114), channel_id=1, source_target_pairs={{0,3},{1,0},{2,1},{3,2},{4,7},{5,4},{6,5},{7,6},{8,11},{9,8},{10,9... | collective-permute-start | bytes 393224 | tf_op jit(solution)/shard_map/ppermute | solution.py:39
  25.8 4.2 %collective-permute-done.4.refs_2_ = f32[32,1024]{1,0:T(8,128)S(1)} collective-permute-done((f32[32,1024]{1,0:T(8,128)S(1)}, f32[32,1024]{1,0:T(8,128)S(1)}, u32[]{:S(2)}, u32[]{:S(2)}) %collective-permute-start.4) | collective-permute-done | bytes 131104 | tf_op jit(solution)/shard_map/ppermute | solution.py:39
  31.9 4.6 %collective-permute-start.9 = (s16[96,1152]{1,0:T(8,128)(2,1)S(1)}, s16[96,1152]{1,0:T(8,128)(2,1)S(1)}, u32[]{:S(2)}, u32[]{:S(2)}) collective-permute-start(s16[96,1152]{1,0:T(8,128)(2,1)S(1)} %get-tuple-element.54), channel_id=1, source_target_pairs={{0,1},{1,2},{2,3},{3,0},{4,5},{5,6},{6,7},{7,4},{8,9},{9,10},{10,1... | collective-permute-start | bytes 663560 | tf_op jit(solution)/shard_map/ppermute | solution.py:39
  36.5 2.8 %collective-permute-start.14 = (s16[32,1152]{1,0:T(8,128)(2,1)S(1)}, s16[32,1152]{1,0:T(8,128)(2,1)S(1)}, u32[]{:S(2)}, u32[]{:S(2)}) collective-permute-start(s16[32,1152]{1,0:T(8,128)(2,1)S(1)} %get-tuple-element.52.refs_2_.refs_0_.refs_8_), channel_id=1, source_target_pairs={{0,3},{1,0},{2,1},{3,2},{4,7},{5,4},{6,5},{7,6},{8,11},{9,8},{10,9... | collective-permute-start | bytes 221192 | tf_op jit(solution)/shard_map/ppermute | solution.py:39
  39.9 2.0 %collective-permute-start.12 = (s16[32,1152]{1,0:T(8,128)(2,1)S(1)}, s16[32,1152]{1,0:T(8,128)(2,1)S(1)}, u32[]{:S(2)}, u32[]{:S(2)}) collective-permute-start(s16[32,1152]{1,0:T(8,128)(2,1)S(1)} %get-tuple-element.52.refs_2_.refs_0_.refs_8_), channel_id=1, source_target_pairs={{0,1},{1,2},{2,3},{3,0},{4,5},{5,6},{6,7},{7,4},{8,9},{9,10},{10,1... | collective-permute-start | bytes 221192 | tf_op jit(solution)/shard_map/ppermute | solution.py:39
  41.9 3.7 %collective-permute-done.14.refs_3_.refs_11_ = s16[32,1152]{1,0:T(8,128)(2,1)S(1)} collective-permute-done((s16[32,1152]{1,0:T(8,128)(2,1)S(1)}, s16[32,1152]{1,0:T(8,128)(2,1)S(1)}, u32[]{:S(2)}, u32[]{:S(2)}) %collective-permute-start.14) | collective-permute-done | bytes 73760 | tf_op jit(solution)/shard_map/ppermute | solution.py:39
  45.6 5.6 %collective-permute-done.13.refs_2_.refs_10_ = s16[32,1152]{1,0:T(8,128)(2,1)S(1)} collective-permute-done((s16[32,1152]{1,0:T(8,128)(2,1)S(1)}, s16[32,1152]{1,0:T(8,128)(2,1)S(1)}, u32[]{:S(2)}, u32[]{:S(2)}) %collective-permute-start.13) | collective-permute-done | bytes 73760 | tf_op jit(solution)/shard_map/ppermute | solution.py:39
  53.8 1.9 %collective-permute-start.15 = (s16[128,1152]{1,0:T(8,128)(2,1)S(1)}, s16[128,1152]{1,0:T(8,128)(2,1)}, u32[]{:S(2)}, u32[]{:S(2)}) collective-permute-start(s16[128,1152]{1,0:T(8,128)(2,1)S(1)} %shard_map.191), channel_id=1, source_target_pairs={{0,4},{4,8},{8,12},{1,5},{5,9},{9,13},{2,6},{6,10},{10,14},{3,7},{... | collective-permute-start | bytes 884744 | tf_op jit(solution)/shard_map/ppermute | solution.py:26
  58.3 8.1 %collective-permute-done.10.refs_2_ = s16[96,1152]{1,0:T(8,128)(2,1)} collective-permute-done((s16[96,1152]{1,0:T(8,128)(2,1)S(1)}, s16[96,1152]{1,0:T(8,128)(2,1)}, u32[]{:S(2)}, u32[]{:S(2)}) %collective-permute-start.10) | collective-permute-done | bytes 221216 | tf_op jit(solution)/shard_map/ppermute | solution.py:39
  69.0 13.7 %shard_map.192 = (bf16[1024,1024]{1,0:T(8,128)(2,1)}, bf16[1024,1024]{1,0:T(8,128)(2,1)}, bf16[512,1024]{1,0:T(8,128)(2,1)}, bf16[512,1024]{1,0:T(8,128)(2,1)}, ...) custom-call(s16[96,1152]{1,0:T(8,128)(2,1)} %copy-done.20, ...), custom_call_target="tpu_custom_call" | custom-call | flops 6442450944 | bytes 12165120 | tf_op jit(solution)/shard_map/pallas_call | solution.py:122
  82.7 2.1 %collective-permute-start.18 = (s16[128,1152]{1,0:T(8,128)(2,1)}, s16[128,1152]{1,0:T(8,128)(2,1)}, u32[]{:S(2)}, u32[]{:S(2)}) collective-permute-start(s16[128,1152]{1,0:T(8,128)(2,1)} %get-tuple-element.59), channel_id=1, source_target_pairs={{4,0},{8,4},{12,8},{5,1},{9,5},{13,9},{6,2},{10,6},{14,10},{7,3},{... | collective-permute-start | bytes 884744 | tf_op jit(solution)/shard_map/ppermute | solution.py:26
  84.8 4.0 %collective-permute-start.19 = (s16[128,1152]{1,0:T(8,128)(2,1)}, s16[128,1152]{1,0:T(8,128)(2,1)}, u32[]{:S(2)}, u32[]{:S(2)}) collective-permute-start(s16[128,1152]{1,0:T(8,128)(2,1)} %get-tuple-element.60), channel_id=1, source_target_pairs={{8,0},{12,4},{9,1},{13,5},{10,2},{14,6},{11,3},{15,7},{24,16},{28,... | collective-permute-start | bytes 884744 | tf_op jit(solution)/shard_map/ppermute | solution.py:26
  90.1 10.4 %shard_map.193 = (s16[96,1152]{1,0:T(8,128)(2,1)}, s16[96,1152]{1,0:T(8,128)(2,1)}, s16[96,1152]{1,0:T(8,128)(2,1)}, s16[96,1152]{1,0:T(8,128)(2,1)}, s16[32,115...) custom-call(bf16[512,1024]{1,0:T(8,128)(2,1)} %get-tuple-element.62.refs_0_, ...), custom_call_target="tpu_custom_call" | custom-call | flops 3221225472 | bytes 7471104 | tf_op jit(solution)/shard_map/pallas_call | solution.py:122
  100.5 4.9 %collective-permute-start.24 = (s16[96,1152]{1,0:T(8,128)(2,1)}, s16[96,1152]{1,0:T(8,128)(2,1)S(1)}, u32[]{:S(2)}, u32[]{:S(2)}) collective-permute-start(s16[96,1152]{1,0:T(8,128)(2,1)} %get-tuple-element.72), channel_id=1, source_target_pairs={{0,3},{1,0},{2,1},{3,2},{4,7},{5,4},{6,5},{7,6},{8,11},{9,8},{10,9... | collective-permute-start | bytes 663560 | tf_op jit(solution)/shard_map/ppermute | solution.py:39
  109.1 1.5 shard_map.194
  110.6 3.7 %collective-permute-start.21 = (s16[32,1152]{1,0:T(8,128)(2,1)S(1)}, s16[32,1152]{1,0:T(8,128)(2,1)S(1)}, u32[]{:S(2)}, u32[]{:S(2)}) collective-permute-start(s16[32,1152]{1,0:T(8,128)(2,1)S(1)} %get-tuple-element.68), channel_id=1, source_target_pairs={{0,3},{1,0},{2,1},{3,2},{4,7},{5,4},{6,5},{7,6},{8,11},{9,8},{10,9... | collective-permute-start | bytes 221192 | tf_op jit(solution)/shard_map/ppermute | solution.py:39
  115.7 13.6 %collective-permute-done.25.refs_6_.refs_3_ = s16[96,1152]{1,0:T(8,128)(2,1)S(1)} collective-permute-done((s16[96,1152]{1,0:T(8,128)(2,1)}, s16[96,1152]{1,0:T(8,128)(2,1)S(1)}, u32[]{:S(2)}, u32[]{:S(2)}) %collective-permute-start.25) | collective-permute-done | bytes 221216 | tf_op jit(solution)/shard_map/ppermute | solution.py:39
  130.6 1.8 %collective-permute-done.22.refs_2_ = s16[32,1152]{1,0:T(8,128)(2,1)S(1)} collective-permute-done((s16[32,1152]{1,0:T(8,128)(2,1)S(1)}, s16[32,1152]{1,0:T(8,128)(2,1)S(1)}, u32[]{:S(2)}, u32[]{:S(2)}) %collective-permute-start.22) | collective-permute-done | bytes 73760 | tf_op jit(solution)/shard_map/ppermute | solution.py:39
  135.5 1.9 %collective-permute-start.27 = (s16[32,1152]{1,0:T(8,128)(2,1)S(1)}, s16[32,1152]{1,0:T(8,128)(2,1)S(1)}, u32[]{:S(2)}, u32[]{:S(2)}) collective-permute-start(s16[32,1152]{1,0:T(8,128)(2,1)S(1)} %get-tuple-element.75.refs_0_), channel_id=1, source_target_pairs={{0,1},{1,2},{2,3},{3,0},{4,5},{5,6},{6,7},{7,4},{8,9},{9,10},{10,1... | collective-permute-start | bytes 221192 | tf_op jit(solution)/shard_map/ppermute | solution.py:39
  139.9 4.5 %collective-permute-done.28.refs_2_ = s16[32,1152]{1,0:T(8,128)(2,1)S(1)} collective-permute-done((s16[32,1152]{1,0:T(8,128)(2,1)S(1)}, s16[32,1152]{1,0:T(8,128)(2,1)S(1)}, u32[]{:S(2)}, u32[]{:S(2)}) %collective-permute-start.28) | collective-permute-done | bytes 73760 | tf_op jit(solution)/shard_map/ppermute | solution.py:39
  144.4 1.6 copy-done.3
  146.0 1.7 %shard_map.196 = (s16[32,1152]{1,0:T(8,128)(2,1)S(1)}, s16[32,1152]{1,0:T(8,128)(2,1)S(1)}, s16[32,1152]{1,0:T(8,128)(2,1)S(1)}, s16[32,1152]{1,0:T(8,128)(2,1)S(1)}) custom-call(s16[32,1152]{1,0:T(8,128)(2,1)S(1)} %get-tuple-element.75.refs_0_, s16[32,1152]{1,0:T(8,128)(2,1)S(1)} %collective-permute-done.27.refs_1_, ...), custom_call_target="tpu_custom_call" | custom-call | flops 536870912 | bytes 2686976 | tf_op jit(solution)/shard_map/pallas_call | solution.py:122
  148.5 1.9 %collective-permute-start.32 = (s16[32,1152]{1,0:T(8,128)(2,1)S(1)}, s16[32,1152]{1,0:T(8,128)(2,1)S(1)}, u32[]{:S(2)}, u32[]{:S(2)}) collective-permute-start(s16[32,1152]{1,0:T(8,128)(2,1)S(1)} %get-tuple-element.79), channel_id=1, source_target_pairs={{0,1},{1,2},{2,3},{3,0},{4,5},{5,6},{6,7},{7,4},{8,9},{9,10},{10,1... | collective-permute-start | bytes 221192 | tf_op jit(solution)/shard_map/ppermute | solution.py:39
  151.1 2.2 %copy-done.4 = f32[2,1,4,32,4096]{4,3,2,1,0:T(8,128)S(1)} copy-done((f32[2,1,4,32,4096]{4,3,2,1,0:T(8,128)S(1)}, f32[2,1,4,32,4096]{4,3,2,1,0:T(8,128)}, u32[]{:S(2)}) %copy-start.4) | copy-done | bytes 4194328
  154.1 4.6 %shard_map.198 = (f32[4,32,4096]{2,1,0:T(8,128)}, f32[2,4,32,4096]{3,2,1,0:T(8,128)}) custom-call(s32[1]{0:T(128)} %bitcast.refs_0_, s16[96,1152]{1,0:T(8,128)(2,1)S(1)} %copy-done.8, s16[96,1152]{1,0:T(8,128)(2,1)S(1)} %collective-permute-done.24.refs_5_.refs_2_, s16[96,1152]{1,0:T(8,128)(2,1)S(1)} %collective-permute-done.25.refs_6_.refs_3_, ...), custom_call_target="tpu_custom_call" | custom-call | flops 10485760 | bytes 13631488 | tf_op jit(solution)/shard_map/pallas_call | solution.py:221
  158.8 1.7 %shard_map.197 = (f32[1,32,4096]{2,1,0:T(8,128)}, f32[2,1,32,4096]{3,2,1,0:T(8,128)}) custom-call(s32[1]{0:T(128)} %bitcast.refs_0_, s16[32,1152]{1,0:T(8,128)(2,1)S(1)} %get-tuple-element.76.refs_1_.refs_11_, s16[32,1152]{1,0:T(8,128)(2,1)S(1)} %collective-permute-done.30.refs_2_, s16[32,1152]{1,0:T(8,128)(2,1)S(1)} %collective-permute-done.31.refs_3_, ...), custom_call_target="tpu_custom_call" | custom-call | flops 2621440 | bytes 3407872 | tf_op jit(solution)/shard_map/pallas_call | solution.py:221
  (125 shorter events, 33.1 us)
Async XLA Ops:
  1.8 13.0 %collective-permute-start.1 = (f32[32,1024]{1,0:T(8,128)S(1)}, f32[32,1024]{1,0:T(8,128)S(1)}, u32[]{:S(2)}, u32[]{:S(2)}) collective-permute-start(f32[32,1024]{1,0:T(8,128)S(1)} %get-tuple-element.117), channel_id=1, source_target_pairs={{0,2},{1,3},{2,0},{3,1},{4,6},{5,7},{6,4},{7,5},{8,10},{9,11},{10,... | collective-permute-start | bytes 393224 | tf_op jit(solution)/shard_map/ppermute | solution.py:39
  4.5 10.3 %collective-permute-start = (f32[32,1024]{1,0:T(8,128)S(1)}, f32[32,1024]{1,0:T(8,128)S(1)}, u32[]{:S(2)}, u32[]{:S(2)}) collective-permute-start(f32[32,1024]{1,0:T(8,128)S(1)} %get-tuple-element.118), channel_id=1, source_target_pairs={{0,1},{1,2},{2,3},{3,0},{4,5},{5,6},{6,7},{7,4},{8,9},{9,10},{10,1... | collective-permute-start | bytes 393224 | tf_op jit(solution)/shard_map/ppermute | solution.py:39
  6.0 9.2 %collective-permute-start.2 = (f32[32,1024]{1,0:T(8,128)S(1)}, f32[32,1024]{1,0:T(8,128)S(1)}, u32[]{:S(2)}, u32[]{:S(2)}) collective-permute-start(f32[32,1024]{1,0:T(8,128)S(1)} %get-tuple-element.119), channel_id=1, source_target_pairs={{0,3},{1,0},{2,1},{3,2},{4,7},{5,4},{6,5},{7,6},{8,11},{9,8},{10,9... | collective-permute-start | bytes 393224 | tf_op jit(solution)/shard_map/ppermute | solution.py:39
  10.7 13.9 %collective-permute-start.6 = (s16[32,1152]{1,0:T(8,128)(2,1)S(1)}, s16[32,1152]{1,0:T(8,128)(2,1)S(1)}, u32[]{:S(2)}, u32[]{:S(2)}) collective-permute-start(s16[32,1152]{1,0:T(8,128)(2,1)S(1)} %get-tuple-element.49), channel_id=1, source_target_pairs={{12,13},{13,14},{14,15},{15,12},{28,29},{29,30},{30,31},{31,28}} | collective-permute-start | bytes 221192 | tf_op jit(solution)/shard_map/ppermute | solution.py:39
  16.4 9.4 %collective-permute-start.5 = (f32[32,1024]{1,0:T(8,128)S(1)}, f32[32,1024]{1,0:T(8,128)S(1)}, u32[]{:S(2)}, u32[]{:S(2)}) collective-permute-start(f32[32,1024]{1,0:T(8,128)S(1)} %get-tuple-element.112), channel_id=1, source_target_pairs={{0,1},{1,2},{2,3},{3,0},{4,5},{5,6},{6,7},{7,4},{8,9},{9,10},{10,1... | collective-permute-start | bytes 393224 | tf_op jit(solution)/shard_map/ppermute | solution.py:39
  19.0 10.9 %collective-permute-start.4 = (f32[32,1024]{1,0:T(8,128)S(1)}, f32[32,1024]{1,0:T(8,128)S(1)}, u32[]{:S(2)}, u32[]{:S(2)}) collective-permute-start(f32[32,1024]{1,0:T(8,128)S(1)} %get-tuple-element.113), channel_id=1, source_target_pairs={{0,2},{1,3},{2,0},{3,1},{4,6},{5,7},{6,4},{7,5},{8,10},{9,11},{10,... | collective-permute-start | bytes 393224 | tf_op jit(solution)/shard_map/ppermute | solution.py:39
  20.4 9.5 %collective-permute-start.3 = (f32[32,1024]{1,0:T(8,128)S(1)}, f32[32,1024]{1,0:T(8,128)S(1)}, u32[]{:S(2)}, u32[]{:S(2)}) collective-permute-start(f32[32,1024]{1,0:T(8,128)S(1)} %get-tuple-element.114), channel_id=1, source_target_pairs={{0,3},{1,0},{2,1},{3,2},{4,7},{5,4},{6,5},{7,6},{8,11},{9,8},{10,9... | collective-permute-start | bytes 393224 | tf_op jit(solution)/shard_map/ppermute | solution.py:39
  31.9 24.0 %collective-permute-start.9 = (s16[96,1152]{1,0:T(8,128)(2,1)S(1)}, s16[96,1152]{1,0:T(8,128)(2,1)S(1)}, u32[]{:S(2)}, u32[]{:S(2)}) collective-permute-start(s16[96,1152]{1,0:T(8,128)(2,1)S(1)} %get-tuple-element.54), channel_id=1, source_target_pairs={{0,1},{1,2},{2,3},{3,0},{4,5},{5,6},{6,7},{7,4},{8,9},{9,10},{10,1... | collective-permute-start | bytes 663560 | tf_op jit(solution)/shard_map/ppermute | solution.py:39
  36.5 9.1 %collective-permute-start.14 = (s16[32,1152]{1,0:T(8,128)(2,1)S(1)}, s16[32,1152]{1,0:T(8,128)(2,1)S(1)}, u32[]{:S(2)}, u32[]{:S(2)}) collective-permute-start(s16[32,1152]{1,0:T(8,128)(2,1)S(1)} %get-tuple-element.52.refs_2_.refs_0_.refs_8_), channel_id=1, source_target_pairs={{0,3},{1,0},{2,1},{3,2},{4,7},{5,4},{6,5},{7,6},{8,11},{9,8},{10,9... | collective-permute-start | bytes 221192 | tf_op jit(solution)/shard_map/ppermute | solution.py:39
  39.3 11.8 %collective-permute-start.13 = (s16[32,1152]{1,0:T(8,128)(2,1)S(1)}, s16[32,1152]{1,0:T(8,128)(2,1)S(1)}, u32[]{:S(2)}, u32[]{:S(2)}) collective-permute-start(s16[32,1152]{1,0:T(8,128)(2,1)S(1)} %get-tuple-element.52.refs_2_.refs_0_.refs_8_), channel_id=1, source_target_pairs={{0,2},{1,3},{2,0},{3,1},{4,6},{5,7},{6,4},{7,5},{8,10},{9,11},{10,... | collective-permute-start | bytes 221192 | tf_op jit(solution)/shard_map/ppermute | solution.py:39
  39.9 11.3 %collective-permute-start.12 = (s16[32,1152]{1,0:T(8,128)(2,1)S(1)}, s16[32,1152]{1,0:T(8,128)(2,1)S(1)}, u32[]{:S(2)}, u32[]{:S(2)}) collective-permute-start(s16[32,1152]{1,0:T(8,128)(2,1)S(1)} %get-tuple-element.52.refs_2_.refs_0_.refs_8_), channel_id=1, source_target_pairs={{0,1},{1,2},{2,3},{3,0},{4,5},{5,6},{6,7},{7,4},{8,9},{9,10},{10,1... | collective-permute-start | bytes 221192 | tf_op jit(solution)/shard_map/ppermute | solution.py:39
  51.2 16.3 %collective-permute-start.17 = (s16[128,1152]{1,0:T(8,128)(2,1)S(1)}, s16[128,1152]{1,0:T(8,128)(2,1)}, u32[]{:S(2)}, u32[]{:S(2)}) collective-permute-start(s16[128,1152]{1,0:T(8,128)(2,1)S(1)} %shard_map.191), channel_id=1, source_target_pairs={{0,12},{1,13},{2,14},{3,15},{16,28},{17,29},{18,30},{19,31}} | collective-permute-start | bytes 884744 | tf_op jit(solution)/shard_map/ppermute | solution.py:26
  52.5 15.8 %collective-permute-start.16 = (s16[128,1152]{1,0:T(8,128)(2,1)S(1)}, s16[128,1152]{1,0:T(8,128)(2,1)}, u32[]{:S(2)}, u32[]{:S(2)}) collective-permute-start(s16[128,1152]{1,0:T(8,128)(2,1)S(1)} %shard_map.191), channel_id=1, source_target_pairs={{0,8},{4,12},{1,9},{5,13},{2,10},{6,14},{3,11},{7,15},{16,24},{20,... | collective-permute-start | bytes 884744 | tf_op jit(solution)/shard_map/ppermute | solution.py:26
  53.8 15.2 %collective-permute-start.15 = (s16[128,1152]{1,0:T(8,128)(2,1)S(1)}, s16[128,1152]{1,0:T(8,128)(2,1)}, u32[]{:S(2)}, u32[]{:S(2)}) collective-permute-start(s16[128,1152]{1,0:T(8,128)(2,1)S(1)} %shard_map.191), channel_id=1, source_target_pairs={{0,4},{4,8},{8,12},{1,5},{5,9},{9,13},{2,6},{6,10},{10,14},{3,7},{... | collective-permute-start | bytes 884744 | tf_op jit(solution)/shard_map/ppermute | solution.py:26
  55.7 10.7 %collective-permute-start.10 = (s16[96,1152]{1,0:T(8,128)(2,1)S(1)}, s16[96,1152]{1,0:T(8,128)(2,1)}, u32[]{:S(2)}, u32[]{:S(2)}) collective-permute-start(s16[96,1152]{1,0:T(8,128)(2,1)S(1)} %get-tuple-element.55), channel_id=1, source_target_pairs={{0,2},{1,3},{2,0},{3,1},{4,6},{5,7},{6,4},{7,5},{8,10},{9,11},{10,... | collective-permute-start | bytes 663560 | tf_op jit(solution)/shard_map/ppermute | solution.py:39
  55.8 11.6 %collective-permute-start.11 = (s16[96,1152]{1,0:T(8,128)(2,1)S(1)}, s16[96,1152]{1,0:T(8,128)(2,1)}, u32[]{:S(2)}, u32[]{:S(2)}) collective-permute-start(s16[96,1152]{1,0:T(8,128)(2,1)S(1)} %get-tuple-element.56), channel_id=1, source_target_pairs={{0,3},{1,0},{2,1},{3,2},{4,7},{5,4},{6,5},{7,6},{8,11},{9,8},{10,9... | collective-permute-start | bytes 663560 | tf_op jit(solution)/shard_map/ppermute | solution.py:39
  82.7 24.4 %collective-permute-start.18 = (s16[128,1152]{1,0:T(8,128)(2,1)}, s16[128,1152]{1,0:T(8,128)(2,1)}, u32[]{:S(2)}, u32[]{:S(2)}) collective-permute-start(s16[128,1152]{1,0:T(8,128)(2,1)} %get-tuple-element.59), channel_id=1, source_target_pairs={{4,0},{8,4},{12,8},{5,1},{9,5},{13,9},{6,2},{10,6},{14,10},{7,3},{... | collective-permute-start | bytes 884744 | tf_op jit(solution)/shard_map/ppermute | solution.py:26
  84.8 23.4 %collective-permute-start.19 = (s16[128,1152]{1,0:T(8,128)(2,1)}, s16[128,1152]{1,0:T(8,128)(2,1)}, u32[]{:S(2)}, u32[]{:S(2)}) collective-permute-start(s16[128,1152]{1,0:T(8,128)(2,1)} %get-tuple-element.60), channel_id=1, source_target_pairs={{8,0},{12,4},{9,1},{13,5},{10,2},{14,6},{11,3},{15,7},{24,16},{28,... | collective-permute-start | bytes 884744 | tf_op jit(solution)/shard_map/ppermute | solution.py:26
  88.8 19.4 %collective-permute-start.20 = (s16[128,1152]{1,0:T(8,128)(2,1)}, s16[128,1152]{1,0:T(8,128)(2,1)}, u32[]{:S(2)}, u32[]{:S(2)}) collective-permute-start(s16[128,1152]{1,0:T(8,128)(2,1)} %get-tuple-element.61), channel_id=1, source_target_pairs={{12,0},{13,1},{14,2},{15,3},{28,16},{29,17},{30,18},{31,19}} | collective-permute-start | bytes 884744 | tf_op jit(solution)/shard_map/ppermute | solution.py:26
  100.5 14.5 %collective-permute-start.24 = (s16[96,1152]{1,0:T(8,128)(2,1)}, s16[96,1152]{1,0:T(8,128)(2,1)S(1)}, u32[]{:S(2)}, u32[]{:S(2)}) collective-permute-start(s16[96,1152]{1,0:T(8,128)(2,1)} %get-tuple-element.72), channel_id=1, source_target_pairs={{0,3},{1,0},{2,1},{3,2},{4,7},{5,4},{6,5},{7,6},{8,11},{9,8},{10,9... | collective-permute-start | bytes 663560 | tf_op jit(solution)/shard_map/ppermute | solution.py:39
  105.4 23.9 %collective-permute-start.25 = (s16[96,1152]{1,0:T(8,128)(2,1)}, s16[96,1152]{1,0:T(8,128)(2,1)S(1)}, u32[]{:S(2)}, u32[]{:S(2)}) collective-permute-start(s16[96,1152]{1,0:T(8,128)(2,1)} %get-tuple-element.73), channel_id=1, source_target_pairs={{0,2},{1,3},{2,0},{3,1},{4,6},{5,7},{6,4},{7,5},{8,10},{9,11},{10,... | collective-permute-start | bytes 663560 | tf_op jit(solution)/shard_map/ppermute | solution.py:39
  107.1 22.8 %collective-permute-start.26 = (s16[96,1152]{1,0:T(8,128)(2,1)}, s16[96,1152]{1,0:T(8,128)(2,1)S(1)}, u32[]{:S(2)}, u32[]{:S(2)}) collective-permute-start(s16[96,1152]{1,0:T(8,128)(2,1)} %get-tuple-element.74), channel_id=1, source_target_pairs={{0,1},{1,2},{2,3},{3,0},{4,5},{5,6},{6,7},{7,4},{8,9},{9,10},{10,1... | collective-permute-start | bytes 663560 | tf_op jit(solution)/shard_map/ppermute | solution.py:39
  110.6 20.0 %collective-permute-start.21 = (s16[32,1152]{1,0:T(8,128)(2,1)S(1)}, s16[32,1152]{1,0:T(8,128)(2,1)S(1)}, u32[]{:S(2)}, u32[]{:S(2)}) collective-permute-start(s16[32,1152]{1,0:T(8,128)(2,1)S(1)} %get-tuple-element.68), channel_id=1, source_target_pairs={{0,3},{1,0},{2,1},{3,2},{4,7},{5,4},{6,5},{7,6},{8,11},{9,8},{10,9... | collective-permute-start | bytes 221192 | tf_op jit(solution)/shard_map/ppermute | solution.py:39
  114.3 18.1 %collective-permute-start.22 = (s16[32,1152]{1,0:T(8,128)(2,1)S(1)}, s16[32,1152]{1,0:T(8,128)(2,1)S(1)}, u32[]{:S(2)}, u32[]{:S(2)}) collective-permute-start(s16[32,1152]{1,0:T(8,128)(2,1)S(1)} %get-tuple-element.69), channel_id=1, source_target_pairs={{0,2},{1,3},{2,0},{3,1},{4,6},{5,7},{6,4},{7,5},{8,10},{9,11},{10,... | collective-permute-start | bytes 221192 | tf_op jit(solution)/shard_map/ppermute | solution.py:39
  115.0 17.4 %collective-permute-start.23 = (s16[32,1152]{1,0:T(8,128)(2,1)S(1)}, s16[32,1152]{1,0:T(8,128)(2,1)S(1)}, u32[]{:S(2)}, u32[]{:S(2)}) collective-permute-start(s16[32,1152]{1,0:T(8,128)(2,1)S(1)} %get-tuple-element.70), channel_id=1, source_target_pairs={{0,1},{1,2},{2,3},{3,0},{4,5},{5,6},{6,7},{7,4},{8,9},{9,10},{10,1... | collective-permute-start | bytes 221192 | tf_op jit(solution)/shard_map/ppermute | solution.py:39
  129.3 19.3 %collective-permute-start.33 = (s16[32,1152]{1,0:T(8,128)(2,1)}, s16[32,1152]{1,0:T(8,128)(2,1)S(1)}, u32[]{:S(2)}, u32[]{:S(2)}) collective-permute-start(s16[32,1152]{1,0:T(8,128)(2,1)} %get-tuple-element.83), channel_id=1, source_target_pairs={{12,15},{13,12},{14,13},{15,14},{28,31},{29,28},{30,29},{31,30}} | collective-permute-start | bytes 221192 | tf_op jit(solution)/shard_map/ppermute | solution.py:39
  129.9 21.1 %collective-permute-start.34 = (s16[32,1152]{1,0:T(8,128)(2,1)}, s16[32,1152]{1,0:T(8,128)(2,1)S(1)}, u32[]{:S(2)}, u32[]{:S(2)}) collective-permute-start(s16[32,1152]{1,0:T(8,128)(2,1)} %get-tuple-element.84), channel_id=1, source_target_pairs={{12,14},{13,15},{14,12},{15,13},{28,30},{29,31},{30,28},{31,29}} | collective-permute-start | bytes 221192 | tf_op jit(solution)/shard_map/ppermute | solution.py:39
  134.7 9.7 %collective-permute-start.28 = (s16[32,1152]{1,0:T(8,128)(2,1)S(1)}, s16[32,1152]{1,0:T(8,128)(2,1)S(1)}, u32[]{:S(2)}, u32[]{:S(2)}) collective-permute-start(s16[32,1152]{1,0:T(8,128)(2,1)S(1)} %get-tuple-element.75.refs_0_), channel_id=1, source_target_pairs={{0,2},{1,3},{2,0},{3,1},{4,6},{5,7},{6,4},{7,5},{8,10},{9,11},{10,... | collective-permute-start | bytes 221192 | tf_op jit(solution)/shard_map/ppermute | solution.py:39
  139.3 11.8 %collective-permute-start.35 = (s16[32,1152]{1,0:T(8,128)(2,1)}, s16[32,1152]{1,0:T(8,128)(2,1)S(1)}, u32[]{:S(2)}, u32[]{:S(2)}) collective-permute-start(s16[32,1152]{1,0:T(8,128)(2,1)} %get-tuple-element.85), channel_id=1, source_target_pairs={{12,13},{13,14},{14,15},{15,12},{28,29},{29,30},{30,31},{31,28}} | collective-permute-start | bytes 221192 | tf_op jit(solution)/shard_map/ppermute | solution.py:39
  147.7 11.0 %collective-permute-start.30 = (s16[32,1152]{1,0:T(8,128)(2,1)S(1)}, s16[32,1152]{1,0:T(8,128)(2,1)S(1)}, u32[]{:S(2)}, u32[]{:S(2)}) collective-permute-start(s16[32,1152]{1,0:T(8,128)(2,1)S(1)} %get-tuple-element.77), channel_id=1, source_target_pairs={{0,3},{1,0},{2,1},{3,2},{4,7},{5,4},{6,5},{7,6},{8,11},{9,8},{10,9... | collective-permute-start | bytes 221192 | tf_op jit(solution)/shard_map/ppermute | solution.py:39
  148.2 10.6 %collective-permute-start.31 = (s16[32,1152]{1,0:T(8,128)(2,1)S(1)}, s16[32,1152]{1,0:T(8,128)(2,1)S(1)}, u32[]{:S(2)}, u32[]{:S(2)}) collective-permute-start(s16[32,1152]{1,0:T(8,128)(2,1)S(1)} %get-tuple-element.78), channel_id=1, source_target_pairs={{0,2},{1,3},{2,0},{3,1},{4,6},{5,7},{6,4},{7,5},{8,10},{9,11},{10,... | collective-permute-start | bytes 221192 | tf_op jit(solution)/shard_map/ppermute | solution.py:39
  148.5 10.2 %collective-permute-start.32 = (s16[32,1152]{1,0:T(8,128)(2,1)S(1)}, s16[32,1152]{1,0:T(8,128)(2,1)S(1)}, u32[]{:S(2)}, u32[]{:S(2)}) collective-permute-start(s16[32,1152]{1,0:T(8,128)(2,1)S(1)} %get-tuple-element.79), channel_id=1, source_target_pairs={{0,1},{1,2},{2,3},{3,0},{4,5},{5,6},{6,7},{7,4},{8,9},{9,10},{10,1... | collective-permute-start | bytes 221192 | tf_op jit(solution)/shard_map/ppermute | solution.py:39
  (33 other events, 461.7 us)

commit v3 on v2

v3 whole, which is shorter than its diff:
```python
import functools

import jax
import jax.numpy as jnp
from jax import lax
from jax.experimental import pallas as pl
from jax.experimental.pallas import tpu as pltpu
from jax.sharding import PartitionSpec as P

beta_one = 0.9
beta_two = 0.999
learn_rate = 0.001
adam_eps = 1e-08
step_count = 100.0
highest = lax.Precision.HIGHEST
lanes = 128
log_two = 0.6931471805599453
levels = 32767.0
vmem_bytes = 60 * 1024 * 1024
held_types = (jnp.float32, jnp.bfloat16, jnp.int16)


def shifted(value, axis, steps):
    count = lax.axis_size(axis)
    initial, last = (max(0, -steps), min(count, count - steps))
    return lax.ppermute(value, axis, [(source, source + steps) for source in range(initial, last)])


def rotated(value, steps, first_layer=0):
    count = lax.axis_size("feat")
    steps = steps % count
    if steps == 0:
        return value
    pairs = [
        (layer * count + s, layer * count + (s + steps) % count)
        for layer in range(first_layer, lax.axis_size("layer"))
        for s in range(count)
    ]
    return lax.ppermute(value, ("layer", "feat"), pairs)


def adam_update(weight, moments, grad):
    first = beta_one * moments[0] + (1.0 - beta_one) * grad
    second = beta_two * moments[1] + (1.0 - beta_two) * grad * grad
    scaled_first = first / (1.0 - beta_one**step_count)
    scaled_second = second / (1.0 - beta_two**step_count)
    updated = weight - learn_rate * scaled_first / (jnp.sqrt(scaled_second) + adam_eps)
    return (updated, jnp.stack([first, second]))


def slab_of(value, steps, width):
    count = lax.axis_size("feat")
    place = lax.rem(lax.axis_index("feat") + steps, count) * width
    return lax.dynamic_slice_in_dim(value, place, width, axis=value.ndim - 1)


exponent_bits = 12
exponent_offset = 1024


def lane_index(rows):
    return lax.broadcasted_iota(jnp.int32, (rows, lanes), 1)


def code_into(out_ref, rows, value):
    count, width = value.shape
    top = jnp.max(jnp.abs(value), axis=1, keepdims=True)
    exponent = jnp.ceil(jnp.log(jnp.maximum(top, 1e-30)) * (8.0 / log_two))
    scale = levels * jnp.exp(exponent * (-log_two / 8.0))
    whole = jnp.clip(jnp.round(value * scale), -levels, levels).astype(jnp.int32)
    lane = lane_index(count)
    shown = jnp.broadcast_to(exponent.astype(jnp.int32) + exponent_offset, (count, lanes))
    bits = lax.shift_right_logical(shown, jnp.minimum(lane, exponent_bits)) & 1
    first = whole[:, 0:lanes]
    first = jnp.where(lane < exponent_bits, (first & -2) | bits, first)
    out_ref[rows, 0:lanes] = first.astype(jnp.int16)
    if width > lanes:
        out_ref[rows, lanes:width] = whole[:, lanes:width].astype(jnp.int16)


def decoded(ref, rows):
    whole = ref[rows, :].astype(jnp.int32)
    count = whole.shape[0]
    lane = lane_index(count)
    bits = lax.shift_left(whole[:, 0:lanes] & 1, jnp.minimum(lane, exponent_bits))
    bits = jnp.where(lane < exponent_bits, bits, 0).astype(jnp.float32)
    exponent = jnp.sum(bits, axis=1, keepdims=True) - exponent_offset
    step = jnp.exp(jnp.maximum(exponent, -880.0) * (log_two / 8.0)) * (1.0 / levels)
    return whole.astype(jnp.float32) * step


def split(value):
    upper = value.astype(jnp.bfloat16)
    return upper, (value - upper.astype(jnp.float32)).astype(jnp.bfloat16)


def product(left, right, dims):
    dot = functools.partial(
        lax.dot_general, dimension_numbers=(dims, ((), ())), preferred_element_type=jnp.float32
    )
    return dot(left[0], right[0]) + (dot(left[0], right[1]) + dot(left[1], right[0]))


def blocks_of(size, block):
    block = min(size, block)
    return [slice(start, start + block) for start in range(0, size, block)]


def held_bytes(array):
    size = array.dtype.itemsize
    if len(array.shape) == 1:
        return 4096
    rows, columns = array.shape[-2:]
    tile = 32 // size
    rows, columns = -(-rows // tile) * tile, -(-columns // lanes) * lanes
    for extent in array.shape[:-2]:
        rows = rows * extent
    return rows * columns * size


def call(kernel, out_shape, args, flops=0, scratch=(), after=(), far=(), far_out=(), alone=True):
    size = sum(a.size * a.dtype.itemsize for a in [*far, *args])
    size += sum(o.size * o.dtype.itemsize for o in [*far_out, *out_shape])
    distant, taken, skipped = len(far), len(args), len(after)
    need = sum(held_bytes(a) for a in [*args, *out_shape]) + 4 * 1024 * 1024
    need += sum(held_bytes(a) for a in scratch if a.dtype in held_types)

    def body(*refs):
        kernel(*refs[: distant + taken], *refs[distant + taken + skipped :])

    spaces = [pltpu.HBM] * distant
    spaces += [pltpu.SMEM if a.shape == (1,) else pltpu.VMEM for a in args]
    spaces += [pl.ANY] * skipped
    out_spaces = [pltpu.HBM] * len(far_out) + [pltpu.VMEM] * len(out_shape)
    return pl.pallas_call(
        body,
        out_shape=(*far_out, *out_shape),
        in_specs=[pl.BlockSpec(memory_space=space) for space in spaces],
        out_specs=tuple(pl.BlockSpec(memory_space=space) for space in out_spaces),
        scratch_shapes=list(scratch),
        cost_estimate=pl.CostEstimate(flops=flops, bytes_accessed=size, transcendentals=0),
        compiler_params=pltpu.CompilerParams(vmem_limit_bytes=max(need, vmem_bytes if far and alone else 0)),
    )(*far, *args, *after)


def buffer_like(array):
    return pltpu.VMEM(array.shape, array.dtype)


class Fetched:
    def __init__(self, sources, buffers, semaphores):
        self.copies = [
            pltpu.make_async_copy(source, held, semaphores.at[i])
            for i, (source, held) in enumerate(zip(sources, buffers, strict=True))
        ]
        self.buffers = buffers
        for copy in self.copies:
            copy.start()

    def __getitem__(self, i):
        self.copies[i].wait()
        return self.buffers[i]


def shape(rows, columns, dtype=jnp.float32):
    return jax.ShapeDtypeStruct((rows, columns), dtype)


def coded_shape(rows, columns):
    return jax.ShapeDtypeStruct((rows, columns), jnp.int16)


def pack_kernel(count, first, last, me_ref, in_ref, *outs):
    reach, feats, total = in_ref.shape
    width = total // count
    for j in range(count):
        place = pl.multiple_of(lax.rem(me_ref[0] + j, count) * width, lanes)
        for k in range(first, last):
            rows = slice((k - first) * feats, (k - first + 1) * feats)
            code_into(outs[j], rows, in_ref[k, :, pl.ds(place, width)])


def packed(me, weights, first, last, after=()):
    count = lax.axis_size("feat")
    reach, feats, total = weights.shape
    out = coded_shape((last - first) * feats, total // count)
    kernel = functools.partial(pack_kernel, count, first, last)
    return call(kernel, [out] * count, [me, weights], after=after)


def adam_kernel(count, me_ref, *refs):
    grads, (weight_ref, moments_ref), (new_ref, new_moments_ref) = refs[:count], refs[count : count + 2], refs[-2:]
    width = weight_ref.shape[2] // count
    for j in range(count):
        place = pl.multiple_of(lax.rem(me_ref[0] + j, count) * width, lanes)
        cols = pl.ds(place, width)
        grad = decoded(grads[j], slice(None))
        first = beta_one * moments_ref[0, 0, :, cols] + (1.0 - beta_one) * grad
        second = beta_two * moments_ref[1, 0, :, cols] + (1.0 - beta_two) * grad * grad
        new_moments_ref[0, 0, :, cols] = first
        new_moments_ref[1, 0, :, cols] = second
        scaled_first = first * (learn_rate / (1.0 - beta_one**step_count))
        scaled_second = second * (1.0 / (1.0 - beta_two**step_count))
        new_ref[0, :, cols] = weight_ref[0, :, cols] - scaled_first / (
            jnp.sqrt(scaled_second) + adam_eps
        )


def adam_call(me, start, stop, grads, weight, moments, filled=(), after=()):
    count = lax.axis_size("feat")
    feats, total = weight.shape[1:]
    grad_spec = pl.BlockSpec((feats, total // count), lambda k: (k, 0))
    weight_spec = pl.BlockSpec((1, feats, total), lambda k: (start + k, 0, 0))
    moments_spec = pl.BlockSpec((2, 1, feats, total), lambda k: (0, start + k, 0, 0))
    place = 1 + count + 2
    return pl.pallas_call(
        functools.partial(adam_kernel, count),
        grid=(stop - start,),
        out_shape=(
            jax.ShapeDtypeStruct(weight.shape, weight.dtype),
            jax.ShapeDtypeStruct(moments.shape, moments.dtype),
        ),
        in_specs=[pl.BlockSpec(memory_space=pltpu.SMEM)]
        + [grad_spec] * count
        + [weight_spec, moments_spec]
        + [pl.BlockSpec(memory_space=pl.ANY)] * (len(filled) + len(after)),
        out_specs=(weight_spec, moments_spec),
        input_output_aliases={place + i: i for i in range(len(filled))},
        cost_estimate=pl.CostEstimate(
            flops=20 * (stop - start) * feats * total,
            bytes_accessed=26 * (stop - start) * feats * total,
            transcendentals=(stop - start) * feats * total,
        ),
        compiler_params=pltpu.CompilerParams(vmem_limit_bytes=24 * 1024 * 1024),
    )(me, *grads, weight, moments, *filled, *after)


def gather_kernel(*refs):
    *parts, out_ref = refs
    feats = parts[0].shape[0]
    for j, part in enumerate(parts):
        out_ref[j * feats : (j + 1) * feats, :] = part[...]


def codes_kernel(count, *refs):
    parts, bias_ref, mask_ref, codes_ref, coded_ref = refs[:count], *refs[count:]
    pre = bias_ref[...] + sum(part[...] for part in parts)
    codes = jnp.maximum(pre, 0.0) * mask_ref[...]
    codes_ref[...] = codes
    code_into(coded_ref, slice(None), codes)


def weights_kernel(count, feats, starts, *refs):
    parts = len(starts)
    fars, up_ref, low_ref, refs = refs[: parts * count], *refs[parts * count :][:2], refs[parts * count + 2 :]
    *buffers, full, arrive = refs
    held = Fetched(fars, buffers, arrive)
    for part, (start, stop) in enumerate(starts):
        for j in range(count):
            weights = held[part * count + j]
            for k in range(start, stop):
                row = (k * count + j) * feats
                rows = slice((k - start) * feats, (k - start + 1) * feats)
                full[row : row + feats, :] = decoded(weights, rows)
    for rows in blocks_of(full.shape[0], 32):
        up_ref[rows, :], low_ref[rows, :] = split(full[rows, :])


def main_kernel(count, reach, feats, starts, *refs):
    sources, results = count + reach - 1 + 4, reach + len(starts) * count
    fars, far_outs, sum_ref = refs[:sources], refs[sources : sources + results], refs[sources + results]
    refs = refs[sources + results + 1 :]
    buffers, outs, refs = refs[:sources], refs[sources : sources + results], refs[sources + results :]
    full, grad, res_up, res_low, src_up, src_low, arrive, leave = refs
    held = Fetched(fars, buffers, arrive)
    sends = [
        pltpu.make_async_copy(source, out, leave.at[i])
        for i, (source, out) in enumerate(zip(outs, far_outs, strict=True))
    ]
    block = count * feats
    for j in range(count):
        full[j * feats : (j + 1) * feats, :] = decoded(held[j], slice(None))
    for k in range(1, reach):
        moved = held[count + k - 1]
        for rows in blocks_of(block, 32):
            full[k * block + rows.start : k * block + rows.stop, :] = decoded(moved, rows)
    for rows in blocks_of(reach * block, 32):
        src_up[rows, :], src_low[rows, :] = split(full[rows, :])
    w_up, w_low = held[sources - 4], held[sources - 3]
    bias_ref, targets_ref = held[sources - 2], held[sources - 1]
    width, row_count = targets_ref.shape
    for cols in blocks_of(width, 256):
        recon = product(
            (w_up[:, cols], w_low[:, cols]), (src_up[...], src_low[...]), ((0,), (0,))
        )
        resid = recon + bias_ref[cols, :] - targets_ref[cols, :].astype(jnp.float32)
        sum_ref[cols, :] = jnp.sum(resid, axis=1, keepdims=True)
        res_up[cols, :], res_low[cols, :] = split(resid)
    for cols in blocks_of(row_count, 256):
        full[:, cols] = product(
            (w_up[...], w_low[...]), (res_up[:, cols], res_low[:, cols]), ((1,), (0,))
        )
    outs[0][...] = full[0:block, :]
    sends[0].start()
    for k in range(1, reach):
        for rows in blocks_of(block, 32):
            source = slice(k * block + rows.start, k * block + rows.stop)
            code_into(outs[k], rows, full[source, :])
        sends[k].start()
    for rows in blocks_of(width, 256):
        grad[:, rows] = product(
            (src_up[...], src_low[...]), (res_up[rows, :], res_low[rows, :]), ((1,), (1,))
        )
    for part, (start, stop) in enumerate(starts):
        for j in range(count):
            place = reach + part * count + j
            for k in range(start, stop):
                row = (k * count + j) * feats
                rows = slice((k - start) * feats, (k - start + 1) * feats)
                code_into(outs[place], rows, grad[row : row + feats, :])
            sends[place].start()
    for send in sends:
        send.wait()


def code_sum_kernel(count, feats, moved_count, *refs):
    own, moved, outs = refs[0], refs[1 : 1 + moved_count], refs[1 + moved_count :]
    for j in range(count):
        rows = slice(j * feats, (j + 1) * feats)
        total = own[rows, :]
        for ref in moved:
            total = total + decoded(ref, rows)
        if j == 0:
            outs[0][...] = total
        else:
            code_into(outs[j], slice(None), total)


def pre_grad_kernel(count, *refs):
    own, arrived, codes_ref, coded_ref, sum_ref = refs[0], refs[1:count], *refs[count:]
    total = own[...]
    for ref in arrived:
        total = total + decoded(ref, slice(None))
    pre_grad = jnp.where(codes_ref[...] > 0.0, total, 0.0)
    sum_ref[...] = jnp.sum(pre_grad, axis=1, keepdims=True)
    code_into(coded_ref, slice(None), pre_grad)


def grad_enc_kernel(count, feats, *refs):
    far, grads, refs = refs[0], refs[1 : 1 + count], refs[1 + count :]
    outs, (inputs_ref, full, grad, arrive) = refs[:count], refs[count:]
    held = Fetched([far], [inputs_ref], arrive)
    for j in range(count):
        full[j * feats : (j + 1) * feats, :] = decoded(grads[j], slice(None))
    upper, lower = split(full[...])
    inputs_ref = held[0]
    dot = functools.partial(
        lax.dot_general,
        dimension_numbers=(((1,), (1,)), ((), ())),
        preferred_element_type=jnp.float32,
    )
    for rows in blocks_of(inputs_ref.shape[0], 256):
        right = inputs_ref[rows, :]
        grad[:, rows] = dot(upper, right) + dot(lower, right)
    for j in range(count):
        code_into(outs[j], slice(None), grad[j * feats : (j + 1) * feats, :])


def local(
    inputs,
    targets,
    enc_weight,
    enc_bias,
    dec_weight,
    dec_bias,
    enc_moments,
    enc_bias_moments,
    dec_moments,
    dec_bias_moments,
    block_lists,
    block_counts,
    slot_block,
):
    inputs_local = inputs[0]
    targets_local = targets[0]
    enc_local = enc_weight[0]
    encb_local = enc_bias[0]
    dec_local = dec_weight[0]
    decb_local = dec_bias[0]
    reach = dec_local.shape[0]
    width, row_count = inputs_local.shape
    feats = enc_local.shape[0]
    count = lax.axis_size("feat")
    block = count * feats
    depth = reach * block
    tile_count = block_counts.shape[1]
    tile_rows = row_count // tile_count
    live = jnp.arange(block_lists.shape[2])[None, :] < block_counts[0][:, None]
    hits = (block_lists[0] == slot_block[0]) & live
    tile_active = jnp.any(hits, axis=1).astype(jnp.float32)
    row_mask = jnp.repeat(tile_active, tile_rows, axis=0)[None, :]

    enc_cols = jnp.concatenate(
        [rotated(slab_of(enc_local, j, width), j) for j in range(count)], axis=0
    )
    me = lax.axis_index("feat").astype(jnp.int32).reshape(1)
    half_way = max(1, reach // 2)
    starts = [(0, half_way)] + [(k, k + 1) for k in range(half_way, reach)]
    dec_cols = []
    for first, last in starts[1:]:
        sent = packed(me, dec_local, first, last)
        dec_cols += [rotated(sent[j], j, first) for j in range(count)]
    partial = jnp.dot(
        enc_cols,
        inputs_local.astype(jnp.float32),
        precision=highest,
        preferred_element_type=jnp.float32,
    ).reshape(count, feats, row_count)
    partials = [rotated(partial[j], -j) for j in range(count)]
    codes, coded_codes = call(
        functools.partial(codes_kernel, count),
        [shape(feats, row_count), coded_shape(feats, row_count)],
        [*partials, encb_local[:, None], row_mask],
        after=[a for i, a in enumerate(dec_cols) if i % count],
    )
    own = [rotated(coded_codes, j) for j in range(count)]
    gathered = call(gather_kernel, [coded_shape(block, row_count)], own)[0]
    moved = [shifted(gathered, "layer", k) for k in range(1, reach)]
    sent = packed(me, dec_local, *starts[0], after=[coded_codes])
    dec_cols = [rotated(sent[j], j) for j in range(count)] + dec_cols
    half = jnp.bfloat16
    weights = call(
        functools.partial(weights_kernel, count, feats, starts),
        [shape(depth, width, half)] * 2,
        [],
        scratch=[buffer_like(a) for a in dec_cols]
        + [pltpu.VMEM((depth, width), jnp.float32), pltpu.SemaphoreType.DMA((len(dec_cols),))],
        far=dec_cols,
    )
    backs = ((0, reach - 1), (reach - 1, reach)) if reach > 1 else ((0, reach),)
    far = [*own, *moved, *weights, decb_local[:, None], targets_local]
    far_out = [shape(block, row_count)] + [coded_shape(block, row_count)] * (reach - 1)
    for first, last in backs:
        far_out += [coded_shape((last - first) * feats, width)] * count
    outs = call(
        functools.partial(main_kernel, count, reach, feats, backs),
        [shape(width, 1)],
        [],
        flops=18 * depth * width * row_count,
        scratch=[buffer_like(a) for a in [*far, *far_out]]
        + [pltpu.VMEM((depth, row_count), jnp.float32), pltpu.VMEM((depth, width), jnp.float32)]
        + [pltpu.VMEM((width, row_count), half)] * 2
        + [pltpu.VMEM((depth, row_count), half)] * 2
        + [pltpu.SemaphoreType.DMA((len(far),)), pltpu.SemaphoreType.DMA((len(far_out),))],
        far=far,
        far_out=far_out,
    )
    part, parts, grad_parts, grad_dec_bias = outs[0], outs[1:reach], outs[reach:-1], outs[-1]
    returned = [shifted(parts[k - 1], "layer", -k) for k in range(1, reach)]
    grad_dec_cols = [
        [rotated(grad_parts[i * count + j], -j, first if i else 0) for j in range(count)]
        for i, (first, last) in enumerate(backs)
    ]
    sums = call(
        functools.partial(code_sum_kernel, count, feats, reach - 1),
        [shape(feats, row_count)] + [coded_shape(feats, row_count)] * (count - 1),
        [part, *returned],
    )
    arrived = [rotated(sums[j], -j) for j in range(count)]
    coded_grad, grad_enc_bias = call(
        functools.partial(pre_grad_kernel, count),
        [coded_shape(feats, row_count), shape(feats, 1)],
        [*arrived, codes],
        after=grad_dec_cols[0][1:],
    )
    pre_grads = [rotated(coded_grad, j) for j in range(count)]
    grad_enc_cols = call(
        functools.partial(grad_enc_kernel, count, feats),
        [coded_shape(feats, width)] * count,
        pre_grads,
        flops=4 * block * width * row_count,
        scratch=[
            buffer_like(inputs_local),
            pltpu.VMEM((block, row_count), jnp.float32),
            pltpu.VMEM((block, width), jnp.float32),
            pltpu.SemaphoreType.DMA((1,)),
        ],
        far=[inputs_local],
        alone=False,
    )
    dec_done = ()
    for (first, last), grads in zip(backs, grad_dec_cols):
        dec_done = adam_call(
            me, first, last, grads, dec_local, dec_moments[:, 0], dec_done, [grad_enc_cols[0]]
        )
    dec_new, dec_mom = dec_done
    enc_arrived = [rotated(grad_enc_cols[j], -j) for j in range(count)]
    enc_new, enc_mom = adam_call(me, 0, 1, enc_arrived, enc_local[None], enc_moments)
    encb_new, encb_mom = adam_update(encb_local, enc_bias_moments[:, 0], grad_enc_bias[:, 0])
    decb_new, decb_mom = adam_update(decb_local, dec_bias_moments[:, 0], grad_dec_bias[:, 0])
    return (
        enc_new,
        encb_new[None],
        dec_new[None],
        decb_new[None],
        enc_mom,
        encb_mom[:, None],
        dec_mom[:, None],
        decb_mom[:, None],
    )


def solution(mesh):
    cols = P(("group", "layer"), "feat", None)
    vec = P(("group", "layer"), "feat")
    dec = P(("group", "layer"), None, "feat", None)
    cols_mom = P(None, ("group", "layer"), "feat", None)
    vec_mom = P(None, ("group", "layer"), "feat")
    dec_mom = P(None, ("group", "layer"), None, "feat", None)
    return jax.shard_map(
        local,
        mesh=mesh,
        in_specs=(
            cols,
            cols,
            cols,
            vec,
            dec,
            vec,
            cols_mom,
            vec_mom,
            dec_mom,
            vec_mom,
            P(("group", "layer"), None, None),
            P(("group", "layer"), None),
            P(("group", "layer")),
        ),
        out_specs=(cols, vec, dec, vec, cols_mom, vec_mom, dec_mom, vec_mom),
        check_vma=False,
    )
```

time: 162 us -> 150 us (0.926)
  waiting for transfers between devices: 49.1 us -> 26.5 us
  starting transfers between devices: 57.6 us -> 71.5 us
  Pallas kernels: 34.5 us -> 29.8 us
    ppermute x30 -> x33, waiting for transfers between devices: 47.5 us -> 26.4 us  [rotated(): return lax.ppermute(value, ('layer', 'feat'), pairs)]
    ppermute x30 -> x33, starting transfers between devices: 45.6 us -> 57.1 us  [rotated(): return lax.ppermute(value, ('layer', 'feat'), pairs)]
    pallas_call x9 -> x10, Pallas kernels: 28.2 us -> 22.4 us  [call(): pl.pallas_call(body, out_shape=(*far_out, *out_shape), in_specs=[pl.Block...]
    ppermute x6, starting transfers between devices: 12 us -> 14.4 us  [shifted(): lax.ppermute(value, axis, [(source, source + steps) for source in range(i...]
    pallas_call x2 -> x3, Pallas kernels: 6.32 us -> 7.41 us  [adam_call(): pl.pallas_call(functools.partial(adam_kernel, count), grid=(stop - start,...]
    unnamed x59 -> x67, local copies, waits for them, and re-layouts: 10.8 us -> 9.89 us
  transfers between devices with their start and end apart: 36 -> 39, of which waited for: 13 -> 9; matrix products, arithmetic and copies ran while one was open for 4% -> 5% of each run, Pallas kernels for 12% -> 9%
where the time goes in v3:
time: 150 us; the launch traced here: 147 us
  starting transfers between devices  71.5 us (48%)
  Pallas kernels  29.8 us (20%)
  waiting for transfers between devices  26.5 us (18%)
  local copies, waits for them, and re-layouts  13 us (9%)
  other arithmetic  3.28 us (2%)
  between operations  1.87 us (1%)
    ppermute x33, starting transfers between devices, rotated(): return lax.ppermute(value, ('layer', 'feat'), pairs)  57.1 us
    ppermute x33, waiting for transfers between devices, rotated(): return lax.ppermute(value, ('layer', 'feat'), pairs)  26.4 us
    pallas_call x10, Pallas kernels, call(): pl.pallas_call(body, out_shape=(*far_out, *out_shape), in_specs=[pl.Block...  22.4 us
    ppermute x6, starting transfers between devices, shifted(): lax.ppermute(value, axis, [(source, source + steps) for source in range(i...  14.4 us
    unnamed x67, local copies, waits for them, and re-layouts  9.89 us
    pallas_call x3, Pallas kernels, adam_call(): pl.pallas_call(functools.partial(adam_kernel, count), grid=(stop - start,...  7.41 us
  transfers between devices with their start and end apart: 39, of which 9 were waited for; matrix products, arithmetic and copies ran while one was open for 5% of the time, Pallas kernels for 9%

profile of v3, /device:TPU:2, one launch (start us, length us, event | category | flops | bytes accessed | tf_op | source)
XLA Modules:
  0.0 147.0 jit_solution(7905843602882649300)
XLA Ops:
  1.8 1.6 %collective-permute-start = (f32[32,1024]{1,0:T(8,128)S(1)}, f32[32,1024]{1,0:T(8,128)S(1)}, u32[]{:S(2)}, u32[]{:S(2)}) collective-permute-start(f32[32,1024]{1,0:T(8,128)S(1)} %get-tuple-element.126), channel_id=1, source_target_pairs={{0,1},{1,2},{2,3},{3,0},{4,5},{5,6},{6,7},{7,4},{8,9},{9,10},{10,1... | collective-permute-start | bytes 393224 | tf_op jit(solution)/shard_map/ppermute | solution.py:39
  3.4 2.6 %collective-permute-start.1 = (f32[32,1024]{1,0:T(8,128)S(1)}, f32[32,1024]{1,0:T(8,128)S(1)}, u32[]{:S(2)}, u32[]{:S(2)}) collective-permute-start(f32[32,1024]{1,0:T(8,128)S(1)} %get-tuple-element.125), channel_id=1, source_target_pairs={{0,2},{1,3},{2,0},{3,1},{4,6},{5,7},{6,4},{7,5},{8,10},{9,11},{10,... | collective-permute-start | bytes 393224 | tf_op jit(solution)/shard_map/ppermute | solution.py:39
  7.4 1.6 %copy-done = f32[1,4,32,4096]{3,2,1,0:T(8,128)S(1)} copy-done((f32[1,4,32,4096]{3,2,1,0:T(8,128)S(1)}, f32[1,4,32,4096]{3,2,1,0:T(8,128)}, u32[]{:S(2)}) %copy-start) | copy-done | bytes 2097176
  11.9 5.2 %collective-permute-start.6 = (s16[32,1024]{1,0:T(8,128)(2,1)S(1)}, s16[32,1024]{1,0:T(8,128)(2,1)S(1)}, u32[]{:S(2)}, u32[]{:S(2)}) collective-permute-start(s16[32,1024]{1,0:T(8,128)(2,1)S(1)} %get-tuple-element.53), channel_id=1, source_target_pairs={{8,9},{9,10},{10,11},{11,8},{12,13},{13,14},{14,15},{15,12},{24,25... | collective-permute-start | bytes 196616 | tf_op jit(solution)/shard_map/ppermute | solution.py:39
  17.1 3.9 %collective-permute-start.7 = (s16[32,1024]{1,0:T(8,128)(2,1)S(1)}, s16[32,1024]{1,0:T(8,128)(2,1)S(1)}, u32[]{:S(2)}, u32[]{:S(2)}) collective-permute-start(s16[32,1024]{1,0:T(8,128)(2,1)S(1)} %get-tuple-element.54), channel_id=1, source_target_pairs={{8,10},{9,11},{10,8},{11,9},{12,14},{13,15},{14,12},{15,13},{24,26... | collective-permute-start | bytes 196616 | tf_op jit(solution)/shard_map/ppermute | solution.py:39
  22.8 2.9 %collective-permute-start.3 = (f32[32,1024]{1,0:T(8,128)}, f32[32,1024]{1,0:T(8,128)S(1)}, u32[]{:S(2)}, u32[]{:S(2)}) collective-permute-start(f32[32,1024]{1,0:T(8,128)} %get-tuple-element.122), channel_id=1, source_target_pairs={{0,3},{1,0},{2,1},{3,2},{4,7},{5,4},{6,5},{7,6},{8,11},{9,8},{10,9... | collective-permute-start | bytes 393224 | tf_op jit(solution)/shard_map/ppermute | solution.py:39
  27.5 5.7 %collective-permute-start.8 = (s16[32,1024]{1,0:T(8,128)(2,1)S(1)}, s16[32,1024]{1,0:T(8,128)(2,1)S(1)}, u32[]{:S(2)}, u32[]{:S(2)}) collective-permute-start(s16[32,1024]{1,0:T(8,128)(2,1)S(1)} %get-tuple-element.55), channel_id=1, source_target_pairs={{8,11},{9,8},{10,9},{11,10},{12,15},{13,12},{14,13},{15,14},{24,27... | collective-permute-start | bytes 196616 | tf_op jit(solution)/shard_map/ppermute | solution.py:39
  34.4 1.7 %collective-permute-done.8.refs_8_.refs_7_ = s16[32,1024]{1,0:T(8,128)(2,1)S(1)} collective-permute-done((s16[32,1024]{1,0:T(8,128)(2,1)S(1)}, s16[32,1024]{1,0:T(8,128)(2,1)S(1)}, u32[]{:S(2)}, u32[]{:S(2)}) %collective-permute-start.8) | collective-permute-done | bytes 65568 | tf_op jit(solution)/shard_map/ppermute | solution.py:39
  36.1 4.1 %collective-permute-done.4.refs_2_ = f32[32,1024]{1,0:T(8,128)S(1)} collective-permute-done((f32[32,1024]{1,0:T(8,128)S(1)}, f32[32,1024]{1,0:T(8,128)S(1)}, u32[]{:S(2)}, u32[]{:S(2)}) %collective-permute-start.4) | collective-permute-done | bytes 131104 | tf_op jit(solution)/shard_map/ppermute | solution.py:39
  42.4 2.7 %collective-permute-start.14 = (s16[32,1024]{1,0:T(8,128)(2,1)S(1)}, s16[32,1024]{1,0:T(8,128)(2,1)S(1)}, u32[]{:S(2)}, u32[]{:S(2)}) collective-permute-start(s16[32,1024]{1,0:T(8,128)(2,1)S(1)} %get-tuple-element.59.refs_0_.refs_2_), channel_id=1, source_target_pairs={{0,3},{1,0},{2,1},{3,2},{4,7},{5,4},{6,5},{7,6},{8,11},{9,8},{10,9... | collective-permute-start | bytes 196616 | tf_op jit(solution)/shard_map/ppermute | solution.py:39
  45.8 1.8 %collective-permute-done.12.refs_1_ = s16[32,1024]{1,0:T(8,128)(2,1)S(1)} collective-permute-done((s16[32,1024]{1,0:T(8,128)(2,1)S(1)}, s16[32,1024]{1,0:T(8,128)(2,1)S(1)}, u32[]{:S(2)}, u32[]{:S(2)}) %collective-permute-start.12) | collective-permute-done | bytes 65568 | tf_op jit(solution)/shard_map/ppermute | solution.py:39
  47.6 3.0 %collective-permute-done.13.refs_2_ = s16[32,1024]{1,0:T(8,128)(2,1)S(1)} collective-permute-done((s16[32,1024]{1,0:T(8,128)(2,1)S(1)}, s16[32,1024]{1,0:T(8,128)(2,1)S(1)}, u32[]{:S(2)}, u32[]{:S(2)}) %collective-permute-start.13) | collective-permute-done | bytes 65568 | tf_op jit(solution)/shard_map/ppermute | solution.py:39
  50.7 1.9 %collective-permute-start.15 = (s16[128,1024]{1,0:T(8,128)(2,1)S(1)}, s16[128,1024]{1,0:T(8,128)(2,1)}, u32[]{:S(2)}, u32[]{:S(2)}) collective-permute-start(s16[128,1024]{1,0:T(8,128)(2,1)S(1)} %shard_map.191), channel_id=1, source_target_pairs={{0,4},{4,8},{8,12},{1,5},{5,9},{9,13},{2,6},{6,10},{10,14},{3,7},{... | collective-permute-start | bytes 786440 | tf_op jit(solution)/shard_map/ppermute | solution.py:26
  55.3 1.7 %collective-permute-start.19 = (s16[64,1024]{1,0:T(8,128)(2,1)S(1)}, s16[64,1024]{1,0:T(8,128)(2,1)}, u32[]{:S(2)}, u32[]{:S(2)}) collective-permute-start(s16[64,1024]{1,0:T(8,128)(2,1)S(1)} %get-tuple-element.62), channel_id=1, source_target_pairs={{0,2},{1,3},{2,0},{3,1},{4,6},{5,7},{6,4},{7,5},{8,10},{9,11},{10,... | collective-permute-start | bytes 393224 | tf_op jit(solution)/shard_map/ppermute | solution.py:39
  56.9 3.3 %collective-permute-start.20 = (s16[64,1024]{1,0:T(8,128)(2,1)S(1)}, s16[64,1024]{1,0:T(8,128)(2,1)}, u32[]{:S(2)}, u32[]{:S(2)}) collective-permute-start(s16[64,1024]{1,0:T(8,128)(2,1)S(1)} %get-tuple-element.63), channel_id=1, source_target_pairs={{0,3},{1,0},{2,1},{3,2},{4,7},{5,4},{6,5},{7,6},{8,11},{9,8},{10,9... | collective-permute-start | bytes 393224 | tf_op jit(solution)/shard_map/ppermute | solution.py:39
  62.8 3.8 %shard_map.193 = (bf16[512,1024]{1,0:T(8,128)(2,1)}, bf16[512,1024]{1,0:T(8,128)(2,1)}) custom-call(s16[64,1024]{1,0:T(8,128)(2,1)} %copy-done.19, s16[64,1024]{1,0:T(8,128)(2,1)} %copy-done.26, s16[64,1024]{1,0:T(8,128)(2,1)} %collective-permute-done.19.refs_2_, s16[64,1024]{1,0:T(8,128)(2,1)} %collective-permute-done.20.refs_3_, ...), custom_call_target="tpu_custom_call" | custom-call | bytes 3145728 | tf_op jit(solution)/shard_map/pallas_call | solution.py:135
  66.7 15.0 %shard_map.194 = (f32[128,1024]{1,0:T(8,128)}, s16[128,1024]{1,0:T(8,128)(2,1)}, s16[128,1024]{1,0:T(8,128)(2,1)}, s16[128,1024]{1,0:T(8,128)(2,1)}, s16[96,1024...) custom-call(s16[32,1024]{1,0:T(8,128)(2,1)} %copy-done.15, ...), custom_call_target="tpu_custom_call" | custom-call | flops 9663676416 | bytes 7610368 | tf_op jit(solution)/shard_map/pallas_call | solution.py:135
  81.8 3.7 %collective-permute-start.21 = (s16[128,1024]{1,0:T(8,128)(2,1)}, s16[128,1024]{1,0:T(8,128)(2,1)S(1)}, u32[]{:S(2)}, u32[]{:S(2)}) collective-permute-start(s16[128,1024]{1,0:T(8,128)(2,1)} %get-tuple-element.69), channel_id=1, source_target_pairs={{4,0},{8,4},{12,8},{5,1},{9,5},{13,9},{6,2},{10,6},{14,10},{7,3},{... | collective-permute-start | bytes 786440 | tf_op jit(solution)/shard_map/ppermute | solution.py:26
  85.5 5.5 %collective-permute-start.22 = (s16[128,1024]{1,0:T(8,128)(2,1)}, s16[128,1024]{1,0:T(8,128)(2,1)S(1)}, u32[]{:S(2)}, u32[]{:S(2)}) collective-permute-start(s16[128,1024]{1,0:T(8,128)(2,1)} %get-tuple-element.70), channel_id=1, source_target_pairs={{8,0},{12,4},{9,1},{13,5},{10,2},{14,6},{11,3},{15,7},{24,16},{28,... | collective-permute-start | bytes 786440 | tf_op jit(solution)/shard_map/ppermute | solution.py:26
  91.7 3.8 %collective-permute-start.27 = (s16[96,1024]{1,0:T(8,128)(2,1)}, s16[96,1024]{1,0:T(8,128)(2,1)S(1)}, u32[]{:S(2)}, u32[]{:S(2)}) collective-permute-start(s16[96,1024]{1,0:T(8,128)(2,1)} %get-tuple-element.77), channel_id=1, source_target_pairs={{0,3},{1,0},{2,1},{3,2},{4,7},{5,4},{6,5},{7,6},{8,11},{9,8},{10,9... | collective-permute-start | bytes 589832 | tf_op jit(solution)/shard_map/ppermute | solution.py:39
  99.5 5.0 %collective-permute-start.24 = (s16[32,1024]{1,0:T(8,128)(2,1)S(1)}, s16[32,1024]{1,0:T(8,128)(2,1)S(1)}, u32[]{:S(2)}, u32[]{:S(2)}) collective-permute-start(s16[32,1024]{1,0:T(8,128)(2,1)S(1)} %get-tuple-element.73), channel_id=1, source_target_pairs={{0,3},{1,0},{2,1},{3,2},{4,7},{5,4},{6,5},{7,6},{8,11},{9,8},{10,9... | collective-permute-start | bytes 196616 | tf_op jit(solution)/shard_map/ppermute | solution.py:39
  105.8 10.4 %collective-permute-done.28.refs_6_.refs_2_ = s16[96,1024]{1,0:T(8,128)(2,1)S(1)} collective-permute-done((s16[96,1024]{1,0:T(8,128)(2,1)}, s16[96,1024]{1,0:T(8,128)(2,1)S(1)}, u32[]{:S(2)}, u32[]{:S(2)}) %collective-permute-start.28) | collective-permute-done | bytes 196640 | tf_op jit(solution)/shard_map/ppermute | solution.py:39
  120.7 2.0 %collective-permute-start.31 = (s16[32,1024]{1,0:T(8,128)(2,1)S(1)}, s16[32,1024]{1,0:T(8,128)(2,1)S(1)}, u32[]{:S(2)}, u32[]{:S(2)}) collective-permute-start(s16[32,1024]{1,0:T(8,128)(2,1)S(1)} %get-tuple-element.80.refs_1_), channel_id=1, source_target_pairs={{0,2},{1,3},{2,0},{3,1},{4,6},{5,7},{6,4},{7,5},{8,10},{9,11},{10,... | collective-permute-start | bytes 196616 | tf_op jit(solution)/shard_map/ppermute | solution.py:39
  122.7 2.8 %collective-permute-start.32 = (s16[32,1024]{1,0:T(8,128)(2,1)S(1)}, s16[32,1024]{1,0:T(8,128)(2,1)S(1)}, u32[]{:S(2)}, u32[]{:S(2)}) collective-permute-start(s16[32,1024]{1,0:T(8,128)(2,1)S(1)} %get-tuple-element.80.refs_1_), channel_id=1, source_target_pairs={{0,3},{1,0},{2,1},{3,2},{4,7},{5,4},{6,5},{7,6},{8,11},{9,8},{10,9... | collective-permute-start | bytes 196616 | tf_op jit(solution)/shard_map/ppermute | solution.py:39
  128.0 1.6 %collective-permute-done.31.refs_3_ = s16[32,1024]{1,0:T(8,128)(2,1)S(1)} collective-permute-done((s16[32,1024]{1,0:T(8,128)(2,1)S(1)}, s16[32,1024]{1,0:T(8,128)(2,1)S(1)}, u32[]{:S(2)}, u32[]{:S(2)}) %collective-permute-start.31) | collective-permute-done | bytes 65568 | tf_op jit(solution)/shard_map/ppermute | solution.py:39
  129.6 1.6 %copy-done.5 = bf16[1,1024,1024]{2,1,0:T(8,128)(2,1)S(1)} copy-done((bf16[1,1024,1024]{2,1,0:T(8,128)(2,1)S(1)}, bf16[1,1024,1024]{2,1,0:T(8,128)(2,1)}, u32[]{:S(2)}) %copy-start.5) | copy-done | bytes 2097176
  131.2 2.0 %shard_map.197 = (s16[32,1024]{1,0:T(8,128)(2,1)S(1)}, s16[32,1024]{1,0:T(8,128)(2,1)S(1)}, s16[32,1024]{1,0:T(8,128)(2,1)S(1)}, s16[32,1024]{1,0:T(8,128)(2,1)S(1)}) custom-call(bf16[1024,1024]{1,0:T(8,128)(2,1)S(1)} %bitcast.58, s16[32,1024]{1,0:T(8,128)(2,1)S(1)} %get-tuple-element.80.refs_1_, s16[32,1024]{1,0:T(8,128)(2,1)S(1)} %collective-permute-done.30.refs_2_, ...), custom_call_target="tpu_custom_call" | custom-call | flops 536870912 | bytes 2621440 | tf_op jit(solution)/shard_map/pallas_call | solution.py:135
  133.2 2.8 %collective-permute-start.33 = (s16[32,1024]{1,0:T(8,128)(2,1)S(1)}, s16[32,1024]{1,0:T(8,128)(2,1)S(1)}, u32[]{:S(2)}, u32[]{:S(2)}) collective-permute-start(s16[32,1024]{1,0:T(8,128)(2,1)S(1)} %get-tuple-element.82), channel_id=1, source_target_pairs={{0,3},{1,0},{2,1},{3,2},{4,7},{5,4},{6,5},{7,6},{8,11},{9,8},{10,9... | collective-permute-start | bytes 196616 | tf_op jit(solution)/shard_map/ppermute | solution.py:39
  137.3 2.2 %copy-done.2 = f32[2,1,4,32,4096]{4,3,2,1,0:T(8,128)S(1)} copy-done((f32[2,1,4,32,4096]{4,3,2,1,0:T(8,128)S(1)}, f32[2,1,4,32,4096]{4,3,2,1,0:T(8,128)}, u32[]{:S(2)}) %copy-start.2) | copy-done | bytes 4194328
  139.5 3.8 %shard_map.199 = (f32[4,32,4096]{2,1,0:T(8,128)}, f32[2,4,32,4096]{3,2,1,0:T(8,128)}) custom-call(s32[1]{0:T(128)} %bitcast.refs_0_.me_ref, s16[96,1024]{1,0:T(8,128)(2,1)S(1)} %copy-done.16, s16[96,1024]{1,0:T(8,128)(2,1)S(1)} %collective-permute-done.27.refs_5_.refs_1_, s16[96,1024]{1,0:T(8,128)(2,1)S(1)} %collective-permute-done.28.refs_6_.refs_2_, ...), custom_call_target="tpu_custom_call" | custom-call | flops 7864320 | bytes 10223616 | tf_op jit(solution)/shard_map/pallas_call | solution.py:216
  143.3 1.8 %shard_map.200 = (f32[4,32,4096]{2,1,0:T(8,128)}, f32[2,4,32,4096]{3,2,1,0:T(8,128)}) custom-call(s32[1]{0:T(128)} %bitcast.refs_0_.me_ref, s16[32,1024]{1,0:T(8,128)(2,1)S(1)} %copy-done.20, s16[32,1024]{1,0:T(8,128)(2,1)S(1)} %collective-permute-done.36.refs_1_, ...), custom_call_target="tpu_custom_call", output_to_operand_aliasing={{0}: (7, {}), {1}: (8, {})} | custom-call | flops 2621440 | bytes 3407872 | tf_op jit(solution)/shard_map/pallas_call | solution.py:216
  145.2 1.7 %shard_map.198 = (f32[1,32,4096]{2,1,0:T(8,128)}, f32[2,1,32,4096]{3,2,1,0:T(8,128)}) custom-call(s32[1]{0:T(128)} %bitcast.refs_0_.me_ref, s16[32,1024]{1,0:T(8,128)(2,1)S(1)} %get-tuple-element.81.refs_0_.refs_6_.refs_8_, s16[32,1024]{1,0:T(8,128)(2,1)S(1)} %collective-permute-done.33.refs_1_, s16[32,1024]{1,0:T(8,128)(2,1)S(1)} %collective-permute-done.34.refs_2_, ...), custom_call_target="tpu_custom_call" | custom-call | flops 2621440 | bytes 3407872 | tf_op jit(solution)/shard_map/pallas_call | solution.py:216
  (141 shorter events, 31.8 us)
Async XLA Ops:
  1.8 10.1 %collective-permute-start = (f32[32,1024]{1,0:T(8,128)S(1)}, f32[32,1024]{1,0:T(8,128)S(1)}, u32[]{:S(2)}, u32[]{:S(2)}) collective-permute-start(f32[32,1024]{1,0:T(8,128)S(1)} %get-tuple-element.126), channel_id=1, source_target_pairs={{0,1},{1,2},{2,3},{3,0},{4,5},{5,6},{6,7},{7,4},{8,9},{9,10},{10,1... | collective-permute-start | bytes 393224 | tf_op jit(solution)/shard_map/ppermute | solution.py:39
  3.4 13.7 %collective-permute-start.1 = (f32[32,1024]{1,0:T(8,128)S(1)}, f32[32,1024]{1,0:T(8,128)S(1)}, u32[]{:S(2)}, u32[]{:S(2)}) collective-permute-start(f32[32,1024]{1,0:T(8,128)S(1)} %get-tuple-element.125), channel_id=1, source_target_pairs={{0,2},{1,3},{2,0},{3,1},{4,6},{5,7},{6,4},{7,5},{8,10},{9,11},{10,... | collective-permute-start | bytes 393224 | tf_op jit(solution)/shard_map/ppermute | solution.py:39
  6.0 15.0 %collective-permute-start.2 = (f32[32,1024]{1,0:T(8,128)S(1)}, f32[32,1024]{1,0:T(8,128)S(1)}, u32[]{:S(2)}, u32[]{:S(2)}) collective-permute-start(f32[32,1024]{1,0:T(8,128)S(1)} %get-tuple-element.127), channel_id=1, source_target_pairs={{0,3},{1,0},{2,1},{3,2},{4,7},{5,4},{6,5},{7,6},{8,11},{9,8},{10,9... | collective-permute-start | bytes 393224 | tf_op jit(solution)/shard_map/ppermute | solution.py:39
  9.8 15.9 %collective-permute-start.10 = (s16[32,1024]{1,0:T(8,128)(2,1)S(1)}, s16[32,1024]{1,0:T(8,128)(2,1)S(1)}, u32[]{:S(2)}, u32[]{:S(2)}) collective-permute-start(s16[32,1024]{1,0:T(8,128)(2,1)S(1)} %get-tuple-element.57), channel_id=1, source_target_pairs={{12,14},{13,15},{14,12},{15,13},{28,30},{29,31},{30,28},{31,29}} | collective-permute-start | bytes 196616 | tf_op jit(solution)/shard_map/ppermute | solution.py:39
  10.4 16.4 %collective-permute-start.11 = (s16[32,1024]{1,0:T(8,128)(2,1)S(1)}, s16[32,1024]{1,0:T(8,128)(2,1)S(1)}, u32[]{:S(2)}, u32[]{:S(2)}) collective-permute-start(s16[32,1024]{1,0:T(8,128)(2,1)S(1)} %get-tuple-element.58), channel_id=1, source_target_pairs={{12,15},{13,12},{14,13},{15,14},{28,31},{29,28},{30,29},{31,30}} | collective-permute-start | bytes 196616 | tf_op jit(solution)/shard_map/ppermute | solution.py:39
  11.9 15.6 %collective-permute-start.6 = (s16[32,1024]{1,0:T(8,128)(2,1)S(1)}, s16[32,1024]{1,0:T(8,128)(2,1)S(1)}, u32[]{:S(2)}, u32[]{:S(2)}) collective-permute-start(s16[32,1024]{1,0:T(8,128)(2,1)S(1)} %get-tuple-element.53), channel_id=1, source_target_pairs={{8,9},{9,10},{10,11},{11,8},{12,13},{13,14},{14,15},{15,12},{24,25... | collective-permute-start | bytes 196616 | tf_op jit(solution)/shard_map/ppermute | solution.py:39
  17.1 16.1 %collective-permute-start.7 = (s16[32,1024]{1,0:T(8,128)(2,1)S(1)}, s16[32,1024]{1,0:T(8,128)(2,1)S(1)}, u32[]{:S(2)}, u32[]{:S(2)}) collective-permute-start(s16[32,1024]{1,0:T(8,128)(2,1)S(1)} %get-tuple-element.54), channel_id=1, source_target_pairs={{8,10},{9,11},{10,8},{11,9},{12,14},{13,15},{14,12},{15,13},{24,26... | collective-permute-start | bytes 196616 | tf_op jit(solution)/shard_map/ppermute | solution.py:39
  22.8 13.3 %collective-permute-start.3 = (f32[32,1024]{1,0:T(8,128)}, f32[32,1024]{1,0:T(8,128)S(1)}, u32[]{:S(2)}, u32[]{:S(2)}) collective-permute-start(f32[32,1024]{1,0:T(8,128)} %get-tuple-element.122), channel_id=1, source_target_pairs={{0,3},{1,0},{2,1},{3,2},{4,7},{5,4},{6,5},{7,6},{8,11},{9,8},{10,9... | collective-permute-start | bytes 393224 | tf_op jit(solution)/shard_map/ppermute | solution.py:39
  25.7 14.5 %collective-permute-start.4 = (f32[32,1024]{1,0:T(8,128)S(1)}, f32[32,1024]{1,0:T(8,128)S(1)}, u32[]{:S(2)}, u32[]{:S(2)}) collective-permute-start(f32[32,1024]{1,0:T(8,128)S(1)} %get-tuple-element.121), channel_id=1, source_target_pairs={{0,2},{1,3},{2,0},{3,1},{4,6},{5,7},{6,4},{7,5},{8,10},{9,11},{10,... | collective-permute-start | bytes 393224 | tf_op jit(solution)/shard_map/ppermute | solution.py:39
  26.9 13.4 %collective-permute-start.5 = (f32[32,1024]{1,0:T(8,128)S(1)}, f32[32,1024]{1,0:T(8,128)S(1)}, u32[]{:S(2)}, u32[]{:S(2)}) collective-permute-start(f32[32,1024]{1,0:T(8,128)S(1)} %get-tuple-element.120), channel_id=1, source_target_pairs={{0,1},{1,2},{2,3},{3,0},{4,5},{5,6},{6,7},{7,4},{8,9},{9,10},{10,1... | collective-permute-start | bytes 393224 | tf_op jit(solution)/shard_map/ppermute | solution.py:39
  27.5 8.6 %collective-permute-start.8 = (s16[32,1024]{1,0:T(8,128)(2,1)S(1)}, s16[32,1024]{1,0:T(8,128)(2,1)S(1)}, u32[]{:S(2)}, u32[]{:S(2)}) collective-permute-start(s16[32,1024]{1,0:T(8,128)(2,1)S(1)} %get-tuple-element.55), channel_id=1, source_target_pairs={{8,11},{9,8},{10,9},{11,10},{12,15},{13,12},{14,13},{15,14},{24,27... | collective-permute-start | bytes 196616 | tf_op jit(solution)/shard_map/ppermute | solution.py:39
  42.4 8.2 %collective-permute-start.13 = (s16[32,1024]{1,0:T(8,128)(2,1)S(1)}, s16[32,1024]{1,0:T(8,128)(2,1)S(1)}, u32[]{:S(2)}, u32[]{:S(2)}) collective-permute-start(s16[32,1024]{1,0:T(8,128)(2,1)S(1)} %get-tuple-element.59.refs_0_.refs_2_), channel_id=1, source_target_pairs={{0,2},{1,3},{2,0},{3,1},{4,6},{5,7},{6,4},{7,5},{8,10},{9,11},{10,... | collective-permute-start | bytes 196616 | tf_op jit(solution)/shard_map/ppermute | solution.py:39
  42.4 8.3 %collective-permute-start.14 = (s16[32,1024]{1,0:T(8,128)(2,1)S(1)}, s16[32,1024]{1,0:T(8,128)(2,1)S(1)}, u32[]{:S(2)}, u32[]{:S(2)}) collective-permute-start(s16[32,1024]{1,0:T(8,128)(2,1)S(1)} %get-tuple-element.59.refs_0_.refs_2_), channel_id=1, source_target_pairs={{0,3},{1,0},{2,1},{3,2},{4,7},{5,4},{6,5},{7,6},{8,11},{9,8},{10,9... | collective-permute-start | bytes 196616 | tf_op jit(solution)/shard_map/ppermute | solution.py:39
  45.4 11.5 %collective-permute-start.18 = (s16[64,1024]{1,0:T(8,128)(2,1)S(1)}, s16[64,1024]{1,0:T(8,128)(2,1)S(1)}, u32[]{:S(2)}, u32[]{:S(2)}) collective-permute-start(s16[64,1024]{1,0:T(8,128)(2,1)S(1)} %get-tuple-element.61), channel_id=1, source_target_pairs={{0,1},{1,2},{2,3},{3,0},{4,5},{5,6},{6,7},{7,4},{8,9},{9,10},{10,1... | collective-permute-start | bytes 393224 | tf_op jit(solution)/shard_map/ppermute | solution.py:39
  50.7 16.0 %collective-permute-start.15 = (s16[128,1024]{1,0:T(8,128)(2,1)S(1)}, s16[128,1024]{1,0:T(8,128)(2,1)}, u32[]{:S(2)}, u32[]{:S(2)}) collective-permute-start(s16[128,1024]{1,0:T(8,128)(2,1)S(1)} %shard_map.191), channel_id=1, source_target_pairs={{0,4},{4,8},{8,12},{1,5},{5,9},{9,13},{2,6},{6,10},{10,14},{3,7},{... | collective-permute-start | bytes 786440 | tf_op jit(solution)/shard_map/ppermute | solution.py:26
  52.6 14.1 %collective-permute-start.16 = (s16[128,1024]{1,0:T(8,128)(2,1)S(1)}, s16[128,1024]{1,0:T(8,128)(2,1)}, u32[]{:S(2)}, u32[]{:S(2)}) collective-permute-start(s16[128,1024]{1,0:T(8,128)(2,1)S(1)} %shard_map.191), channel_id=1, source_target_pairs={{0,8},{4,12},{1,9},{5,13},{2,10},{6,14},{3,11},{7,15},{16,24},{20,... | collective-permute-start | bytes 786440 | tf_op jit(solution)/shard_map/ppermute | solution.py:26
  53.9 12.8 %collective-permute-start.17 = (s16[128,1024]{1,0:T(8,128)(2,1)S(1)}, s16[128,1024]{1,0:T(8,128)(2,1)}, u32[]{:S(2)}, u32[]{:S(2)}) collective-permute-start(s16[128,1024]{1,0:T(8,128)(2,1)S(1)} %shard_map.191), channel_id=1, source_target_pairs={{0,12},{1,13},{2,14},{3,15},{16,28},{17,29},{18,30},{19,31}} | collective-permute-start | bytes 786440 | tf_op jit(solution)/shard_map/ppermute | solution.py:26
  81.8 14.9 %collective-permute-start.21 = (s16[128,1024]{1,0:T(8,128)(2,1)}, s16[128,1024]{1,0:T(8,128)(2,1)S(1)}, u32[]{:S(2)}, u32[]{:S(2)}) collective-permute-start(s16[128,1024]{1,0:T(8,128)(2,1)} %get-tuple-element.69), channel_id=1, source_target_pairs={{4,0},{8,4},{12,8},{5,1},{9,5},{13,9},{6,2},{10,6},{14,10},{7,3},{... | collective-permute-start | bytes 786440 | tf_op jit(solution)/shard_map/ppermute | solution.py:26
  85.5 12.6 %collective-permute-start.22 = (s16[128,1024]{1,0:T(8,128)(2,1)}, s16[128,1024]{1,0:T(8,128)(2,1)S(1)}, u32[]{:S(2)}, u32[]{:S(2)}) collective-permute-start(s16[128,1024]{1,0:T(8,128)(2,1)} %get-tuple-element.70), channel_id=1, source_target_pairs={{8,0},{12,4},{9,1},{13,5},{10,2},{14,6},{11,3},{15,7},{24,16},{28,... | collective-permute-start | bytes 786440 | tf_op jit(solution)/shard_map/ppermute | solution.py:26
  91.7 12.8 %collective-permute-start.27 = (s16[96,1024]{1,0:T(8,128)(2,1)}, s16[96,1024]{1,0:T(8,128)(2,1)S(1)}, u32[]{:S(2)}, u32[]{:S(2)}) collective-permute-start(s16[96,1024]{1,0:T(8,128)(2,1)} %get-tuple-element.77), channel_id=1, source_target_pairs={{0,3},{1,0},{2,1},{3,2},{4,7},{5,4},{6,5},{7,6},{8,11},{9,8},{10,9... | collective-permute-start | bytes 589832 | tf_op jit(solution)/shard_map/ppermute | solution.py:39
  95.5 20.7 %collective-permute-start.28 = (s16[96,1024]{1,0:T(8,128)(2,1)}, s16[96,1024]{1,0:T(8,128)(2,1)S(1)}, u32[]{:S(2)}, u32[]{:S(2)}) collective-permute-start(s16[96,1024]{1,0:T(8,128)(2,1)} %get-tuple-element.78), channel_id=1, source_target_pairs={{0,2},{1,3},{2,0},{3,1},{4,6},{5,7},{6,4},{7,5},{8,10},{9,11},{10,... | collective-permute-start | bytes 589832 | tf_op jit(solution)/shard_map/ppermute | solution.py:39
  96.7 20.1 %collective-permute-start.29 = (s16[96,1024]{1,0:T(8,128)(2,1)}, s16[96,1024]{1,0:T(8,128)(2,1)S(1)}, u32[]{:S(2)}, u32[]{:S(2)}) collective-permute-start(s16[96,1024]{1,0:T(8,128)(2,1)} %get-tuple-element.79), channel_id=1, source_target_pairs={{0,1},{1,2},{2,3},{3,0},{4,5},{5,6},{6,7},{7,4},{8,9},{9,10},{10,1... | collective-permute-start | bytes 589832 | tf_op jit(solution)/shard_map/ppermute | solution.py:39
  99.5 17.9 %collective-permute-start.24 = (s16[32,1024]{1,0:T(8,128)(2,1)S(1)}, s16[32,1024]{1,0:T(8,128)(2,1)S(1)}, u32[]{:S(2)}, u32[]{:S(2)}) collective-permute-start(s16[32,1024]{1,0:T(8,128)(2,1)S(1)} %get-tuple-element.73), channel_id=1, source_target_pairs={{0,3},{1,0},{2,1},{3,2},{4,7},{5,4},{6,5},{7,6},{8,11},{9,8},{10,9... | collective-permute-start | bytes 196616 | tf_op jit(solution)/shard_map/ppermute | solution.py:39
  104.5 14.4 %collective-permute-start.25 = (s16[32,1024]{1,0:T(8,128)(2,1)S(1)}, s16[32,1024]{1,0:T(8,128)(2,1)S(1)}, u32[]{:S(2)}, u32[]{:S(2)}) collective-permute-start(s16[32,1024]{1,0:T(8,128)(2,1)S(1)} %get-tuple-element.74), channel_id=1, source_target_pairs={{0,2},{1,3},{2,0},{3,1},{4,6},{5,7},{6,4},{7,5},{8,10},{9,11},{10,... | collective-permute-start | bytes 196616 | tf_op jit(solution)/shard_map/ppermute | solution.py:39
  104.5 14.4 %collective-permute-start.26 = (s16[32,1024]{1,0:T(8,128)(2,1)S(1)}, s16[32,1024]{1,0:T(8,128)(2,1)S(1)}, u32[]{:S(2)}, u32[]{:S(2)}) collective-permute-start(s16[32,1024]{1,0:T(8,128)(2,1)S(1)} %get-tuple-element.75), channel_id=1, source_target_pairs={{0,1},{1,2},{2,3},{3,0},{4,5},{5,6},{6,7},{7,4},{8,9},{9,10},{10,1... | collective-permute-start | bytes 196616 | tf_op jit(solution)/shard_map/ppermute | solution.py:39
  116.1 20.6 %collective-permute-start.36 = (s16[32,1024]{1,0:T(8,128)(2,1)}, s16[32,1024]{1,0:T(8,128)(2,1)S(1)}, u32[]{:S(2)}, u32[]{:S(2)}) collective-permute-start(s16[32,1024]{1,0:T(8,128)(2,1)} %get-tuple-element.88), channel_id=1, source_target_pairs={{12,15},{13,12},{14,13},{15,14},{28,31},{29,28},{30,29},{31,30}} | collective-permute-start | bytes 196616 | tf_op jit(solution)/shard_map/ppermute | solution.py:39
  116.8 26.5 %collective-permute-start.37 = (s16[32,1024]{1,0:T(8,128)(2,1)}, s16[32,1024]{1,0:T(8,128)(2,1)S(1)}, u32[]{:S(2)}, u32[]{:S(2)}) collective-permute-start(s16[32,1024]{1,0:T(8,128)(2,1)} %get-tuple-element.89), channel_id=1, source_target_pairs={{12,14},{13,15},{14,12},{15,13},{28,30},{29,31},{30,28},{31,29}} | collective-permute-start | bytes 196616 | tf_op jit(solution)/shard_map/ppermute | solution.py:39
  120.7 8.9 %collective-permute-start.31 = (s16[32,1024]{1,0:T(8,128)(2,1)S(1)}, s16[32,1024]{1,0:T(8,128)(2,1)S(1)}, u32[]{:S(2)}, u32[]{:S(2)}) collective-permute-start(s16[32,1024]{1,0:T(8,128)(2,1)S(1)} %get-tuple-element.80.refs_1_), channel_id=1, source_target_pairs={{0,2},{1,3},{2,0},{3,1},{4,6},{5,7},{6,4},{7,5},{8,10},{9,11},{10,... | collective-permute-start | bytes 196616 | tf_op jit(solution)/shard_map/ppermute | solution.py:39
  127.1 16.2 %collective-permute-start.38 = (s16[32,1024]{1,0:T(8,128)(2,1)}, s16[32,1024]{1,0:T(8,128)(2,1)S(1)}, u32[]{:S(2)}, u32[]{:S(2)}) collective-permute-start(s16[32,1024]{1,0:T(8,128)(2,1)} %get-tuple-element.90), channel_id=1, source_target_pairs={{12,13},{13,14},{14,15},{15,12},{28,29},{29,30},{30,31},{31,28}} | collective-permute-start | bytes 196616 | tf_op jit(solution)/shard_map/ppermute | solution.py:39
  133.2 12.0 %collective-permute-start.33 = (s16[32,1024]{1,0:T(8,128)(2,1)S(1)}, s16[32,1024]{1,0:T(8,128)(2,1)S(1)}, u32[]{:S(2)}, u32[]{:S(2)}) collective-permute-start(s16[32,1024]{1,0:T(8,128)(2,1)S(1)} %get-tuple-element.82), channel_id=1, source_target_pairs={{0,3},{1,0},{2,1},{3,2},{4,7},{5,4},{6,5},{7,6},{8,11},{9,8},{10,9... | collective-permute-start | bytes 196616 | tf_op jit(solution)/shard_map/ppermute | solution.py:39
  136.0 9.2 %collective-permute-start.34 = (s16[32,1024]{1,0:T(8,128)(2,1)S(1)}, s16[32,1024]{1,0:T(8,128)(2,1)S(1)}, u32[]{:S(2)}, u32[]{:S(2)}) collective-permute-start(s16[32,1024]{1,0:T(8,128)(2,1)S(1)} %get-tuple-element.83), channel_id=1, source_target_pairs={{0,2},{1,3},{2,0},{3,1},{4,6},{5,7},{6,4},{7,5},{8,10},{9,11},{10,... | collective-permute-start | bytes 196616 | tf_op jit(solution)/shard_map/ppermute | solution.py:39
  136.7 8.5 %collective-permute-start.35 = (s16[32,1024]{1,0:T(8,128)(2,1)S(1)}, s16[32,1024]{1,0:T(8,128)(2,1)S(1)}, u32[]{:S(2)}, u32[]{:S(2)}) collective-permute-start(s16[32,1024]{1,0:T(8,128)(2,1)S(1)} %get-tuple-element.84), channel_id=1, source_target_pairs={{0,1},{1,2},{2,3},{3,0},{4,5},{5,6},{6,7},{7,4},{8,9},{9,10},{10,1... | collective-permute-start | bytes 196616 | tf_op jit(solution)/shard_map/ppermute | solution.py:39
  (40 other events, 571.0 us)

commit v4 on v3

--- a/solution.py
+++ b/solution.py
@@ -12,7 +12,6 @@
 learn_rate = 0.001
 adam_eps = 1e-08
 step_count = 100.0
-highest = lax.Precision.HIGHEST
 lanes = 128
 log_two = 0.6931471805599453
 levels = 32767.0
@@ -231,7 +230,9 @@
             bytes_accessed=26 * (stop - start) * feats * total,
             transcendentals=(stop - start) * feats * total,
         ),
-        compiler_params=pltpu.CompilerParams(vmem_limit_bytes=24 * 1024 * 1024),
+        compiler_params=pltpu.CompilerParams(
+            vmem_limit_bytes=24 * 1024 * 1024
+        ),
     )(me, *grads, weight, moments, *filled, *after)
 
 
@@ -242,9 +243,45 @@
         out_ref[j * feats : (j + 1) * feats, :] = part[...]
 
 
+def exact_add(total, lost, term):
+    added = total + term
+    seen = added - total
+    return added, lost + ((total - (added - seen)) + (term - seen))
+
+
+def partial_kernel(count, *refs):
+    encs, inputs_ref, outs, full = refs[:count], refs[count], refs[count + 1 : -1], refs[-1]
+    feats = encs[0].shape[0]
+    for j in range(count):
+        full[j * feats : (j + 1) * feats, :] = encs[j][...]
+    upper = full[...].astype(jnp.bfloat16)
+    rest = full[...] - upper.astype(jnp.float32)
+    middle = rest.astype(jnp.bfloat16)
+    lower = (rest - middle.astype(jnp.float32)).astype(jnp.bfloat16)
+    total, lost = None, 0.0
+    for cols in blocks_of(full.shape[1], 256):
+        right = inputs_ref[cols, :]
+        term, fine, finest = (
+            jnp.dot(left[:, cols], right, preferred_element_type=jnp.float32)
+            for left in (upper, middle, lower)
+        )
+        lost = lost + (fine + finest)
+        if total is None:
+            total = term
+        else:
+            total, lost = exact_add(total, lost, term)
+    total = total + lost
+    for j in range(count):
+        outs[j][...] = total[j * feats : (j + 1) * feats, :]
+
+
 def codes_kernel(count, *refs):
     parts, bias_ref, mask_ref, codes_ref, coded_ref = refs[:count], *refs[count:]
-    pre = bias_ref[...] + sum(part[...] for part in parts)
+    pre, lost = parts[0][...], 0.0
+    for part in parts[1:]:
+        pre, lost = exact_add(pre, lost, part[...])
+    pre, lost = exact_add(pre, lost, jnp.broadcast_to(bias_ref[...], pre.shape))
+    pre = pre + lost
     codes = jnp.maximum(pre, 0.0) * mask_ref[...]
     codes_ref[...] = codes
     code_into(coded_ref, slice(None), codes)
@@ -252,32 +289,38 @@
 
 def weights_kernel(count, feats, starts, *refs):
     parts = len(starts)
-    fars, up_ref, low_ref, refs = refs[: parts * count], *refs[parts * count :][:2], refs[parts * count + 2 :]
-    *buffers, full, arrive = refs
+    fars, refs = refs[: parts * count], refs[parts * count :]
+    (up_ref, low_ref), (*buffers, full, arrive) = refs[:2], refs[2:]
     held = Fetched(fars, buffers, arrive)
     for part, (start, stop) in enumerate(starts):
         for j in range(count):
             weights = held[part * count + j]
             for k in range(start, stop):
-                row = (k * count + j) * feats
+                row = ((k - starts[0][0]) * count + j) * feats
                 rows = slice((k - start) * feats, (k - start + 1) * feats)
                 full[row : row + feats, :] = decoded(weights, rows)
     for rows in blocks_of(full.shape[0], 32):
         up_ref[rows, :], low_ref[rows, :] = split(full[rows, :])
 
 
-def main_kernel(count, reach, feats, starts, *refs):
-    sources, results = count + reach - 1 + 4, reach + len(starts) * count
+def main_kernel(count, reach, feats, starts, pieces, lates, *refs):
+    fetched = count * len(lates)
+    sources = count + reach - 1 + 2 * len(pieces) + fetched + 2
+    results = reach + len(starts) * count
     fars, far_outs, sum_ref = refs[:sources], refs[sources : sources + results], refs[sources + results]
     refs = refs[sources + results + 1 :]
-    buffers, outs, refs = refs[:sources], refs[sources : sources + results], refs[sources + results :]
-    full, grad, res_up, res_low, src_up, src_low, arrive, leave = refs
-    held = Fetched(fars, buffers, arrive)
+    plain = count + reach - 1
+    buffers, refs = refs[: plain + fetched + 2], refs[plain + fetched + 2 :]
+    outs, refs = refs[:results], refs[results:]
+    full, grad, w_up, w_low, res_up, res_low, src_up, src_low, arrive, leave = refs
+    block = count * feats
+    places = [pl.ds(start * block, (stop - start) * block) for start, stop in pieces]
+    rooms = [ref.at[place] for place in places for ref in (w_up, w_low)]
+    held = Fetched(fars, [*buffers[:plain], *rooms, *buffers[plain:]], arrive)
     sends = [
         pltpu.make_async_copy(source, out, leave.at[i])
         for i, (source, out) in enumerate(zip(outs, far_outs, strict=True))
     ]
-    block = count * feats
     for j in range(count):
         full[j * feats : (j + 1) * feats, :] = decoded(held[j], slice(None))
     for k in range(1, reach):
@@ -286,7 +329,18 @@
             full[k * block + rows.start : k * block + rows.stop, :] = decoded(moved, rows)
     for rows in blocks_of(reach * block, 32):
         src_up[rows, :], src_low[rows, :] = split(full[rows, :])
-    w_up, w_low = held[sources - 4], held[sources - 3]
+    for i in range(2 * len(pieces)):
+        held[plain + i]
+    for part, (start, stop) in enumerate(lates):
+        for j in range(count):
+            weights = held[plain + 2 * len(pieces) + part * count + j]
+            for k in range(start, stop):
+                row = (k * count + j) * feats
+                rows = slice((k - start) * feats, (k - start + 1) * feats)
+                grad[row : row + feats, :] = decoded(weights, rows)
+        for rows in blocks_of((stop - start) * block, 32):
+            rows = slice(start * block + rows.start, start * block + rows.stop)
+            w_up[rows, :], w_low[rows, :] = split(grad[rows, :])
     bias_ref, targets_ref = held[sources - 2], held[sources - 1]
     width, row_count = targets_ref.shape
     for cols in blocks_of(width, 256):
@@ -307,11 +361,14 @@
             source = slice(k * block + rows.start, k * block + rows.stop)
             code_into(outs[k], rows, full[source, :])
         sends[k].start()
-    for rows in blocks_of(width, 256):
-        grad[:, rows] = product(
-            (src_up[...], src_low[...]), (res_up[rows, :], res_low[rows, :]), ((1,), (1,))
-        )
     for part, (start, stop) in enumerate(starts):
+        held_rows = slice(start * block, stop * block)
+        for rows in blocks_of(width, 256):
+            grad[held_rows, rows] = product(
+                (src_up[held_rows, :], src_low[held_rows, :]),
+                (res_up[rows, :], res_low[rows, :]),
+                ((1,), (1,)),
+            )
         for j in range(count):
             place = reach + part * count + j
             for k in range(start, stop):
@@ -324,7 +381,9 @@
 
 
 def code_sum_kernel(count, feats, moved_count, *refs):
-    own, moved, outs = refs[0], refs[1 : 1 + moved_count], refs[1 + moved_count :]
+    codes_ref, kept_ref = refs[0], refs[-1]
+    own, moved, outs = refs[1], refs[2 : 2 + moved_count], refs[2 + moved_count : -1]
+    kept_ref[...] = codes_ref[...]
     for j in range(count):
         rows = slice(j * feats, (j + 1) * feats)
         total = own[rows, :]
@@ -400,55 +459,60 @@
     tile_active = jnp.any(hits, axis=1).astype(jnp.float32)
     row_mask = jnp.repeat(tile_active, tile_rows, axis=0)[None, :]
 
-    enc_cols = jnp.concatenate(
-        [rotated(slab_of(enc_local, j, width), j) for j in range(count)], axis=0
-    )
+    enc_cols = [rotated(slab_of(enc_local, j, width), j) for j in range(count)]
     me = lax.axis_index("feat").astype(jnp.int32).reshape(1)
     half_way = max(1, reach // 2)
-    starts = [(0, half_way)] + [(k, k + 1) for k in range(half_way, reach)]
-    dec_cols = []
-    for first, last in starts[1:]:
-        sent = packed(me, dec_local, first, last)
-        dec_cols += [rotated(sent[j], j, first) for j in range(count)]
-    partial = jnp.dot(
-        enc_cols,
-        inputs_local.astype(jnp.float32),
-        precision=highest,
-        preferred_element_type=jnp.float32,
-    ).reshape(count, feats, row_count)
+    sent = packed(me, dec_local, 0, half_way)
+    early = [rotated(sent[j], j) for j in range(count)]
+    partial = call(
+        functools.partial(partial_kernel, count),
+        [shape(feats, row_count)] * count,
+        [*enc_cols, inputs_local],
+        flops=6 * block * width * row_count,
+        scratch=[pltpu.VMEM((block, width), jnp.float32)],
+    )
     partials = [rotated(partial[j], -j) for j in range(count)]
     codes, coded_codes = call(
         functools.partial(codes_kernel, count),
         [shape(feats, row_count), coded_shape(feats, row_count)],
         [*partials, encb_local[:, None], row_mask],
-        after=[a for i, a in enumerate(dec_cols) if i % count],
+        after=early[1:],
     )
     own = [rotated(coded_codes, j) for j in range(count)]
-    gathered = call(gather_kernel, [coded_shape(block, row_count)], own)[0]
+    half = jnp.bfloat16
+
+    def weights_of(starts, columns):
+        rows = (starts[-1][1] - starts[0][0]) * block
+        return call(
+            functools.partial(weights_kernel, count, feats, starts),
+            [shape(rows, width, half)] * 2,
+            [],
+            scratch=[buffer_like(a) for a in columns]
+            + [pltpu.VMEM((rows, width), jnp.float32), pltpu.SemaphoreType.DMA((len(columns),))],
+            far=columns,
+        )
+
+    pieces = [(0, half_way)]
+    weights = [*weights_of(pieces, early)]
+    gathered = call(gather_kernel, [coded_shape(block, row_count)], own, after=weights[:1])[0]
     moved = [shifted(gathered, "layer", k) for k in range(1, reach)]
-    sent = packed(me, dec_local, *starts[0], after=[coded_codes])
-    dec_cols = [rotated(sent[j], j) for j in range(count)] + dec_cols
-    half = jnp.bfloat16
-    weights = call(
-        functools.partial(weights_kernel, count, feats, starts),
-        [shape(depth, width, half)] * 2,
-        [],
-        scratch=[buffer_like(a) for a in dec_cols]
-        + [pltpu.VMEM((depth, width), jnp.float32), pltpu.SemaphoreType.DMA((len(dec_cols),))],
-        far=dec_cols,
-    )
-    backs = ((0, reach - 1), (reach - 1, reach)) if reach > 1 else ((0, reach),)
-    far = [*own, *moved, *weights, decb_local[:, None], targets_local]
+    late, lates = [], [(half_way, reach)] if half_way < reach else []
+    for first, last in lates:
+        sent = packed(me, dec_local, first, last, after=[coded_codes])
+        late += [rotated(sent[j], j, first) for j in range(count)]
+    backs = (*pieces, *lates)
+    far = [*own, *moved, *weights, *late, decb_local[:, None], targets_local]
     far_out = [shape(block, row_count)] + [coded_shape(block, row_count)] * (reach - 1)
     for first, last in backs:
         far_out += [coded_shape((last - first) * feats, width)] * count
     outs = call(
-        functools.partial(main_kernel, count, reach, feats, backs),
+        functools.partial(main_kernel, count, reach, feats, backs, pieces, lates),
         [shape(width, 1)],
         [],
         flops=18 * depth * width * row_count,
-        scratch=[buffer_like(a) for a in [*far, *far_out]]
+        scratch=[buffer_like(a) for a in [*own, *moved, *late, *far[-2:], *far_out]]
         + [pltpu.VMEM((depth, row_count), jnp.float32), pltpu.VMEM((depth, width), jnp.float32)]
+        + [pltpu.VMEM((depth, width), half)] * 2
         + [pltpu.VMEM((width, row_count), half)] * 2
         + [pltpu.VMEM((depth, row_count), half)] * 2
         + [pltpu.SemaphoreType.DMA((len(far),)), pltpu.SemaphoreType.DMA((len(far_out),))],
@@ -463,15 +527,20 @@
     ]
     sums = call(
         functools.partial(code_sum_kernel, count, feats, reach - 1),
-        [shape(feats, row_count)] + [coded_shape(feats, row_count)] * (count - 1),
-        [part, *returned],
+        [shape(feats, row_count)]
+        + [coded_shape(feats, row_count)] * (count - 1)
+        + [shape(feats, row_count)],
+        [codes, part, *returned],
     )
     arrived = [rotated(sums[j], -j) for j in range(count)]
     coded_grad, grad_enc_bias = call(
         functools.partial(pre_grad_kernel, count),
         [coded_shape(feats, row_count), shape(feats, 1)],
-        [*arrived, codes],
+        [*arrived, sums[-1]],
         after=grad_dec_cols[0][1:],
+    )
+    dec_done = adam_call(
+        me, *backs[0], grad_dec_cols[0], dec_local, dec_moments[:, 0], after=[coded_grad]
     )
     pre_grads = [rotated(coded_grad, j) for j in range(count)]
     grad_enc_cols = call(
@@ -485,11 +554,11 @@
             pltpu.VMEM((block, width), jnp.float32),
             pltpu.SemaphoreType.DMA((1,)),
         ],
+        after=dec_done[:1],
         far=[inputs_local],
         alone=False,
     )
-    dec_done = ()
-    for (first, last), grads in zip(backs, grad_dec_cols):
+    for (first, last), grads in zip(backs[1:], grad_dec_cols[1:]):
         dec_done = adam_call(
             me, first, last, grads, dec_local, dec_moments[:, 0], dec_done, [grad_enc_cols[0]]
         )

time: 150 us -> 138 us (0.920); the launches traced: 147 us -> 137 us
  starting transfers between devices: 71.5 us -> 64.8 us
  local copies, waits for them, and re-layouts: 13 us -> 10.8 us
    ppermute x6, starting transfers between devices: 14.4 us -> 7.93 us  [shifted(): lax.ppermute(value, axis, [(source, source + steps) for source in range(i...]
    ppermute x33 -> x30, waiting for transfers between devices: 26.4 us -> 22.5 us  [rotated(): return lax.ppermute(value, ('layer', 'feat'), pairs)]
    ppermute x6, waiting for transfers between devices: 0.02 us -> 3.27 us  [shifted(): lax.ppermute(value, axis, [(source, source + steps) for source in range(i...]
    unnamed x67 -> x63, local copies, waits for them, and re-layouts: 9.89 us -> 8.4 us
    ppermute x33 -> x30, starting transfers between devices: 57.1 us -> 56.9 us  [rotated(): return lax.ppermute(value, ('layer', 'feat'), pairs)]
  transfers between devices with their start and end apart: 39 -> 36, of which waited for: 9 -> 7; matrix products, arithmetic and copies ran while one was open for 5% -> 4% of each run, Pallas kernels for 9% -> 10%
where the time goes in v4:
time: 138 us; the launch traced here: 137 us
  starting transfers between devices  64.8 us (47%)
  Pallas kernels  29.8 us (22%)
  waiting for transfers between devices  25.7 us (19%)
  local copies, waits for them, and re-layouts  10.8 us (8%)
  other arithmetic  3.97 us (3%)
  between operations  1.88 us (1%)
    ppermute x30, starting transfers between devices, rotated(): return lax.ppermute(value, ('layer', 'feat'), pairs)  56.9 us
    pallas_call x10, Pallas kernels, call(): pl.pallas_call(body, out_shape=(*far_out, *out_shape), in_specs=[pl.Block...  22.6 us
    ppermute x30, waiting for transfers between devices, rotated(): return lax.ppermute(value, ('layer', 'feat'), pairs)  22.5 us
    unnamed x63, local copies, waits for them, and re-layouts  8.4 us
    ppermute x6, starting transfers between devices, shifted(): lax.ppermute(value, axis, [(source, source + steps) for source in range(i...  7.93 us
    pallas_call x3, Pallas kernels, adam_call(): pl.pallas_call(functools.partial(adam_kernel, count), grid=(stop - start,...  7.19 us
    ppermute x6, waiting for transfers between devices, shifted(): lax.ppermute(value, axis, [(source, source + steps) for source in range(i...  3.27 us
  transfers between devices with their start and end apart: 36, of which 7 were waited for; matrix products, arithmetic and copies ran while one was open for 4% of the time, Pallas kernels for 10%

profile of v4, /device:TPU:2, one launch (start us, length us, event | category | flops | bytes accessed | tf_op | source)
XLA Modules:
  0.0 137.0 jit_solution(17973528053326490018)
XLA Ops:
  1.8 3.7 %collective-permute-start.2 = (f32[32,1024]{1,0:T(8,128)S(1)}, f32[32,1024]{1,0:T(8,128)S(1)}, u32[]{:S(2)}, u32[]{:S(2)}) collective-permute-start(f32[32,1024]{1,0:T(8,128)S(1)} %get-tuple-element.122), channel_id=1, source_target_pairs={{0,3},{1,0},{2,1},{3,2},{4,7},{5,4},{6,5},{7,6},{8,11},{9,8},{10,9... | collective-permute-start | bytes 393224 | tf_op jit(solution)/shard_map/ppermute | solution.py:38
  8.4 2.5 %collective-permute-start.6 = (s16[64,1024]{1,0:T(8,128)(2,1)S(1)}, s16[64,1024]{1,0:T(8,128)(2,1)S(1)}, u32[]{:S(2)}, u32[]{:S(2)}) collective-permute-start(s16[64,1024]{1,0:T(8,128)(2,1)S(1)} %get-tuple-element.58), channel_id=1, source_target_pairs={{0,1},{1,2},{2,3},{3,0},{4,5},{5,6},{6,7},{7,4},{8,9},{9,10},{10,1... | collective-permute-start | bytes 393224 | tf_op jit(solution)/shard_map/ppermute | solution.py:38
  11.8 1.9 %collective-permute-start.8 = (s16[64,1024]{1,0:T(8,128)(2,1)S(1)}, s16[64,1024]{1,0:T(8,128)(2,1)S(1)}, u32[]{:S(2)}, u32[]{:S(2)}) collective-permute-start(s16[64,1024]{1,0:T(8,128)(2,1)S(1)} %get-tuple-element.60), channel_id=1, source_target_pairs={{0,3},{1,0},{2,1},{3,2},{4,7},{5,4},{6,5},{7,6},{8,11},{9,8},{10,9... | collective-permute-start | bytes 393224 | tf_op jit(solution)/shard_map/ppermute | solution.py:38
  13.7 9.4 %collective-permute-done.1.refs_2_ = f32[32,1024]{1,0:T(8,128)S(1)} collective-permute-done((f32[32,1024]{1,0:T(8,128)S(1)}, f32[32,1024]{1,0:T(8,128)S(1)}, u32[]{:S(2)}, u32[]{:S(2)}) %collective-permute-start.1) | collective-permute-done | bytes 131104 | tf_op jit(solution)/shard_map/ppermute | solution.py:38
  23.1 1.9 %shard_map.188 = (f32[32,1024]{1,0:T(8,128)S(1)}, f32[32,1024]{1,0:T(8,128)}, f32[32,1024]{1,0:T(8,128)}, f32[32,1024]{1,0:T(8,128)S(1)}) custom-call(f32[32,1024]{1,0:T(8,128)S(1)} %get-tuple-element.125.refs_0_, f32[32,1024]{1,0:T(8,128)S(1)} %collective-permute-done.refs_1_, f32[32,1024]{1,0:T(8,128)S(1)} %collective-permute-done.1.refs_2_, ...), custom_call_target="tpu_custom_call" | custom-call | flops 805306368 | bytes 3145728 | tf_op jit(solution)/shard_map/pallas_call | solution.py:134
  25.0 2.7 %collective-permute-start.4 = (f32[32,1024]{1,0:T(8,128)}, f32[32,1024]{1,0:T(8,128)S(1)}, u32[]{:S(2)}, u32[]{:S(2)}) collective-permute-start(f32[32,1024]{1,0:T(8,128)} %get-tuple-element.56), channel_id=1, source_target_pairs={{0,2},{1,3},{2,0},{3,1},{4,6},{5,7},{6,4},{7,5},{8,10},{9,11},{10,... | collective-permute-start | bytes 393224 | tf_op jit(solution)/shard_map/ppermute | solution.py:38
  27.7 2.9 %collective-permute-start.5 = (f32[32,1024]{1,0:T(8,128)S(1)}, f32[32,1024]{1,0:T(8,128)S(1)}, u32[]{:S(2)}, u32[]{:S(2)}) collective-permute-start(f32[32,1024]{1,0:T(8,128)S(1)} %get-tuple-element.57), channel_id=1, source_target_pairs={{0,1},{1,2},{2,3},{3,0},{4,5},{5,6},{6,7},{7,4},{8,9},{9,10},{10,1... | collective-permute-start | bytes 393224 | tf_op jit(solution)/shard_map/ppermute | solution.py:38
  31.8 7.4 %collective-permute-done.4.refs_2_ = f32[32,1024]{1,0:T(8,128)S(1)} collective-permute-done((f32[32,1024]{1,0:T(8,128)}, f32[32,1024]{1,0:T(8,128)S(1)}, u32[]{:S(2)}, u32[]{:S(2)}) %collective-permute-start.4) | collective-permute-done | bytes 131104 | tf_op jit(solution)/shard_map/ppermute | solution.py:38
  39.5 2.1 %collective-permute-start.11 = (s16[32,1024]{1,0:T(8,128)(2,1)S(1)}, s16[32,1024]{1,0:T(8,128)(2,1)S(1)}, u32[]{:S(2)}, u32[]{:S(2)}) collective-permute-start(s16[32,1024]{1,0:T(8,128)(2,1)S(1)} %get-tuple-element.62.refs_0_.refs_2_), channel_id=1, source_target_pairs={{0,3},{1,0},{2,1},{3,2},{4,7},{5,4},{6,5},{7,6},{8,11},{9,8},{10,9... | collective-permute-start | bytes 196616 | tf_op jit(solution)/shard_map/ppermute | solution.py:38
  42.2 1.9 %collective-permute-start.9 = (s16[32,1024]{1,0:T(8,128)(2,1)S(1)}, s16[32,1024]{1,0:T(8,128)(2,1)S(1)}, u32[]{:S(2)}, u32[]{:S(2)}) collective-permute-start(s16[32,1024]{1,0:T(8,128)(2,1)S(1)} %get-tuple-element.62.refs_0_.refs_2_), channel_id=1, source_target_pairs={{0,1},{1,2},{2,3},{3,0},{4,5},{5,6},{6,7},{7,4},{8,9},{9,10},{10,1... | collective-permute-start | bytes 196616 | tf_op jit(solution)/shard_map/ppermute | solution.py:38
  44.2 2.4 %shard_map.191 = (bf16[256,1024]{1,0:T(8,128)(2,1)}, bf16[256,1024]{1,0:T(8,128)(2,1)}) custom-call(s16[64,1024]{1,0:T(8,128)(2,1)} %copy-done.17, s16[64,1024]{1,0:T(8,128)(2,1)} %copy-done.10, s16[64,1024]{1,0:T(8,128)(2,1)} %copy-done.11, s16[64,1024]{1,0:T(8,128)(2,1)} %copy-done.12), custom_call_target="tpu_custom_call" | custom-call | bytes 1572864 | tf_op jit(solution)/shard_map/pallas_call | solution.py:134
  47.6 2.8 %collective-permute-start.15 = (s16[64,1024]{1,0:T(8,128)(2,1)S(1)}, s16[64,1024]{1,0:T(8,128)(2,1)S(1)}, u32[]{:S(2)}, u32[]{:S(2)}) collective-permute-start(s16[64,1024]{1,0:T(8,128)(2,1)S(1)} %get-tuple-element.67), channel_id=1, source_target_pairs={{8,9},{9,10},{10,11},{11,8},{12,13},{13,14},{14,15},{15,12},{24,25... | collective-permute-start | bytes 393224 | tf_op jit(solution)/shard_map/ppermute | solution.py:38
  52.5 1.9 %collective-permute-start.12 = (s16[128,1024]{1,0:T(8,128)(2,1)S(1)}, s16[128,1024]{1,0:T(8,128)(2,1)}, u32[]{:S(2)}, u32[]{:S(2)}) collective-permute-start(s16[128,1024]{1,0:T(8,128)(2,1)S(1)} %shard_map.192), channel_id=1, source_target_pairs={{0,4},{4,8},{8,12},{1,5},{5,9},{9,13},{2,6},{6,10},{10,14},{3,7},{... | collective-permute-start | bytes 786440 | tf_op jit(solution)/shard_map/ppermute | solution.py:25
  54.4 3.4 %collective-permute-start.16 = (s16[64,1024]{1,0:T(8,128)(2,1)S(1)}, s16[64,1024]{1,0:T(8,128)(2,1)S(1)}, u32[]{:S(2)}, u32[]{:S(2)}) collective-permute-start(s16[64,1024]{1,0:T(8,128)(2,1)S(1)} %get-tuple-element.68), channel_id=1, source_target_pairs={{8,10},{9,11},{10,8},{11,9},{12,14},{13,15},{14,12},{15,13},{24,26... | collective-permute-start | bytes 393224 | tf_op jit(solution)/shard_map/ppermute | solution.py:38
  57.9 3.5 %collective-permute-start.17 = (s16[64,1024]{1,0:T(8,128)(2,1)S(1)}, s16[64,1024]{1,0:T(8,128)(2,1)}, u32[]{:S(2)}, u32[]{:S(2)}) collective-permute-start(s16[64,1024]{1,0:T(8,128)(2,1)S(1)} %get-tuple-element.69), channel_id=1, source_target_pairs={{8,11},{9,8},{10,9},{11,10},{12,15},{13,12},{14,13},{15,14},{24,27... | collective-permute-start | bytes 393224 | tf_op jit(solution)/shard_map/ppermute | solution.py:38
  62.4 2.3 %collective-permute-done.16.refs_11_ = s16[64,1024]{1,0:T(8,128)(2,1)S(1)} collective-permute-done((s16[64,1024]{1,0:T(8,128)(2,1)S(1)}, s16[64,1024]{1,0:T(8,128)(2,1)S(1)}, u32[]{:S(2)}, u32[]{:S(2)}) %collective-permute-start.16) | collective-permute-done | bytes 131104 | tf_op jit(solution)/shard_map/ppermute | solution.py:38
  66.2 14.7 %shard_map.194 = (f32[128,1024]{1,0:T(8,128)}, s16[128,1024]{1,0:T(8,128)(2,1)}, s16[128,1024]{1,0:T(8,128)(2,1)}, s16[128,1024]{1,0:T(8,128)(2,1)}, s16[64,1024...) custom-call(s16[32,1024]{1,0:T(8,128)(2,1)} %copy-done.14, ...), custom_call_target="tpu_custom_call" | custom-call | flops 9663676416 | bytes 7086080 | tf_op jit(solution)/shard_map/pallas_call | solution.py:134
  81.0 2.1 %collective-permute-start.18 = (s16[128,1024]{1,0:T(8,128)(2,1)}, s16[128,1024]{1,0:T(8,128)(2,1)S(1)}, u32[]{:S(2)}, u32[]{:S(2)}) collective-permute-start(s16[128,1024]{1,0:T(8,128)(2,1)} %get-tuple-element.71), channel_id=1, source_target_pairs={{4,0},{8,4},{12,8},{5,1},{9,5},{13,9},{6,2},{10,6},{14,10},{7,3},{... | collective-permute-start | bytes 786440 | tf_op jit(solution)/shard_map/ppermute | solution.py:25
  85.0 3.6 %collective-permute-start.24 = (s16[64,1024]{1,0:T(8,128)(2,1)}, s16[64,1024]{1,0:T(8,128)(2,1)S(1)}, u32[]{:S(2)}, u32[]{:S(2)}) collective-permute-start(s16[64,1024]{1,0:T(8,128)(2,1)} %get-tuple-element.79), channel_id=1, source_target_pairs={{0,3},{1,0},{2,1},{3,2},{4,7},{5,4},{6,5},{7,6},{8,11},{9,8},{10,9... | collective-permute-start | bytes 393224 | tf_op jit(solution)/shard_map/ppermute | solution.py:38
  91.2 3.3 %collective-permute-done.19.refs_3_ = s16[128,1024]{1,0:T(8,128)(2,1)S(1)} collective-permute-done((s16[128,1024]{1,0:T(8,128)(2,1)}, s16[128,1024]{1,0:T(8,128)(2,1)S(1)}, u32[]{:S(2)}, u32[]{:S(2)}) %collective-permute-start.19) | collective-permute-done | bytes 262176 | tf_op jit(solution)/shard_map/ppermute | solution.py:25
  96.0 3.6 %collective-permute-start.21 = (s16[32,1024]{1,0:T(8,128)(2,1)S(1)}, s16[32,1024]{1,0:T(8,128)(2,1)S(1)}, u32[]{:S(2)}, u32[]{:S(2)}) collective-permute-start(s16[32,1024]{1,0:T(8,128)(2,1)S(1)} %get-tuple-element.75), channel_id=1, source_target_pairs={{0,3},{1,0},{2,1},{3,2},{4,7},{5,4},{6,5},{7,6},{8,11},{9,8},{10,9... | collective-permute-start | bytes 196616 | tf_op jit(solution)/shard_map/ppermute | solution.py:38
  101.6 4.4 %collective-permute-start.33 = (s16[64,1024]{1,0:T(8,128)(2,1)}, s16[64,1024]{1,0:T(8,128)(2,1)S(1)}, u32[]{:S(2)}, u32[]{:S(2)}) collective-permute-start(s16[64,1024]{1,0:T(8,128)(2,1)} %get-tuple-element.92), channel_id=1, source_target_pairs={{8,11},{9,8},{10,9},{11,10},{12,15},{13,12},{14,13},{15,14},{24,27... | collective-permute-start | bytes 393224 | tf_op jit(solution)/shard_map/ppermute | solution.py:38
  106.0 3.0 %collective-permute-start.34 = (s16[64,1024]{1,0:T(8,128)(2,1)}, s16[64,1024]{1,0:T(8,128)(2,1)S(1)}, u32[]{:S(2)}, u32[]{:S(2)}) collective-permute-start(s16[64,1024]{1,0:T(8,128)(2,1)} %get-tuple-element.93), channel_id=1, source_target_pairs={{8,10},{9,11},{10,8},{11,9},{12,14},{13,15},{14,12},{15,13},{24,26... | collective-permute-start | bytes 393224 | tf_op jit(solution)/shard_map/ppermute | solution.py:38
  111.2 1.9 %collective-permute-start.27 = (s16[32,1024]{1,0:T(8,128)(2,1)S(1)}, s16[32,1024]{1,0:T(8,128)(2,1)S(1)}, u32[]{:S(2)}, u32[]{:S(2)}) collective-permute-start(s16[32,1024]{1,0:T(8,128)(2,1)S(1)} %get-tuple-element.82.refs_6_.refs_1_), channel_id=1, source_target_pairs={{0,1},{1,2},{2,3},{3,0},{4,5},{5,6},{6,7},{7,4},{8,9},{9,10},{10,1... | collective-permute-start | bytes 196616 | tf_op jit(solution)/shard_map/ppermute | solution.py:38
  114.5 2.2 %copy-done.2 = f32[2,1,4,32,4096]{4,3,2,1,0:T(8,128)S(1)} copy-done((f32[2,1,4,32,4096]{4,3,2,1,0:T(8,128)S(1)}, f32[2,1,4,32,4096]{4,3,2,1,0:T(8,128)}, u32[]{:S(2)}) %copy-start.2) | copy-done | bytes 4194328
  116.7 2.7 %shard_map.197 = (f32[4,32,4096]{2,1,0:T(8,128)}, f32[2,4,32,4096]{3,2,1,0:T(8,128)}) custom-call(s32[1]{0:T(128)} %bitcast.refs_0_.me_ref, s16[64,1024]{1,0:T(8,128)(2,1)S(1)} %copy-done.16, s16[64,1024]{1,0:T(8,128)(2,1)S(1)} %collective-permute-done.24.refs_5_.refs_1_, s16[64,1024]{1,0:T(8,128)(2,1)S(1)} %collective-permute-done.25.refs_6_.refs_2_, ...), custom_call_target="tpu_custom_call" | custom-call | flops 5242880 | bytes 6815744 | tf_op jit(solution)/shard_map/pallas_call | solution.py:215
  119.4 4.0 %collective-permute-start.35 = (s16[64,1024]{1,0:T(8,128)(2,1)S(1)}, s16[64,1024]{1,0:T(8,128)(2,1)S(1)}, u32[]{:S(2)}, u32[]{:S(2)}) collective-permute-start(s16[64,1024]{1,0:T(8,128)(2,1)S(1)} %copy-done.28), channel_id=1, source_target_pairs={{8,9},{9,10},{10,11},{11,8},{12,13},{13,14},{14,15},{15,12},{24,25... | collective-permute-start | bytes 393224 | tf_op jit(solution)/shard_map/ppermute | solution.py:38
  125.1 2.0 %shard_map.198 = (s16[32,1024]{1,0:T(8,128)(2,1)S(1)}, s16[32,1024]{1,0:T(8,128)(2,1)S(1)}, s16[32,1024]{1,0:T(8,128)(2,1)S(1)}, s16[32,1024]{1,0:T(8,128)(2,1)S(1)}) custom-call(bf16[1024,1024]{1,0:T(8,128)(2,1)S(1)} %bitcast.57, s16[32,1024]{1,0:T(8,128)(2,1)S(1)} %get-tuple-element.82.refs_6_.refs_1_, ...), custom_call_target="tpu_custom_call" | custom-call | flops 536870912 | bytes 2621440 | tf_op jit(solution)/shard_map/pallas_call | solution.py:134
  127.1 1.7 %collective-permute-start.30 = (s16[32,1024]{1,0:T(8,128)(2,1)S(1)}, s16[32,1024]{1,0:T(8,128)(2,1)S(1)}, u32[]{:S(2)}, u32[]{:S(2)}) collective-permute-start(s16[32,1024]{1,0:T(8,128)(2,1)S(1)} %get-tuple-element.86), channel_id=1, source_target_pairs={{0,3},{1,0},{2,1},{3,2},{4,7},{5,4},{6,5},{7,6},{8,11},{9,8},{10,9... | collective-permute-start | bytes 196616 | tf_op jit(solution)/shard_map/ppermute | solution.py:38
  130.7 2.7 %shard_map.200 = (f32[4,32,4096]{2,1,0:T(8,128)}, f32[2,4,32,4096]{3,2,1,0:T(8,128)}) custom-call(s32[1]{0:T(128)} %bitcast.refs_0_.me_ref, s16[64,1024]{1,0:T(8,128)(2,1)S(1)} %copy-done.15, s16[64,1024]{1,0:T(8,128)(2,1)S(1)} %collective-permute-done.33.refs_1_, ...), custom_call_target="tpu_custom_call", output_to_operand_aliasing={{0}: (7, {}), {1}: (8, {})} | custom-call | flops 5242880 | bytes 6815744 | tf_op jit(solution)/shard_map/pallas_call | solution.py:215
  133.4 1.9 %collective-permute-done.31.refs_2_ = s16[32,1024]{1,0:T(8,128)(2,1)S(1)} collective-permute-done((s16[32,1024]{1,0:T(8,128)(2,1)S(1)}, s16[32,1024]{1,0:T(8,128)(2,1)S(1)}, u32[]{:S(2)}, u32[]{:S(2)}) %collective-permute-start.31) | collective-permute-done | bytes 65568 | tf_op jit(solution)/shard_map/ppermute | solution.py:38
  135.3 1.8 %shard_map.199 = (f32[1,32,4096]{2,1,0:T(8,128)}, f32[2,1,32,4096]{3,2,1,0:T(8,128)}) custom-call(s32[1]{0:T(128)} %bitcast.refs_0_.me_ref, s16[32,1024]{1,0:T(8,128)(2,1)S(1)} %get-tuple-element.85.refs_0_.refs_8_, s16[32,1024]{1,0:T(8,128)(2,1)S(1)} %collective-permute-done.30.refs_1_, s16[32,1024]{1,0:T(8,128)(2,1)S(1)} %collective-permute-done.31.refs_2_, ...), custom_call_target="tpu_custom_call" | custom-call | flops 2621440 | bytes 3407872 | tf_op jit(solution)/shard_map/pallas_call | solution.py:215
  (129 shorter events, 26.8 us)
Async XLA Ops:
  1.8 10.0 %collective-permute-start.2 = (f32[32,1024]{1,0:T(8,128)S(1)}, f32[32,1024]{1,0:T(8,128)S(1)}, u32[]{:S(2)}, u32[]{:S(2)}) collective-permute-start(f32[32,1024]{1,0:T(8,128)S(1)} %get-tuple-element.122), channel_id=1, source_target_pairs={{0,3},{1,0},{2,1},{3,2},{4,7},{5,4},{6,5},{7,6},{8,11},{9,8},{10,9... | collective-permute-start | bytes 393224 | tf_op jit(solution)/shard_map/ppermute | solution.py:38
  5.5 17.6 %collective-permute-start.1 = (f32[32,1024]{1,0:T(8,128)S(1)}, f32[32,1024]{1,0:T(8,128)S(1)}, u32[]{:S(2)}, u32[]{:S(2)}) collective-permute-start(f32[32,1024]{1,0:T(8,128)S(1)} %get-tuple-element.123), channel_id=1, source_target_pairs={{0,2},{1,3},{2,0},{3,1},{4,6},{5,7},{6,4},{7,5},{8,10},{9,11},{10,... | collective-permute-start | bytes 393224 | tf_op jit(solution)/shard_map/ppermute | solution.py:38
  5.5 17.6 %collective-permute-start = (f32[32,1024]{1,0:T(8,128)S(1)}, f32[32,1024]{1,0:T(8,128)S(1)}, u32[]{:S(2)}, u32[]{:S(2)}) collective-permute-start(f32[32,1024]{1,0:T(8,128)S(1)} %get-tuple-element.124), channel_id=1, source_target_pairs={{0,1},{1,2},{2,3},{3,0},{4,5},{5,6},{6,7},{7,4},{8,9},{9,10},{10,1... | collective-permute-start | bytes 393224 | tf_op jit(solution)/shard_map/ppermute | solution.py:38
  8.4 19.3 %collective-permute-start.6 = (s16[64,1024]{1,0:T(8,128)(2,1)S(1)}, s16[64,1024]{1,0:T(8,128)(2,1)S(1)}, u32[]{:S(2)}, u32[]{:S(2)}) collective-permute-start(s16[64,1024]{1,0:T(8,128)(2,1)S(1)} %get-tuple-element.58), channel_id=1, source_target_pairs={{0,1},{1,2},{2,3},{3,0},{4,5},{5,6},{6,7},{7,4},{8,9},{9,10},{10,1... | collective-permute-start | bytes 393224 | tf_op jit(solution)/shard_map/ppermute | solution.py:38
  10.9 20.8 %collective-permute-start.7 = (s16[64,1024]{1,0:T(8,128)(2,1)S(1)}, s16[64,1024]{1,0:T(8,128)(2,1)S(1)}, u32[]{:S(2)}, u32[]{:S(2)}) collective-permute-start(s16[64,1024]{1,0:T(8,128)(2,1)S(1)} %get-tuple-element.59), channel_id=1, source_target_pairs={{0,2},{1,3},{2,0},{3,1},{4,6},{5,7},{6,4},{7,5},{8,10},{9,11},{10,... | collective-permute-start | bytes 393224 | tf_op jit(solution)/shard_map/ppermute | solution.py:38
  11.8 20.0 %collective-permute-start.8 = (s16[64,1024]{1,0:T(8,128)(2,1)S(1)}, s16[64,1024]{1,0:T(8,128)(2,1)S(1)}, u32[]{:S(2)}, u32[]{:S(2)}) collective-permute-start(s16[64,1024]{1,0:T(8,128)(2,1)S(1)} %get-tuple-element.60), channel_id=1, source_target_pairs={{0,3},{1,0},{2,1},{3,2},{4,7},{5,4},{6,5},{7,6},{8,11},{9,8},{10,9... | collective-permute-start | bytes 393224 | tf_op jit(solution)/shard_map/ppermute | solution.py:38
  25.0 14.2 %collective-permute-start.4 = (f32[32,1024]{1,0:T(8,128)}, f32[32,1024]{1,0:T(8,128)S(1)}, u32[]{:S(2)}, u32[]{:S(2)}) collective-permute-start(f32[32,1024]{1,0:T(8,128)} %get-tuple-element.56), channel_id=1, source_target_pairs={{0,2},{1,3},{2,0},{3,1},{4,6},{5,7},{6,4},{7,5},{8,10},{9,11},{10,... | collective-permute-start | bytes 393224 | tf_op jit(solution)/shard_map/ppermute | solution.py:38
  27.7 11.5 %collective-permute-start.5 = (f32[32,1024]{1,0:T(8,128)S(1)}, f32[32,1024]{1,0:T(8,128)S(1)}, u32[]{:S(2)}, u32[]{:S(2)}) collective-permute-start(f32[32,1024]{1,0:T(8,128)S(1)} %get-tuple-element.57), channel_id=1, source_target_pairs={{0,1},{1,2},{2,3},{3,0},{4,5},{5,6},{6,7},{7,4},{8,9},{9,10},{10,1... | collective-permute-start | bytes 393224 | tf_op jit(solution)/shard_map/ppermute | solution.py:38
  39.5 11.0 %collective-permute-start.11 = (s16[32,1024]{1,0:T(8,128)(2,1)S(1)}, s16[32,1024]{1,0:T(8,128)(2,1)S(1)}, u32[]{:S(2)}, u32[]{:S(2)}) collective-permute-start(s16[32,1024]{1,0:T(8,128)(2,1)S(1)} %get-tuple-element.62.refs_0_.refs_2_), channel_id=1, source_target_pairs={{0,3},{1,0},{2,1},{3,2},{4,7},{5,4},{6,5},{7,6},{8,11},{9,8},{10,9... | collective-permute-start | bytes 196616 | tf_op jit(solution)/shard_map/ppermute | solution.py:38
  41.6 8.9 %collective-permute-start.10 = (s16[32,1024]{1,0:T(8,128)(2,1)S(1)}, s16[32,1024]{1,0:T(8,128)(2,1)S(1)}, u32[]{:S(2)}, u32[]{:S(2)}) collective-permute-start(s16[32,1024]{1,0:T(8,128)(2,1)S(1)} %get-tuple-element.62.refs_0_.refs_2_), channel_id=1, source_target_pairs={{0,2},{1,3},{2,0},{3,1},{4,6},{5,7},{6,4},{7,5},{8,10},{9,11},{10,... | collective-permute-start | bytes 196616 | tf_op jit(solution)/shard_map/ppermute | solution.py:38
  42.2 8.3 %collective-permute-start.9 = (s16[32,1024]{1,0:T(8,128)(2,1)S(1)}, s16[32,1024]{1,0:T(8,128)(2,1)S(1)}, u32[]{:S(2)}, u32[]{:S(2)}) collective-permute-start(s16[32,1024]{1,0:T(8,128)(2,1)S(1)} %get-tuple-element.62.refs_0_.refs_2_), channel_id=1, source_target_pairs={{0,1},{1,2},{2,3},{3,0},{4,5},{5,6},{6,7},{7,4},{8,9},{9,10},{10,1... | collective-permute-start | bytes 196616 | tf_op jit(solution)/shard_map/ppermute | solution.py:38
  47.6 10.3 %collective-permute-start.15 = (s16[64,1024]{1,0:T(8,128)(2,1)S(1)}, s16[64,1024]{1,0:T(8,128)(2,1)S(1)}, u32[]{:S(2)}, u32[]{:S(2)}) collective-permute-start(s16[64,1024]{1,0:T(8,128)(2,1)S(1)} %get-tuple-element.67), channel_id=1, source_target_pairs={{8,9},{9,10},{10,11},{11,8},{12,13},{13,14},{14,15},{15,12},{24,25... | collective-permute-start | bytes 393224 | tf_op jit(solution)/shard_map/ppermute | solution.py:38
  50.5 15.0 %collective-permute-start.14 = (s16[128,1024]{1,0:T(8,128)(2,1)S(1)}, s16[128,1024]{1,0:T(8,128)(2,1)S(1)}, u32[]{:S(2)}, u32[]{:S(2)}) collective-permute-start(s16[128,1024]{1,0:T(8,128)(2,1)S(1)} %shard_map.192), channel_id=1, source_target_pairs={{0,12},{1,13},{2,14},{3,15},{16,28},{17,29},{18,30},{19,31}} | collective-permute-start | bytes 786440 | tf_op jit(solution)/shard_map/ppermute | solution.py:25
  51.2 14.3 %collective-permute-start.13 = (s16[128,1024]{1,0:T(8,128)(2,1)S(1)}, s16[128,1024]{1,0:T(8,128)(2,1)}, u32[]{:S(2)}, u32[]{:S(2)}) collective-permute-start(s16[128,1024]{1,0:T(8,128)(2,1)S(1)} %shard_map.192), channel_id=1, source_target_pairs={{0,8},{4,12},{1,9},{5,13},{2,10},{6,14},{3,11},{7,15},{16,24},{20,... | collective-permute-start | bytes 786440 | tf_op jit(solution)/shard_map/ppermute | solution.py:25
  52.5 13.0 %collective-permute-start.12 = (s16[128,1024]{1,0:T(8,128)(2,1)S(1)}, s16[128,1024]{1,0:T(8,128)(2,1)}, u32[]{:S(2)}, u32[]{:S(2)}) collective-permute-start(s16[128,1024]{1,0:T(8,128)(2,1)S(1)} %shard_map.192), channel_id=1, source_target_pairs={{0,4},{4,8},{8,12},{1,5},{5,9},{9,13},{2,6},{6,10},{10,14},{3,7},{... | collective-permute-start | bytes 786440 | tf_op jit(solution)/shard_map/ppermute | solution.py:25
  54.4 10.2 %collective-permute-start.16 = (s16[64,1024]{1,0:T(8,128)(2,1)S(1)}, s16[64,1024]{1,0:T(8,128)(2,1)S(1)}, u32[]{:S(2)}, u32[]{:S(2)}) collective-permute-start(s16[64,1024]{1,0:T(8,128)(2,1)S(1)} %get-tuple-element.68), channel_id=1, source_target_pairs={{8,10},{9,11},{10,8},{11,9},{12,14},{13,15},{14,12},{15,13},{24,26... | collective-permute-start | bytes 393224 | tf_op jit(solution)/shard_map/ppermute | solution.py:38
  57.9 7.6 %collective-permute-start.17 = (s16[64,1024]{1,0:T(8,128)(2,1)S(1)}, s16[64,1024]{1,0:T(8,128)(2,1)}, u32[]{:S(2)}, u32[]{:S(2)}) collective-permute-start(s16[64,1024]{1,0:T(8,128)(2,1)S(1)} %get-tuple-element.69), channel_id=1, source_target_pairs={{8,11},{9,8},{10,9},{11,10},{12,15},{13,12},{14,13},{15,14},{24,27... | collective-permute-start | bytes 393224 | tf_op jit(solution)/shard_map/ppermute | solution.py:38
  81.0 8.9 %collective-permute-start.18 = (s16[128,1024]{1,0:T(8,128)(2,1)}, s16[128,1024]{1,0:T(8,128)(2,1)S(1)}, u32[]{:S(2)}, u32[]{:S(2)}) collective-permute-start(s16[128,1024]{1,0:T(8,128)(2,1)} %get-tuple-element.71), channel_id=1, source_target_pairs={{4,0},{8,4},{12,8},{5,1},{9,5},{13,9},{6,2},{10,6},{14,10},{7,3},{... | collective-permute-start | bytes 786440 | tf_op jit(solution)/shard_map/ppermute | solution.py:25
  83.0 11.5 %collective-permute-start.19 = (s16[128,1024]{1,0:T(8,128)(2,1)}, s16[128,1024]{1,0:T(8,128)(2,1)S(1)}, u32[]{:S(2)}, u32[]{:S(2)}) collective-permute-start(s16[128,1024]{1,0:T(8,128)(2,1)} %get-tuple-element.72), channel_id=1, source_target_pairs={{8,0},{12,4},{9,1},{13,5},{10,2},{14,6},{11,3},{15,7},{24,16},{28,... | collective-permute-start | bytes 786440 | tf_op jit(solution)/shard_map/ppermute | solution.py:25
  84.3 10.2 %collective-permute-start.20 = (s16[128,1024]{1,0:T(8,128)(2,1)}, s16[128,1024]{1,0:T(8,128)(2,1)S(1)}, u32[]{:S(2)}, u32[]{:S(2)}) collective-permute-start(s16[128,1024]{1,0:T(8,128)(2,1)} %get-tuple-element.73), channel_id=1, source_target_pairs={{12,0},{13,1},{14,2},{15,3},{28,16},{29,17},{30,18},{31,19}} | collective-permute-start | bytes 786440 | tf_op jit(solution)/shard_map/ppermute | solution.py:25
  85.0 14.6 %collective-permute-start.24 = (s16[64,1024]{1,0:T(8,128)(2,1)}, s16[64,1024]{1,0:T(8,128)(2,1)S(1)}, u32[]{:S(2)}, u32[]{:S(2)}) collective-permute-start(s16[64,1024]{1,0:T(8,128)(2,1)} %get-tuple-element.79), channel_id=1, source_target_pairs={{0,3},{1,0},{2,1},{3,2},{4,7},{5,4},{6,5},{7,6},{8,11},{9,8},{10,9... | collective-permute-start | bytes 393224 | tf_op jit(solution)/shard_map/ppermute | solution.py:38
  88.6 12.9 %collective-permute-start.25 = (s16[64,1024]{1,0:T(8,128)(2,1)}, s16[64,1024]{1,0:T(8,128)(2,1)S(1)}, u32[]{:S(2)}, u32[]{:S(2)}) collective-permute-start(s16[64,1024]{1,0:T(8,128)(2,1)} %get-tuple-element.80), channel_id=1, source_target_pairs={{0,2},{1,3},{2,0},{3,1},{4,6},{5,7},{6,4},{7,5},{8,10},{9,11},{10,... | collective-permute-start | bytes 393224 | tf_op jit(solution)/shard_map/ppermute | solution.py:38
  89.9 16.0 %collective-permute-start.26 = (s16[64,1024]{1,0:T(8,128)(2,1)}, s16[64,1024]{1,0:T(8,128)(2,1)S(1)}, u32[]{:S(2)}, u32[]{:S(2)}) collective-permute-start(s16[64,1024]{1,0:T(8,128)(2,1)} %get-tuple-element.81), channel_id=1, source_target_pairs={{0,1},{1,2},{2,3},{3,0},{4,5},{5,6},{6,7},{7,4},{8,9},{9,10},{10,1... | collective-permute-start | bytes 393224 | tf_op jit(solution)/shard_map/ppermute | solution.py:38
  96.0 13.0 %collective-permute-start.21 = (s16[32,1024]{1,0:T(8,128)(2,1)S(1)}, s16[32,1024]{1,0:T(8,128)(2,1)S(1)}, u32[]{:S(2)}, u32[]{:S(2)}) collective-permute-start(s16[32,1024]{1,0:T(8,128)(2,1)S(1)} %get-tuple-element.75), channel_id=1, source_target_pairs={{0,3},{1,0},{2,1},{3,2},{4,7},{5,4},{6,5},{7,6},{8,11},{9,8},{10,9... | collective-permute-start | bytes 196616 | tf_op jit(solution)/shard_map/ppermute | solution.py:38
  99.6 9.4 %collective-permute-start.22 = (s16[32,1024]{1,0:T(8,128)(2,1)S(1)}, s16[32,1024]{1,0:T(8,128)(2,1)S(1)}, u32[]{:S(2)}, u32[]{:S(2)}) collective-permute-start(s16[32,1024]{1,0:T(8,128)(2,1)S(1)} %get-tuple-element.76), channel_id=1, source_target_pairs={{0,2},{1,3},{2,0},{3,1},{4,6},{5,7},{6,4},{7,5},{8,10},{9,11},{10,... | collective-permute-start | bytes 196616 | tf_op jit(solution)/shard_map/ppermute | solution.py:38
  99.6 9.4 %collective-permute-start.23 = (s16[32,1024]{1,0:T(8,128)(2,1)S(1)}, s16[32,1024]{1,0:T(8,128)(2,1)S(1)}, u32[]{:S(2)}, u32[]{:S(2)}) collective-permute-start(s16[32,1024]{1,0:T(8,128)(2,1)S(1)} %get-tuple-element.77), channel_id=1, source_target_pairs={{0,1},{1,2},{2,3},{3,0},{4,5},{5,6},{6,7},{7,4},{8,9},{9,10},{10,1... | collective-permute-start | bytes 196616 | tf_op jit(solution)/shard_map/ppermute | solution.py:38
  101.6 27.3 %collective-permute-start.33 = (s16[64,1024]{1,0:T(8,128)(2,1)}, s16[64,1024]{1,0:T(8,128)(2,1)S(1)}, u32[]{:S(2)}, u32[]{:S(2)}) collective-permute-start(s16[64,1024]{1,0:T(8,128)(2,1)} %get-tuple-element.92), channel_id=1, source_target_pairs={{8,11},{9,8},{10,9},{11,10},{12,15},{13,12},{14,13},{15,14},{24,27... | collective-permute-start | bytes 393224 | tf_op jit(solution)/shard_map/ppermute | solution.py:38
  106.0 24.7 %collective-permute-start.34 = (s16[64,1024]{1,0:T(8,128)(2,1)}, s16[64,1024]{1,0:T(8,128)(2,1)S(1)}, u32[]{:S(2)}, u32[]{:S(2)}) collective-permute-start(s16[64,1024]{1,0:T(8,128)(2,1)} %get-tuple-element.93), channel_id=1, source_target_pairs={{8,10},{9,11},{10,8},{11,9},{12,14},{13,15},{14,12},{15,13},{24,26... | collective-permute-start | bytes 393224 | tf_op jit(solution)/shard_map/ppermute | solution.py:38
  109.3 10.1 %collective-permute-start.29 = (s16[32,1024]{1,0:T(8,128)(2,1)S(1)}, s16[32,1024]{1,0:T(8,128)(2,1)S(1)}, u32[]{:S(2)}, u32[]{:S(2)}) collective-permute-start(s16[32,1024]{1,0:T(8,128)(2,1)S(1)} %get-tuple-element.82.refs_6_.refs_1_), channel_id=1, source_target_pairs={{0,3},{1,0},{2,1},{3,2},{4,7},{5,4},{6,5},{7,6},{8,11},{9,8},{10,9... | collective-permute-start | bytes 196616 | tf_op jit(solution)/shard_map/ppermute | solution.py:38
  110.3 13.2 %collective-permute-start.28 = (s16[32,1024]{1,0:T(8,128)(2,1)S(1)}, s16[32,1024]{1,0:T(8,128)(2,1)S(1)}, u32[]{:S(2)}, u32[]{:S(2)}) collective-permute-start(s16[32,1024]{1,0:T(8,128)(2,1)S(1)} %get-tuple-element.82.refs_6_.refs_1_), channel_id=1, source_target_pairs={{0,2},{1,3},{2,0},{3,1},{4,6},{5,7},{6,4},{7,5},{8,10},{9,11},{10,... | collective-permute-start | bytes 196616 | tf_op jit(solution)/shard_map/ppermute | solution.py:38
  111.2 12.2 %collective-permute-start.27 = (s16[32,1024]{1,0:T(8,128)(2,1)S(1)}, s16[32,1024]{1,0:T(8,128)(2,1)S(1)}, u32[]{:S(2)}, u32[]{:S(2)}) collective-permute-start(s16[32,1024]{1,0:T(8,128)(2,1)S(1)} %get-tuple-element.82.refs_6_.refs_1_), channel_id=1, source_target_pairs={{0,1},{1,2},{2,3},{3,0},{4,5},{5,6},{6,7},{7,4},{8,9},{9,10},{10,1... | collective-permute-start | bytes 196616 | tf_op jit(solution)/shard_map/ppermute | solution.py:38
  119.4 11.2 %collective-permute-start.35 = (s16[64,1024]{1,0:T(8,128)(2,1)S(1)}, s16[64,1024]{1,0:T(8,128)(2,1)S(1)}, u32[]{:S(2)}, u32[]{:S(2)}) collective-permute-start(s16[64,1024]{1,0:T(8,128)(2,1)S(1)} %copy-done.28), channel_id=1, source_target_pairs={{8,9},{9,10},{10,11},{11,8},{12,13},{13,14},{14,15},{15,12},{24,25... | collective-permute-start | bytes 393224 | tf_op jit(solution)/shard_map/ppermute | solution.py:38
  (35 other events, 393.3 us)

commit v5 on v4

--- a/solution.py
+++ b/solution.py
@@ -564,7 +564,14 @@
         )
     dec_new, dec_mom = dec_done
     enc_arrived = [rotated(grad_enc_cols[j], -j) for j in range(count)]
-    enc_new, enc_mom = adam_call(me, 0, 1, enc_arrived, enc_local[None], enc_moments)
+    enc_new, enc_mom = call(
+        functools.partial(adam_kernel, count),
+        [
+            jax.ShapeDtypeStruct((1, *enc_local.shape), enc_local.dtype),
+            jax.ShapeDtypeStruct(enc_moments.shape, enc_moments.dtype),
+        ],
+        [me, *enc_arrived, enc_local[None], enc_moments],
+    )
     encb_new, encb_mom = adam_update(encb_local, enc_bias_moments[:, 0], grad_enc_bias[:, 0])
     decb_new, decb_mom = adam_update(decb_local, dec_bias_moments[:, 0], grad_dec_bias[:, 0])
     return (

time: 138 us -> 138 us (level)
    pallas_call x10 -> x11, Pallas kernels: 22.6 us -> 24.4 us  [call(): pl.pallas_call(body, out_shape=(*far_out, *out_shape), in_specs=[pl.Block...]
    pallas_call x3 -> x2, Pallas kernels: 7.19 us -> 5.43 us  [adam_call(): pl.pallas_call(functools.partial(adam_kernel, count), grid=(stop - start,...]
where the time goes in v5:
time: 138 us; the launch traced here: 137 us
  starting transfers between devices  64.8 us (47%)
  Pallas kernels  29.8 us (22%)
  waiting for transfers between devices  25.7 us (19%)
  local copies, waits for them, and re-layouts  10.8 us (8%)
  other arithmetic  3.97 us (3%)
  between operations  1.88 us (1%)
    ppermute x30, starting transfers between devices, rotated(): return lax.ppermute(value, ('layer', 'feat'), pairs)  56.9 us
    pallas_call x11, Pallas kernels, call(): pl.pallas_call(body, out_shape=(*far_out, *out_shape), in_specs=[pl.Block...  24.4 us
    ppermute x30, waiting for transfers between devices, rotated(): return lax.ppermute(value, ('layer', 'feat'), pairs)  22.5 us
    unnamed x63, local copies, waits for them, and re-layouts  8.4 us
    ppermute x6, starting transfers between devices, shifted(): lax.ppermute(value, axis, [(source, source + steps) for source in range(i...  7.93 us
    pallas_call x2, Pallas kernels, adam_call(): pl.pallas_call(functools.partial(adam_kernel, count), grid=(stop - start,...  5.43 us
    ppermute x6, waiting for transfers between devices, shifted(): lax.ppermute(value, axis, [(source, source + steps) for source in range(i...  3.27 us
  transfers between devices with their start and end apart: 36, of which 7 were waited for; matrix products, arithmetic and copies ran while one was open for 4% of the time, Pallas kernels for 10%

profile of v5, /device:TPU:2, one launch (start us, length us, event | category | flops | bytes accessed | tf_op | source)
XLA Modules:
  0.0 137.0 jit_solution(17973528053326490018)
XLA Ops:
  1.8 3.7 %collective-permute-start.2 = (f32[32,1024]{1,0:T(8,128)S(1)}, f32[32,1024]{1,0:T(8,128)S(1)}, u32[]{:S(2)}, u32[]{:S(2)}) collective-permute-start(f32[32,1024]{1,0:T(8,128)S(1)} %get-tuple-element.122), channel_id=1, source_target_pairs={{0,3},{1,0},{2,1},{3,2},{4,7},{5,4},{6,5},{7,6},{8,11},{9,8},{10,9... | collective-permute-start | bytes 393224 | tf_op jit(solution)/shard_map/ppermute | solution.py:38
  8.4 2.5 %collective-permute-start.6 = (s16[64,1024]{1,0:T(8,128)(2,1)S(1)}, s16[64,1024]{1,0:T(8,128)(2,1)S(1)}, u32[]{:S(2)}, u32[]{:S(2)}) collective-permute-start(s16[64,1024]{1,0:T(8,128)(2,1)S(1)} %get-tuple-element.58), channel_id=1, source_target_pairs={{0,1},{1,2},{2,3},{3,0},{4,5},{5,6},{6,7},{7,4},{8,9},{9,10},{10,1... | collective-permute-start | bytes 393224 | tf_op jit(solution)/shard_map/ppermute | solution.py:38
  11.8 1.9 %collective-permute-start.8 = (s16[64,1024]{1,0:T(8,128)(2,1)S(1)}, s16[64,1024]{1,0:T(8,128)(2,1)S(1)}, u32[]{:S(2)}, u32[]{:S(2)}) collective-permute-start(s16[64,1024]{1,0:T(8,128)(2,1)S(1)} %get-tuple-element.60), channel_id=1, source_target_pairs={{0,3},{1,0},{2,1},{3,2},{4,7},{5,4},{6,5},{7,6},{8,11},{9,8},{10,9... | collective-permute-start | bytes 393224 | tf_op jit(solution)/shard_map/ppermute | solution.py:38
  13.7 9.4 %collective-permute-done.1.refs_2_ = f32[32,1024]{1,0:T(8,128)S(1)} collective-permute-done((f32[32,1024]{1,0:T(8,128)S(1)}, f32[32,1024]{1,0:T(8,128)S(1)}, u32[]{:S(2)}, u32[]{:S(2)}) %collective-permute-start.1) | collective-permute-done | bytes 131104 | tf_op jit(solution)/shard_map/ppermute | solution.py:38
  23.1 1.9 %shard_map.188 = (f32[32,1024]{1,0:T(8,128)S(1)}, f32[32,1024]{1,0:T(8,128)}, f32[32,1024]{1,0:T(8,128)}, f32[32,1024]{1,0:T(8,128)S(1)}) custom-call(f32[32,1024]{1,0:T(8,128)S(1)} %get-tuple-element.125.refs_0_, f32[32,1024]{1,0:T(8,128)S(1)} %collective-permute-done.refs_1_, f32[32,1024]{1,0:T(8,128)S(1)} %collective-permute-done.1.refs_2_, ...), custom_call_target="tpu_custom_call" | custom-call | flops 805306368 | bytes 3145728 | tf_op jit(solution)/shard_map/pallas_call | solution.py:134
  25.0 2.7 %collective-permute-start.4 = (f32[32,1024]{1,0:T(8,128)}, f32[32,1024]{1,0:T(8,128)S(1)}, u32[]{:S(2)}, u32[]{:S(2)}) collective-permute-start(f32[32,1024]{1,0:T(8,128)} %get-tuple-element.56), channel_id=1, source_target_pairs={{0,2},{1,3},{2,0},{3,1},{4,6},{5,7},{6,4},{7,5},{8,10},{9,11},{10,... | collective-permute-start | bytes 393224 | tf_op jit(solution)/shard_map/ppermute | solution.py:38
  27.7 2.9 %collective-permute-start.5 = (f32[32,1024]{1,0:T(8,128)S(1)}, f32[32,1024]{1,0:T(8,128)S(1)}, u32[]{:S(2)}, u32[]{:S(2)}) collective-permute-start(f32[32,1024]{1,0:T(8,128)S(1)} %get-tuple-element.57), channel_id=1, source_target_pairs={{0,1},{1,2},{2,3},{3,0},{4,5},{5,6},{6,7},{7,4},{8,9},{9,10},{10,1... | collective-permute-start | bytes 393224 | tf_op jit(solution)/shard_map/ppermute | solution.py:38
  31.8 7.4 %collective-permute-done.4.refs_2_ = f32[32,1024]{1,0:T(8,128)S(1)} collective-permute-done((f32[32,1024]{1,0:T(8,128)}, f32[32,1024]{1,0:T(8,128)S(1)}, u32[]{:S(2)}, u32[]{:S(2)}) %collective-permute-start.4) | collective-permute-done | bytes 131104 | tf_op jit(solution)/shard_map/ppermute | solution.py:38
  39.5 2.1 %collective-permute-start.11 = (s16[32,1024]{1,0:T(8,128)(2,1)S(1)}, s16[32,1024]{1,0:T(8,128)(2,1)S(1)}, u32[]{:S(2)}, u32[]{:S(2)}) collective-permute-start(s16[32,1024]{1,0:T(8,128)(2,1)S(1)} %get-tuple-element.62.refs_0_.refs_2_), channel_id=1, source_target_pairs={{0,3},{1,0},{2,1},{3,2},{4,7},{5,4},{6,5},{7,6},{8,11},{9,8},{10,9... | collective-permute-start | bytes 196616 | tf_op jit(solution)/shard_map/ppermute | solution.py:38
  42.2 1.9 %collective-permute-start.9 = (s16[32,1024]{1,0:T(8,128)(2,1)S(1)}, s16[32,1024]{1,0:T(8,128)(2,1)S(1)}, u32[]{:S(2)}, u32[]{:S(2)}) collective-permute-start(s16[32,1024]{1,0:T(8,128)(2,1)S(1)} %get-tuple-element.62.refs_0_.refs_2_), channel_id=1, source_target_pairs={{0,1},{1,2},{2,3},{3,0},{4,5},{5,6},{6,7},{7,4},{8,9},{9,10},{10,1... | collective-permute-start | bytes 196616 | tf_op jit(solution)/shard_map/ppermute | solution.py:38
  44.2 2.4 %shard_map.191 = (bf16[256,1024]{1,0:T(8,128)(2,1)}, bf16[256,1024]{1,0:T(8,128)(2,1)}) custom-call(s16[64,1024]{1,0:T(8,128)(2,1)} %copy-done.17, s16[64,1024]{1,0:T(8,128)(2,1)} %copy-done.10, s16[64,1024]{1,0:T(8,128)(2,1)} %copy-done.11, s16[64,1024]{1,0:T(8,128)(2,1)} %copy-done.12), custom_call_target="tpu_custom_call" | custom-call | bytes 1572864 | tf_op jit(solution)/shard_map/pallas_call | solution.py:134
  47.6 2.8 %collective-permute-start.15 = (s16[64,1024]{1,0:T(8,128)(2,1)S(1)}, s16[64,1024]{1,0:T(8,128)(2,1)S(1)}, u32[]{:S(2)}, u32[]{:S(2)}) collective-permute-start(s16[64,1024]{1,0:T(8,128)(2,1)S(1)} %get-tuple-element.67), channel_id=1, source_target_pairs={{8,9},{9,10},{10,11},{11,8},{12,13},{13,14},{14,15},{15,12},{24,25... | collective-permute-start | bytes 393224 | tf_op jit(solution)/shard_map/ppermute | solution.py:38
  52.5 1.9 %collective-permute-start.12 = (s16[128,1024]{1,0:T(8,128)(2,1)S(1)}, s16[128,1024]{1,0:T(8,128)(2,1)}, u32[]{:S(2)}, u32[]{:S(2)}) collective-permute-start(s16[128,1024]{1,0:T(8,128)(2,1)S(1)} %shard_map.192), channel_id=1, source_target_pairs={{0,4},{4,8},{8,12},{1,5},{5,9},{9,13},{2,6},{6,10},{10,14},{3,7},{... | collective-permute-start | bytes 786440 | tf_op jit(solution)/shard_map/ppermute | solution.py:25
  54.4 3.4 %collective-permute-start.16 = (s16[64,1024]{1,0:T(8,128)(2,1)S(1)}, s16[64,1024]{1,0:T(8,128)(2,1)S(1)}, u32[]{:S(2)}, u32[]{:S(2)}) collective-permute-start(s16[64,1024]{1,0:T(8,128)(2,1)S(1)} %get-tuple-element.68), channel_id=1, source_target_pairs={{8,10},{9,11},{10,8},{11,9},{12,14},{13,15},{14,12},{15,13},{24,26... | collective-permute-start | bytes 393224 | tf_op jit(solution)/shard_map/ppermute | solution.py:38
  57.9 3.5 %collective-permute-start.17 = (s16[64,1024]{1,0:T(8,128)(2,1)S(1)}, s16[64,1024]{1,0:T(8,128)(2,1)}, u32[]{:S(2)}, u32[]{:S(2)}) collective-permute-start(s16[64,1024]{1,0:T(8,128)(2,1)S(1)} %get-tuple-element.69), channel_id=1, source_target_pairs={{8,11},{9,8},{10,9},{11,10},{12,15},{13,12},{14,13},{15,14},{24,27... | collective-permute-start | bytes 393224 | tf_op jit(solution)/shard_map/ppermute | solution.py:38
  62.4 2.3 %collective-permute-done.16.refs_11_ = s16[64,1024]{1,0:T(8,128)(2,1)S(1)} collective-permute-done((s16[64,1024]{1,0:T(8,128)(2,1)S(1)}, s16[64,1024]{1,0:T(8,128)(2,1)S(1)}, u32[]{:S(2)}, u32[]{:S(2)}) %collective-permute-start.16) | collective-permute-done | bytes 131104 | tf_op jit(solution)/shard_map/ppermute | solution.py:38
  66.2 14.7 %shard_map.194 = (f32[128,1024]{1,0:T(8,128)}, s16[128,1024]{1,0:T(8,128)(2,1)}, s16[128,1024]{1,0:T(8,128)(2,1)}, s16[128,1024]{1,0:T(8,128)(2,1)}, s16[64,1024...) custom-call(s16[32,1024]{1,0:T(8,128)(2,1)} %copy-done.14, ...), custom_call_target="tpu_custom_call" | custom-call | flops 9663676416 | bytes 7086080 | tf_op jit(solution)/shard_map/pallas_call | solution.py:134
  81.0 2.1 %collective-permute-start.18 = (s16[128,1024]{1,0:T(8,128)(2,1)}, s16[128,1024]{1,0:T(8,128)(2,1)S(1)}, u32[]{:S(2)}, u32[]{:S(2)}) collective-permute-start(s16[128,1024]{1,0:T(8,128)(2,1)} %get-tuple-element.71), channel_id=1, source_target_pairs={{4,0},{8,4},{12,8},{5,1},{9,5},{13,9},{6,2},{10,6},{14,10},{7,3},{... | collective-permute-start | bytes 786440 | tf_op jit(solution)/shard_map/ppermute | solution.py:25
  85.0 3.6 %collective-permute-start.24 = (s16[64,1024]{1,0:T(8,128)(2,1)}, s16[64,1024]{1,0:T(8,128)(2,1)S(1)}, u32[]{:S(2)}, u32[]{:S(2)}) collective-permute-start(s16[64,1024]{1,0:T(8,128)(2,1)} %get-tuple-element.79), channel_id=1, source_target_pairs={{0,3},{1,0},{2,1},{3,2},{4,7},{5,4},{6,5},{7,6},{8,11},{9,8},{10,9... | collective-permute-start | bytes 393224 | tf_op jit(solution)/shard_map/ppermute | solution.py:38
  91.2 3.3 %collective-permute-done.19.refs_3_ = s16[128,1024]{1,0:T(8,128)(2,1)S(1)} collective-permute-done((s16[128,1024]{1,0:T(8,128)(2,1)}, s16[128,1024]{1,0:T(8,128)(2,1)S(1)}, u32[]{:S(2)}, u32[]{:S(2)}) %collective-permute-start.19) | collective-permute-done | bytes 262176 | tf_op jit(solution)/shard_map/ppermute | solution.py:25
  96.0 3.6 %collective-permute-start.21 = (s16[32,1024]{1,0:T(8,128)(2,1)S(1)}, s16[32,1024]{1,0:T(8,128)(2,1)S(1)}, u32[]{:S(2)}, u32[]{:S(2)}) collective-permute-start(s16[32,1024]{1,0:T(8,128)(2,1)S(1)} %get-tuple-element.75), channel_id=1, source_target_pairs={{0,3},{1,0},{2,1},{3,2},{4,7},{5,4},{6,5},{7,6},{8,11},{9,8},{10,9... | collective-permute-start | bytes 196616 | tf_op jit(solution)/shard_map/ppermute | solution.py:38
  101.6 4.4 %collective-permute-start.33 = (s16[64,1024]{1,0:T(8,128)(2,1)}, s16[64,1024]{1,0:T(8,128)(2,1)S(1)}, u32[]{:S(2)}, u32[]{:S(2)}) collective-permute-start(s16[64,1024]{1,0:T(8,128)(2,1)} %get-tuple-element.92), channel_id=1, source_target_pairs={{8,11},{9,8},{10,9},{11,10},{12,15},{13,12},{14,13},{15,14},{24,27... | collective-permute-start | bytes 393224 | tf_op jit(solution)/shard_map/ppermute | solution.py:38
  106.0 3.0 %collective-permute-start.34 = (s16[64,1024]{1,0:T(8,128)(2,1)}, s16[64,1024]{1,0:T(8,128)(2,1)S(1)}, u32[]{:S(2)}, u32[]{:S(2)}) collective-permute-start(s16[64,1024]{1,0:T(8,128)(2,1)} %get-tuple-element.93), channel_id=1, source_target_pairs={{8,10},{9,11},{10,8},{11,9},{12,14},{13,15},{14,12},{15,13},{24,26... | collective-permute-start | bytes 393224 | tf_op jit(solution)/shard_map/ppermute | solution.py:38
  111.2 1.9 %collective-permute-start.27 = (s16[32,1024]{1,0:T(8,128)(2,1)S(1)}, s16[32,1024]{1,0:T(8,128)(2,1)S(1)}, u32[]{:S(2)}, u32[]{:S(2)}) collective-permute-start(s16[32,1024]{1,0:T(8,128)(2,1)S(1)} %get-tuple-element.82.refs_6_.refs_1_), channel_id=1, source_target_pairs={{0,1},{1,2},{2,3},{3,0},{4,5},{5,6},{6,7},{7,4},{8,9},{9,10},{10,1... | collective-permute-start | bytes 196616 | tf_op jit(solution)/shard_map/ppermute | solution.py:38
  114.5 2.2 %copy-done.2 = f32[2,1,4,32,4096]{4,3,2,1,0:T(8,128)S(1)} copy-done((f32[2,1,4,32,4096]{4,3,2,1,0:T(8,128)S(1)}, f32[2,1,4,32,4096]{4,3,2,1,0:T(8,128)}, u32[]{:S(2)}) %copy-start.2) | copy-done | bytes 4194328
  116.7 2.7 %shard_map.197 = (f32[4,32,4096]{2,1,0:T(8,128)}, f32[2,4,32,4096]{3,2,1,0:T(8,128)}) custom-call(s32[1]{0:T(128)} %bitcast.refs_0_.me_ref, s16[64,1024]{1,0:T(8,128)(2,1)S(1)} %copy-done.16, s16[64,1024]{1,0:T(8,128)(2,1)S(1)} %collective-permute-done.24.refs_5_.refs_1_, s16[64,1024]{1,0:T(8,128)(2,1)S(1)} %collective-permute-done.25.refs_6_.refs_2_, ...), custom_call_target="tpu_custom_call" | custom-call | flops 5242880 | bytes 6815744 | tf_op jit(solution)/shard_map/pallas_call | solution.py:215
  119.4 4.0 %collective-permute-start.35 = (s16[64,1024]{1,0:T(8,128)(2,1)S(1)}, s16[64,1024]{1,0:T(8,128)(2,1)S(1)}, u32[]{:S(2)}, u32[]{:S(2)}) collective-permute-start(s16[64,1024]{1,0:T(8,128)(2,1)S(1)} %copy-done.28), channel_id=1, source_target_pairs={{8,9},{9,10},{10,11},{11,8},{12,13},{13,14},{14,15},{15,12},{24,25... | collective-permute-start | bytes 393224 | tf_op jit(solution)/shard_map/ppermute | solution.py:38
  125.1 2.0 %shard_map.198 = (s16[32,1024]{1,0:T(8,128)(2,1)S(1)}, s16[32,1024]{1,0:T(8,128)(2,1)S(1)}, s16[32,1024]{1,0:T(8,128)(2,1)S(1)}, s16[32,1024]{1,0:T(8,128)(2,1)S(1)}) custom-call(bf16[1024,1024]{1,0:T(8,128)(2,1)S(1)} %bitcast.57, s16[32,1024]{1,0:T(8,128)(2,1)S(1)} %get-tuple-element.82.refs_6_.refs_1_, ...), custom_call_target="tpu_custom_call" | custom-call | flops 536870912 | bytes 2621440 | tf_op jit(solution)/shard_map/pallas_call | solution.py:134
  127.1 1.7 %collective-permute-start.30 = (s16[32,1024]{1,0:T(8,128)(2,1)S(1)}, s16[32,1024]{1,0:T(8,128)(2,1)S(1)}, u32[]{:S(2)}, u32[]{:S(2)}) collective-permute-start(s16[32,1024]{1,0:T(8,128)(2,1)S(1)} %get-tuple-element.86), channel_id=1, source_target_pairs={{0,3},{1,0},{2,1},{3,2},{4,7},{5,4},{6,5},{7,6},{8,11},{9,8},{10,9... | collective-permute-start | bytes 196616 | tf_op jit(solution)/shard_map/ppermute | solution.py:38
  130.7 2.7 %shard_map.200 = (f32[4,32,4096]{2,1,0:T(8,128)}, f32[2,4,32,4096]{3,2,1,0:T(8,128)}) custom-call(s32[1]{0:T(128)} %bitcast.refs_0_.me_ref, s16[64,1024]{1,0:T(8,128)(2,1)S(1)} %copy-done.15, s16[64,1024]{1,0:T(8,128)(2,1)S(1)} %collective-permute-done.33.refs_1_, ...), custom_call_target="tpu_custom_call", output_to_operand_aliasing={{0}: (7, {}), {1}: (8, {})} | custom-call | flops 5242880 | bytes 6815744 | tf_op jit(solution)/shard_map/pallas_call | solution.py:215
  133.4 1.9 %collective-permute-done.31.refs_3_ = s16[32,1024]{1,0:T(8,128)(2,1)S(1)} collective-permute-done((s16[32,1024]{1,0:T(8,128)(2,1)S(1)}, s16[32,1024]{1,0:T(8,128)(2,1)S(1)}, u32[]{:S(2)}, u32[]{:S(2)}) %collective-permute-start.31) | collective-permute-done | bytes 65568 | tf_op jit(solution)/shard_map/ppermute | solution.py:38
  135.3 1.8 %shard_map.199 = (f32[1,32,4096]{2,1,0:T(8,128)}, f32[2,1,32,4096]{3,2,1,0:T(8,128)}) custom-call(s32[1]{0:T(128)} %bitcast.refs_0_.me_ref, s16[32,1024]{1,0:T(8,128)(2,1)S(1)} %get-tuple-element.85.refs_1_.refs_8_, s16[32,1024]{1,0:T(8,128)(2,1)S(1)} %collective-permute-done.30.refs_2_, s16[32,1024]{1,0:T(8,128)(2,1)S(1)} %collective-permute-done.31.refs_3_, ...), custom_call_target="tpu_custom_call" | custom-call | bytes 3407876 | tf_op jit(solution)/shard_map/pallas_call | solution.py:134
  (129 shorter events, 26.8 us)
Async XLA Ops:
  1.8 10.0 %collective-permute-start.2 = (f32[32,1024]{1,0:T(8,128)S(1)}, f32[32,1024]{1,0:T(8,128)S(1)}, u32[]{:S(2)}, u32[]{:S(2)}) collective-permute-start(f32[32,1024]{1,0:T(8,128)S(1)} %get-tuple-element.122), channel_id=1, source_target_pairs={{0,3},{1,0},{2,1},{3,2},{4,7},{5,4},{6,5},{7,6},{8,11},{9,8},{10,9... | collective-permute-start | bytes 393224 | tf_op jit(solution)/shard_map/ppermute | solution.py:38
  5.5 17.6 %collective-permute-start.1 = (f32[32,1024]{1,0:T(8,128)S(1)}, f32[32,1024]{1,0:T(8,128)S(1)}, u32[]{:S(2)}, u32[]{:S(2)}) collective-permute-start(f32[32,1024]{1,0:T(8,128)S(1)} %get-tuple-element.123), channel_id=1, source_target_pairs={{0,2},{1,3},{2,0},{3,1},{4,6},{5,7},{6,4},{7,5},{8,10},{9,11},{10,... | collective-permute-start | bytes 393224 | tf_op jit(solution)/shard_map/ppermute | solution.py:38
  5.5 17.6 %collective-permute-start = (f32[32,1024]{1,0:T(8,128)S(1)}, f32[32,1024]{1,0:T(8,128)S(1)}, u32[]{:S(2)}, u32[]{:S(2)}) collective-permute-start(f32[32,1024]{1,0:T(8,128)S(1)} %get-tuple-element.124), channel_id=1, source_target_pairs={{0,1},{1,2},{2,3},{3,0},{4,5},{5,6},{6,7},{7,4},{8,9},{9,10},{10,1... | collective-permute-start | bytes 393224 | tf_op jit(solution)/shard_map/ppermute | solution.py:38
  8.4 19.3 %collective-permute-start.6 = (s16[64,1024]{1,0:T(8,128)(2,1)S(1)}, s16[64,1024]{1,0:T(8,128)(2,1)S(1)}, u32[]{:S(2)}, u32[]{:S(2)}) collective-permute-start(s16[64,1024]{1,0:T(8,128)(2,1)S(1)} %get-tuple-element.58), channel_id=1, source_target_pairs={{0,1},{1,2},{2,3},{3,0},{4,5},{5,6},{6,7},{7,4},{8,9},{9,10},{10,1... | collective-permute-start | bytes 393224 | tf_op jit(solution)/shard_map/ppermute | solution.py:38
  10.9 20.8 %collective-permute-start.7 = (s16[64,1024]{1,0:T(8,128)(2,1)S(1)}, s16[64,1024]{1,0:T(8,128)(2,1)S(1)}, u32[]{:S(2)}, u32[]{:S(2)}) collective-permute-start(s16[64,1024]{1,0:T(8,128)(2,1)S(1)} %get-tuple-element.59), channel_id=1, source_target_pairs={{0,2},{1,3},{2,0},{3,1},{4,6},{5,7},{6,4},{7,5},{8,10},{9,11},{10,... | collective-permute-start | bytes 393224 | tf_op jit(solution)/shard_map/ppermute | solution.py:38
  11.8 20.0 %collective-permute-start.8 = (s16[64,1024]{1,0:T(8,128)(2,1)S(1)}, s16[64,1024]{1,0:T(8,128)(2,1)S(1)}, u32[]{:S(2)}, u32[]{:S(2)}) collective-permute-start(s16[64,1024]{1,0:T(8,128)(2,1)S(1)} %get-tuple-element.60), channel_id=1, source_target_pairs={{0,3},{1,0},{2,1},{3,2},{4,7},{5,4},{6,5},{7,6},{8,11},{9,8},{10,9... | collective-permute-start | bytes 393224 | tf_op jit(solution)/shard_map/ppermute | solution.py:38
  25.0 14.2 %collective-permute-start.4 = (f32[32,1024]{1,0:T(8,128)}, f32[32,1024]{1,0:T(8,128)S(1)}, u32[]{:S(2)}, u32[]{:S(2)}) collective-permute-start(f32[32,1024]{1,0:T(8,128)} %get-tuple-element.56), channel_id=1, source_target_pairs={{0,2},{1,3},{2,0},{3,1},{4,6},{5,7},{6,4},{7,5},{8,10},{9,11},{10,... | collective-permute-start | bytes 393224 | tf_op jit(solution)/shard_map/ppermute | solution.py:38
  27.7 11.5 %collective-permute-start.5 = (f32[32,1024]{1,0:T(8,128)S(1)}, f32[32,1024]{1,0:T(8,128)S(1)}, u32[]{:S(2)}, u32[]{:S(2)}) collective-permute-start(f32[32,1024]{1,0:T(8,128)S(1)} %get-tuple-element.57), channel_id=1, source_target_pairs={{0,1},{1,2},{2,3},{3,0},{4,5},{5,6},{6,7},{7,4},{8,9},{9,10},{10,1... | collective-permute-start | bytes 393224 | tf_op jit(solution)/shard_map/ppermute | solution.py:38
  39.5 11.0 %collective-permute-start.11 = (s16[32,1024]{1,0:T(8,128)(2,1)S(1)}, s16[32,1024]{1,0:T(8,128)(2,1)S(1)}, u32[]{:S(2)}, u32[]{:S(2)}) collective-permute-start(s16[32,1024]{1,0:T(8,128)(2,1)S(1)} %get-tuple-element.62.refs_0_.refs_2_), channel_id=1, source_target_pairs={{0,3},{1,0},{2,1},{3,2},{4,7},{5,4},{6,5},{7,6},{8,11},{9,8},{10,9... | collective-permute-start | bytes 196616 | tf_op jit(solution)/shard_map/ppermute | solution.py:38
  41.6 8.9 %collective-permute-start.10 = (s16[32,1024]{1,0:T(8,128)(2,1)S(1)}, s16[32,1024]{1,0:T(8,128)(2,1)S(1)}, u32[]{:S(2)}, u32[]{:S(2)}) collective-permute-start(s16[32,1024]{1,0:T(8,128)(2,1)S(1)} %get-tuple-element.62.refs_0_.refs_2_), channel_id=1, source_target_pairs={{0,2},{1,3},{2,0},{3,1},{4,6},{5,7},{6,4},{7,5},{8,10},{9,11},{10,... | collective-permute-start | bytes 196616 | tf_op jit(solution)/shard_map/ppermute | solution.py:38
  42.2 8.3 %collective-permute-start.9 = (s16[32,1024]{1,0:T(8,128)(2,1)S(1)}, s16[32,1024]{1,0:T(8,128)(2,1)S(1)}, u32[]{:S(2)}, u32[]{:S(2)}) collective-permute-start(s16[32,1024]{1,0:T(8,128)(2,1)S(1)} %get-tuple-element.62.refs_0_.refs_2_), channel_id=1, source_target_pairs={{0,1},{1,2},{2,3},{3,0},{4,5},{5,6},{6,7},{7,4},{8,9},{9,10},{10,1... | collective-permute-start | bytes 196616 | tf_op jit(solution)/shard_map/ppermute | solution.py:38
  47.6 10.3 %collective-permute-start.15 = (s16[64,1024]{1,0:T(8,128)(2,1)S(1)}, s16[64,1024]{1,0:T(8,128)(2,1)S(1)}, u32[]{:S(2)}, u32[]{:S(2)}) collective-permute-start(s16[64,1024]{1,0:T(8,128)(2,1)S(1)} %get-tuple-element.67), channel_id=1, source_target_pairs={{8,9},{9,10},{10,11},{11,8},{12,13},{13,14},{14,15},{15,12},{24,25... | collective-permute-start | bytes 393224 | tf_op jit(solution)/shard_map/ppermute | solution.py:38
  50.5 15.0 %collective-permute-start.14 = (s16[128,1024]{1,0:T(8,128)(2,1)S(1)}, s16[128,1024]{1,0:T(8,128)(2,1)S(1)}, u32[]{:S(2)}, u32[]{:S(2)}) collective-permute-start(s16[128,1024]{1,0:T(8,128)(2,1)S(1)} %shard_map.192), channel_id=1, source_target_pairs={{0,12},{1,13},{2,14},{3,15},{16,28},{17,29},{18,30},{19,31}} | collective-permute-start | bytes 786440 | tf_op jit(solution)/shard_map/ppermute | solution.py:25
  51.2 14.3 %collective-permute-start.13 = (s16[128,1024]{1,0:T(8,128)(2,1)S(1)}, s16[128,1024]{1,0:T(8,128)(2,1)}, u32[]{:S(2)}, u32[]{:S(2)}) collective-permute-start(s16[128,1024]{1,0:T(8,128)(2,1)S(1)} %shard_map.192), channel_id=1, source_target_pairs={{0,8},{4,12},{1,9},{5,13},{2,10},{6,14},{3,11},{7,15},{16,24},{20,... | collective-permute-start | bytes 786440 | tf_op jit(solution)/shard_map/ppermute | solution.py:25
  52.5 13.0 %collective-permute-start.12 = (s16[128,1024]{1,0:T(8,128)(2,1)S(1)}, s16[128,1024]{1,0:T(8,128)(2,1)}, u32[]{:S(2)}, u32[]{:S(2)}) collective-permute-start(s16[128,1024]{1,0:T(8,128)(2,1)S(1)} %shard_map.192), channel_id=1, source_target_pairs={{0,4},{4,8},{8,12},{1,5},{5,9},{9,13},{2,6},{6,10},{10,14},{3,7},{... | collective-permute-start | bytes 786440 | tf_op jit(solution)/shard_map/ppermute | solution.py:25
  54.4 10.2 %collective-permute-start.16 = (s16[64,1024]{1,0:T(8,128)(2,1)S(1)}, s16[64,1024]{1,0:T(8,128)(2,1)S(1)}, u32[]{:S(2)}, u32[]{:S(2)}) collective-permute-start(s16[64,1024]{1,0:T(8,128)(2,1)S(1)} %get-tuple-element.68), channel_id=1, source_target_pairs={{8,10},{9,11},{10,8},{11,9},{12,14},{13,15},{14,12},{15,13},{24,26... | collective-permute-start | bytes 393224 | tf_op jit(solution)/shard_map/ppermute | solution.py:38
  57.9 7.6 %collective-permute-start.17 = (s16[64,1024]{1,0:T(8,128)(2,1)S(1)}, s16[64,1024]{1,0:T(8,128)(2,1)}, u32[]{:S(2)}, u32[]{:S(2)}) collective-permute-start(s16[64,1024]{1,0:T(8,128)(2,1)S(1)} %get-tuple-element.69), channel_id=1, source_target_pairs={{8,11},{9,8},{10,9},{11,10},{12,15},{13,12},{14,13},{15,14},{24,27... | collective-permute-start | bytes 393224 | tf_op jit(solution)/shard_map/ppermute | solution.py:38
  81.0 8.9 %collective-permute-start.18 = (s16[128,1024]{1,0:T(8,128)(2,1)}, s16[128,1024]{1,0:T(8,128)(2,1)S(1)}, u32[]{:S(2)}, u32[]{:S(2)}) collective-permute-start(s16[128,1024]{1,0:T(8,128)(2,1)} %get-tuple-element.71), channel_id=1, source_target_pairs={{4,0},{8,4},{12,8},{5,1},{9,5},{13,9},{6,2},{10,6},{14,10},{7,3},{... | collective-permute-start | bytes 786440 | tf_op jit(solution)/shard_map/ppermute | solution.py:25
  83.0 11.5 %collective-permute-start.19 = (s16[128,1024]{1,0:T(8,128)(2,1)}, s16[128,1024]{1,0:T(8,128)(2,1)S(1)}, u32[]{:S(2)}, u32[]{:S(2)}) collective-permute-start(s16[128,1024]{1,0:T(8,128)(2,1)} %get-tuple-element.72), channel_id=1, source_target_pairs={{8,0},{12,4},{9,1},{13,5},{10,2},{14,6},{11,3},{15,7},{24,16},{28,... | collective-permute-start | bytes 786440 | tf_op jit(solution)/shard_map/ppermute | solution.py:25
  84.3 10.2 %collective-permute-start.20 = (s16[128,1024]{1,0:T(8,128)(2,1)}, s16[128,1024]{1,0:T(8,128)(2,1)S(1)}, u32[]{:S(2)}, u32[]{:S(2)}) collective-permute-start(s16[128,1024]{1,0:T(8,128)(2,1)} %get-tuple-element.73), channel_id=1, source_target_pairs={{12,0},{13,1},{14,2},{15,3},{28,16},{29,17},{30,18},{31,19}} | collective-permute-start | bytes 786440 | tf_op jit(solution)/shard_map/ppermute | solution.py:25
  85.0 14.6 %collective-permute-start.24 = (s16[64,1024]{1,0:T(8,128)(2,1)}, s16[64,1024]{1,0:T(8,128)(2,1)S(1)}, u32[]{:S(2)}, u32[]{:S(2)}) collective-permute-start(s16[64,1024]{1,0:T(8,128)(2,1)} %get-tuple-element.79), channel_id=1, source_target_pairs={{0,3},{1,0},{2,1},{3,2},{4,7},{5,4},{6,5},{7,6},{8,11},{9,8},{10,9... | collective-permute-start | bytes 393224 | tf_op jit(solution)/shard_map/ppermute | solution.py:38
  88.6 12.9 %collective-permute-start.25 = (s16[64,1024]{1,0:T(8,128)(2,1)}, s16[64,1024]{1,0:T(8,128)(2,1)S(1)}, u32[]{:S(2)}, u32[]{:S(2)}) collective-permute-start(s16[64,1024]{1,0:T(8,128)(2,1)} %get-tuple-element.80), channel_id=1, source_target_pairs={{0,2},{1,3},{2,0},{3,1},{4,6},{5,7},{6,4},{7,5},{8,10},{9,11},{10,... | collective-permute-start | bytes 393224 | tf_op jit(solution)/shard_map/ppermute | solution.py:38
  89.9 16.0 %collective-permute-start.26 = (s16[64,1024]{1,0:T(8,128)(2,1)}, s16[64,1024]{1,0:T(8,128)(2,1)S(1)}, u32[]{:S(2)}, u32[]{:S(2)}) collective-permute-start(s16[64,1024]{1,0:T(8,128)(2,1)} %get-tuple-element.81), channel_id=1, source_target_pairs={{0,1},{1,2},{2,3},{3,0},{4,5},{5,6},{6,7},{7,4},{8,9},{9,10},{10,1... | collective-permute-start | bytes 393224 | tf_op jit(solution)/shard_map/ppermute | solution.py:38
  96.0 13.0 %collective-permute-start.21 = (s16[32,1024]{1,0:T(8,128)(2,1)S(1)}, s16[32,1024]{1,0:T(8,128)(2,1)S(1)}, u32[]{:S(2)}, u32[]{:S(2)}) collective-permute-start(s16[32,1024]{1,0:T(8,128)(2,1)S(1)} %get-tuple-element.75), channel_id=1, source_target_pairs={{0,3},{1,0},{2,1},{3,2},{4,7},{5,4},{6,5},{7,6},{8,11},{9,8},{10,9... | collective-permute-start | bytes 196616 | tf_op jit(solution)/shard_map/ppermute | solution.py:38
  99.6 9.4 %collective-permute-start.22 = (s16[32,1024]{1,0:T(8,128)(2,1)S(1)}, s16[32,1024]{1,0:T(8,128)(2,1)S(1)}, u32[]{:S(2)}, u32[]{:S(2)}) collective-permute-start(s16[32,1024]{1,0:T(8,128)(2,1)S(1)} %get-tuple-element.76), channel_id=1, source_target_pairs={{0,2},{1,3},{2,0},{3,1},{4,6},{5,7},{6,4},{7,5},{8,10},{9,11},{10,... | collective-permute-start | bytes 196616 | tf_op jit(solution)/shard_map/ppermute | solution.py:38
  99.6 9.4 %collective-permute-start.23 = (s16[32,1024]{1,0:T(8,128)(2,1)S(1)}, s16[32,1024]{1,0:T(8,128)(2,1)S(1)}, u32[]{:S(2)}, u32[]{:S(2)}) collective-permute-start(s16[32,1024]{1,0:T(8,128)(2,1)S(1)} %get-tuple-element.77), channel_id=1, source_target_pairs={{0,1},{1,2},{2,3},{3,0},{4,5},{5,6},{6,7},{7,4},{8,9},{9,10},{10,1... | collective-permute-start | bytes 196616 | tf_op jit(solution)/shard_map/ppermute | solution.py:38
  101.6 27.3 %collective-permute-start.33 = (s16[64,1024]{1,0:T(8,128)(2,1)}, s16[64,1024]{1,0:T(8,128)(2,1)S(1)}, u32[]{:S(2)}, u32[]{:S(2)}) collective-permute-start(s16[64,1024]{1,0:T(8,128)(2,1)} %get-tuple-element.92), channel_id=1, source_target_pairs={{8,11},{9,8},{10,9},{11,10},{12,15},{13,12},{14,13},{15,14},{24,27... | collective-permute-start | bytes 393224 | tf_op jit(solution)/shard_map/ppermute | solution.py:38
  106.0 24.7 %collective-permute-start.34 = (s16[64,1024]{1,0:T(8,128)(2,1)}, s16[64,1024]{1,0:T(8,128)(2,1)S(1)}, u32[]{:S(2)}, u32[]{:S(2)}) collective-permute-start(s16[64,1024]{1,0:T(8,128)(2,1)} %get-tuple-element.93), channel_id=1, source_target_pairs={{8,10},{9,11},{10,8},{11,9},{12,14},{13,15},{14,12},{15,13},{24,26... | collective-permute-start | bytes 393224 | tf_op jit(solution)/shard_map/ppermute | solution.py:38
  109.3 10.1 %collective-permute-start.29 = (s16[32,1024]{1,0:T(8,128)(2,1)S(1)}, s16[32,1024]{1,0:T(8,128)(2,1)S(1)}, u32[]{:S(2)}, u32[]{:S(2)}) collective-permute-start(s16[32,1024]{1,0:T(8,128)(2,1)S(1)} %get-tuple-element.82.refs_6_.refs_1_), channel_id=1, source_target_pairs={{0,3},{1,0},{2,1},{3,2},{4,7},{5,4},{6,5},{7,6},{8,11},{9,8},{10,9... | collective-permute-start | bytes 196616 | tf_op jit(solution)/shard_map/ppermute | solution.py:38
  110.3 13.2 %collective-permute-start.28 = (s16[32,1024]{1,0:T(8,128)(2,1)S(1)}, s16[32,1024]{1,0:T(8,128)(2,1)S(1)}, u32[]{:S(2)}, u32[]{:S(2)}) collective-permute-start(s16[32,1024]{1,0:T(8,128)(2,1)S(1)} %get-tuple-element.82.refs_6_.refs_1_), channel_id=1, source_target_pairs={{0,2},{1,3},{2,0},{3,1},{4,6},{5,7},{6,4},{7,5},{8,10},{9,11},{10,... | collective-permute-start | bytes 196616 | tf_op jit(solution)/shard_map/ppermute | solution.py:38
  111.2 12.2 %collective-permute-start.27 = (s16[32,1024]{1,0:T(8,128)(2,1)S(1)}, s16[32,1024]{1,0:T(8,128)(2,1)S(1)}, u32[]{:S(2)}, u32[]{:S(2)}) collective-permute-start(s16[32,1024]{1,0:T(8,128)(2,1)S(1)} %get-tuple-element.82.refs_6_.refs_1_), channel_id=1, source_target_pairs={{0,1},{1,2},{2,3},{3,0},{4,5},{5,6},{6,7},{7,4},{8,9},{9,10},{10,1... | collective-permute-start | bytes 196616 | tf_op jit(solution)/shard_map/ppermute | solution.py:38
  119.4 11.2 %collective-permute-start.35 = (s16[64,1024]{1,0:T(8,128)(2,1)S(1)}, s16[64,1024]{1,0:T(8,128)(2,1)S(1)}, u32[]{:S(2)}, u32[]{:S(2)}) collective-permute-start(s16[64,1024]{1,0:T(8,128)(2,1)S(1)} %copy-done.28), channel_id=1, source_target_pairs={{8,9},{9,10},{10,11},{11,8},{12,13},{13,14},{14,15},{15,12},{24,25... | collective-permute-start | bytes 393224 | tf_op jit(solution)/shard_map/ppermute | solution.py:38
  (35 other events, 393.3 us)
